TPU v7x, 32 devices: a whole 2x2x4 slice. The times are simulated.
32 devices in a mesh: seq: 8 (over z, y), fsdp: 4 (over x, core).
Axes of the slice: x: 2, y: 2, z: 4, core: 2. Of those that a mesh axis runs over, the one named last changes fastest.
Arguments:
- tokens: bfloat16 [65536, 1280], P(('seq', 'fsdp')), may hold values from -6 to 6
- input_mask: int32 [65536], P(('seq', 'fsdp')), may hold values from 0 to 1
- doc_lengths: int32 [129], replicated, may hold values from 1 to 1022, as said below
- cotangent: bfloat16 [65536, 1280], P(('seq', 'fsdp')), may hold values from -6 to 6
- w_in: float32 [1280, 640], P('fsdp'), may hold values from -0.15625 to 0.15625
- w_conv: float32 [3200, 640], P('fsdp'), may hold values from -0.109375 to 0.109375
- w_out: float32 [640, 1280], P('fsdp'), may hold values from -0.25 to 0.25
- norm_params: float32 [2, 2560], replicated, may hold values from -0.6 to 2.3, as said below
- row_in: float32 [1280], P('fsdp'), may hold values from 6160.384 to 24641.535
- col_in: float32 [640], replicated, may hold values from 6160.384 to 24641.535
- row_conv: float32 [3200], P('fsdp'), may hold values from 6160.384 to 24641.535
- col_conv: float32 [640], replicated, may hold values from 6160.384 to 24641.535
- row_out: float32 [640], P('fsdp'), may hold values from 6160.384 to 24641.535
- col_out: float32 [1280], replicated, may hold values from 6160.384 to 24641.535
- norm_second: float32 [2, 2560], replicated, may hold values from 4915.2 to 19660.8
Outputs:
- block_out: bfloat16 [65536, 1280], P(('seq', 'fsdp'))
- input_grad: float32 [65536, 1280], P(('seq', 'fsdp'))
- grad_in: float32 [1280, 640], P('fsdp')
- grad_conv: float32 [3200, 640], P('fsdp')
- grad_out: float32 [640, 1280], P('fsdp')
- new_in: float32 [1280, 640], P('fsdp')
- new_conv: float32 [3200, 640], P('fsdp')
- new_out: float32 [640, 1280], P('fsdp')
- row_in_new: float32 [1280], P('fsdp')
- col_in_new: float32 [640], replicated
- row_conv_new: float32 [3200], P('fsdp')
- col_conv_new: float32 [640], replicated
- row_out_new: float32 [640], P('fsdp')
- col_out_new: float32 [1280], replicated
- norm_grads: float32 [2, 2560], replicated
- norm_second_new: float32 [2, 2560], replicated
- norm_new: float32 [2, 2560], replicated
Inputs may be any that keep to these rules, and one draw needn't show every extreme that they name: `doc_lengths`: the proteins lie end to end and fill all 65536 tokens; each aligned run of 512 tokens holds exactly one protein end before its last token, and the last run one more at its end. `norm_params`: row 0 positive gains, row 1 shifts.
All inputs are finite; a program needn't handle non-finite values.
Results may differ from a plain program's by a relative error of at most 0.0095.
Values may be sent and summed in bfloat16 or wider, within the bound.
No kernel may reach another device: no remote copies, remote signals or barrier semaphores. Data moves between devices by JAX's collectives and lax.ppermute only.
A program may use at most 192 MiB of HBM per device.

v0:
```python
import functools
import math

import jax
import jax.numpy as jnp
from jax import lax
from jax.experimental import pallas as pl
from jax.experimental.pallas import tpu as pltpu
from jax.sharding import PartitionSpec as P

D = 1280
INNER = 640
KERNEL_TAPS = 5
DILATION_STEP = 128
STEP = 10
EPSILON = 1e-05
DECAY = 1.0 - STEP ** (-0.8)

REACH = (KERNEL_TAPS - 1) // 2 * DILATION_STEP
MID = (KERNEL_TAPS - 1) // 2
F32 = jnp.float32
BF16 = jnp.bfloat16
SUB, LANE = 16, 128
AXES = ("seq", "fsdp")
NT = (((1,), (1,)), ((), ()))
TN = (((0,), (0,)), ((), ()))
NN = (((1,), (0,)), ((), ()))


def call(kernel, grid, in_specs, out_specs, out_shape, scratch=(), us=1.0, aliases=None, mib=58):
    params = pltpu.CompilerParams(
        vmem_limit_bytes=mib * 1024 * 1024, dimension_semantics=("arbitrary",) * len(grid)
    )
    return pl.pallas_call(
        kernel,
        grid=grid,
        in_specs=in_specs,
        out_specs=out_specs,
        out_shape=out_shape,
        scratch_shapes=list(scratch),
        compiler_params=params,
        input_output_aliases=aliases or {},
        cost_estimate=pl.CostEstimate(
                flops=int(us * 1.1e9), bytes_accessed=int(us * 3.4e6), transcendentals=0
        ),
    )


def shape(dims, dtype):
    return jax.ShapeDtypeStruct(dims, dtype)


def rows_spec(tile, width):
    return pl.BlockSpec((tile, width), lambda i: (i, 0))


def whole(*dims):
    return pl.BlockSpec(dims, lambda *_: (0,) * len(dims))


ANY = pl.BlockSpec(memory_space=pl.ANY)
SMEM = pl.BlockSpec(memory_space=pltpu.SMEM)


ERFC_P = 0.47 / math.sqrt(2.0)
ERFC_C = (
    0.12357219400743558,
    0.1999878668208835,
    -0.08033356004356296,
    0.3660253986657854,
    -0.1092519747040215,
)
LOG2E = 1.4426950408889634


def gelu_and_slope(y):
    t = pltpu.reciprocal(1.0 + ERFC_P * jnp.abs(y), approx=True)
    bell = jnp.exp2(y * y * (-0.5 * LOG2E))
    poly = ERFC_C[4] * t + ERFC_C[3]
    for c in ERFC_C[2::-1]:
        poly = poly * t + c
    tail = poly * t * bell
    cdf = jnp.where(y > 0.0, 1.0 - tail, tail)
    return y * cdf, cdf + y * (bell * (1.0 / math.sqrt(2.0 * math.pi)))


def lane_blocks(width):
    return [slice(k, k + LANE) for k in range(0, width, LANE)]


def row_stats(ref, rows):
    width = ref.shape[-1]
    blocks = lane_blocks(width)
    total = ref[rows, blocks[0]].astype(F32)
    for b in blocks[1:]:
        total = total + ref[rows, b].astype(F32)
    mean = jnp.sum(total, axis=-1, keepdims=True) * (1.0 / width)
    square = None
    for b in blocks:
        centered = ref[rows, b].astype(F32) - mean
        square = centered * centered if square is None else square + centered * centered
    variance = jnp.sum(square, axis=-1, keepdims=True) * (1.0 / width)
    return mean, lax.rsqrt(variance + EPSILON)


def fold(values):
    total = values[0:8]
    for k in range(8, values.shape[0], 8):
        total = total + values[k : k + 8]
    return total


def in_stages(count, stages, between=()):
    chunks = [slice(k, k + CHUNK) for k in range(0, count, CHUNK)]
    kept, rounds = {}, len(chunks) + len(stages) - 1
    for t in range(rounds):
        for n, stage in enumerate(stages):
            if 0 <= t - n < len(chunks):
                kept[n, t - n] = stage(chunks[t - n], kept.get((n - 1, t - n)))
        for work in between[t * len(between) // rounds : (t + 1) * len(between) // rounds]:
            work()


def halves_of(count):
    return (slice(0, count // 2), slice(count // 2, count))


def row_means(sums, width):
    return [jnp.sum(x, axis=-1, keepdims=True) * (1.0 / width) for x in sums]


def norm_back(rows, dxhat_ref, xhat_ref, means, put):
    mean_d, mean_dx, rstd = means
    for b in lane_blocks(dxhat_ref.shape[-1]):
        xhat = xhat_ref[rows, b].astype(F32)
        put(b, (dxhat_ref[rows, b] - mean_d - xhat * mean_dx) * rstd)


def add_terms(acc_ref, b, dy, xhat):
    acc_ref[0:8, b] += fold(dy * xhat)
    acc_ref[8:16, b] += fold(dy)


def open_sums(acc_ref):
    @pl.when(pl.program_id(0) == 0)
    def _():
        acc_ref[...] = jnp.zeros_like(acc_ref)


def close_sums(out_ref, acc_ref):
    @pl.when(pl.program_id(0) == pl.num_programs(0) - 1)
    def _():
        out_ref[0:1, :] = jnp.sum(acc_ref[0:8, :], axis=0, keepdims=True)
        out_ref[1:2, :] = jnp.sum(acc_ref[8:16, :], axis=0, keepdims=True)


def run_copies(copies):
    for copy in copies:
        copy.start()
    for copy in copies:
        copy.wait()


def piece_copies(pieces, full_ref, me, sem, first=0):
    each = full_ref.shape[0] // len(pieces)
    return [
        pltpu.make_async_copy(
            piece.at[0:each, :],
            full_ref.at[pl.ds(pl.multiple_of((me ^ k) * each, SUB), each), :],
            sem.at[first + k],
        )
        for k, piece in enumerate(pieces)
    ]


def out_copies(pieces, full_ref, me, sem, first=0):
    each, width = full_ref.shape[0] // len(pieces), full_ref.shape[1] // 2
    copies = []
    for k, piece in enumerate(pieces):
        rows = pl.ds(pl.multiple_of((me ^ k) * each, SUB), each)
        for side in range(2):
            at = piece.shape[0] - (2 - side) * each
            copies.append(
                pltpu.make_async_copy(
                    piece.at[at : at + each, :],
                    full_ref.at[rows, side * width : (side + 1) * width],
                    sem.at[first + 2 * k + side],
                )
            )
    return copies


def column(row):
    return jnp.transpose(jnp.broadcast_to(row, (LANE, LANE)))


CHUNK = 64
UPDATE_STEPS = 5
TURNED = 2


def norm_a_kernel(tok_ref, np_ref, hid_ref, slope_ref, xhat_ref, rstd_ref):
    def stats(rows, _):
        mean, rstd = row_stats(tok_ref, rows)
        rstd_ref[rows, :] = jnp.broadcast_to(rstd, (CHUNK, LANE))
        return mean, rstd

    def work(rows, kept):
        mean, rstd = kept
        for b in lane_blocks(D):
            xhat = (tok_ref[rows, b].astype(F32) - mean) * rstd
            hidden, slope = gelu_and_slope(xhat * np_ref[0:1, b] + np_ref[1:2, b])
            hid_ref[rows, b] = hidden.astype(BF16)
            slope_ref[rows, b] = slope.astype(BF16)
            xhat_ref[rows, b] = xhat.astype(BF16)

    in_stages(tok_ref.shape[0], [stats, work])


def running_ends(ends_ref, lengths_ref):
    docs, width = lengths_ref.shape[0], ends_ref.shape[1]
    ends_ref[...] = jnp.zeros_like(ends_ref)
    ends_ref[0:1, 0:docs] = lengths_ref[...].reshape(1, -1).astype(F32)
    before = jnp.zeros((1, 1), F32)
    row = lax.broadcasted_iota(jnp.int32, (LANE, LANE), 0)
    lane = lax.broadcasted_iota(jnp.int32, (LANE, LANE), 1)
    for k in range(0, width, LANE):
        line = ends_ref[0:1, k : k + LANE]
        sums = jnp.sum(jnp.where(row <= lane, column(line), 0.0), axis=0, keepdims=True) + before
        ends_ref[0:1, k : k + LANE] = jnp.where(lane[0:1] + k < docs, sums, 1e9)
        before = before + jnp.sum(line, axis=1, keepdims=True)


def in_kernel(pieces, tiles, place_ref, lengths_ref, hid_ref, live_ref, np_ref, *refs):
    piece_refs = refs[:pieces]
    edges = tiles[0] == 0
    outs = refs[-(11 if edges else 9) :]
    mov_ref, slope_ref, xhat_ref, rstd_ref, mask_ref = outs[:5]
    w_ref, pre_ref, ends_ref, sem = outs[-4:]
    step = pl.program_id(0)
    tile = hid_ref.shape[0]

    @pl.when(step == 0)
    def _():
        copies = piece_copies(piece_refs, w_ref, place_ref[0], sem)
        for copy in copies:
            copy.start()
        running_ends(ends_ref, lengths_ref)
        for copy in copies:
            copy.wait()

    for half in halves_of(tile):
        pre_ref[half, :] = lax.dot_general(
            hid_ref[half, :], w_ref[...], NN, preferred_element_type=F32
        )

    at_tile = tiles[0] + step * tiles[1]
    first = place_ref[1] + at_tile * tile
    ends = ends_ref[0:1, :]
    lanes = lax.broadcasted_iota(jnp.int32, (LANE, LANE), 1)
    offsets = ((lanes - MID) * DILATION_STEP).astype(F32)
    for k in range(tile // LANE):
        at = (first + k * LANE + lax.broadcasted_iota(jnp.int32, (LANE, 1), 0)).astype(F32)
        begin = jnp.max(jnp.where(ends <= at, ends, 0.0), axis=1, keepdims=True)
        end = jnp.min(jnp.where(ends > at, ends, 1e9), axis=1, keepdims=True)
        there = at + offsets
        same = jnp.where((there >= begin) & (there < end), 1.0, 0.0)
        live = column(live_ref[pl.ds(at_tile * (tile // LANE) + k, 1), :].astype(F32))
        mask_ref[k * LANE : (k + 1) * LANE, :] = jnp.where(lanes == MID, live, same)

    def stats(rows, _):
        mean, rstd = row_stats(pre_ref, rows)
        rstd_ref[rows, :] = jnp.broadcast_to(rstd, (CHUNK, LANE))
        return mean, rstd

    def work(rows, kept):
        mean, rstd = kept
        live = mask_ref[rows, MID : MID + 1]
        for b in lane_blocks(INNER):
            gains = slice(D + b.start, D + b.stop)
            xhat = (pre_ref[rows, b] - mean) * rstd
            hidden, slope = gelu_and_slope(xhat * np_ref[0:1, gains] + np_ref[1:2, gains])
            mov_ref[rows, b] = (hidden * live).astype(BF16)
            slope_ref[rows, b] = slope.astype(BF16)
            xhat_ref[rows, b] = xhat.astype(BF16)

    in_stages(tile, [stats, work])
    if edges:
        put_edges(place_ref, outs[5], outs[6], mov_ref, step == 0, step == 1)


def load_window(place_ref, inner, mid, outer, ext_ref, sem):
    rows, core = mid.shape[0], lax.rem(place_ref[0], 2)
    near = pl.multiple_of((1 - core) * (REACH + rows), SUB)
    far = pl.multiple_of(core * (REACH + rows), SUB)
    return [
        pltpu.make_async_copy(inner, ext_ref.at[pl.ds(near, REACH), :], sem.at[0]),
        pltpu.make_async_copy(mid, ext_ref.at[REACH : REACH + rows, :], sem.at[1]),
        pltpu.make_async_copy(outer, ext_ref.at[pl.ds(far, REACH), :], sem.at[2]),
    ]


def put_edges(place_ref, inner_ref, outer_ref, tile_ref, at_first, at_last):
    rows, core = tile_ref.shape[0], lax.rem(place_ref[0], 2)
    for at, edge, first in ((at_first, slice(0, REACH), 0), (at_last, slice(rows - REACH, rows), 1)):

        @pl.when(at & (core == first))
        def _(edge=edge):
            outer_ref[...] = tile_ref[edge, :]

        @pl.when(at & (core != first))
        def _(edge=edge):
            inner_ref[...] = tile_ref[edge, :]


def fill_taps(taps_ref, ext_ref, mask_ref, start):
    tile = taps_ref.shape[0]
    for j in range(KERNEL_TAPS):
        rows = pl.ds(pl.multiple_of(start + j * DILATION_STEP, DILATION_STEP), tile)
        picked = ext_ref[rows, :]
        if j != MID:
            picked = picked * mask_ref[:, j : j + 1].astype(BF16)
        taps_ref[:, j * INNER : (j + 1) * INNER] = picked


def conv_kernel(
    pieces, rows_of, place_ref, low_ref, mov_ref, high_ref, mask_ref, cot_ref, before_ref, np_ref, *refs
):
    piece_refs = refs[:pieces]
    hid_ref, dconv_ref, inner_ref, outer_ref, sums_ref, turned_ref = refs[pieces : pieces + 6]
    outs = refs[pieces + 6 : pieces + 10]
    ext_ref, wc_ref, wct_ref, wo_ref, wt_ref, taps_ref, pre_ref, dh_ref, xhat_ref = refs[
        pieces + 10 : pieces + 19
    ]
    dt_ref, ht_ref, gc_ref, go_ref, acc_ref, stage1_ref, stage2_ref, sem = refs[pieces + 19 :]
    step, steps = pl.program_id(0), pl.num_programs(0) - 1
    tile = taps_ref.shape[1]
    slot = lax.rem(step, 2)

    @pl.when(step == 0)
    def _():
        me = place_ref[0]
        outs = out_copies(piece_refs, wo_ref, me, sem, 3)
        rest = load_window(place_ref, low_ref, mov_ref, high_ref, ext_ref, sem)
        rest += piece_copies(piece_refs, wc_ref, me, sem, 3 + 2 * pieces)
        for copy in outs + rest:
            copy.start()
        for ref in (acc_ref, gc_ref, go_ref):
            ref[...] = jnp.zeros_like(ref)
        for copy in outs:
            copy.wait()
        for k in range(0, D, 256):
            wt_ref[k : k + 256, :] = jnp.transpose(wo_ref[:, k : k + 256])
        for copy in rest:
            copy.wait()

    def grad_conv(cols):
        def work():
            gc_ref[:, cols] += lax.dot_general(
                dt_ref[...], taps_ref[1 - slot, :, cols], NN, preferred_element_type=F32
            )

        return work

    def grad_out(cols):
        def work():
            go_ref[:, cols] += lax.dot_general(
                ht_ref[...], before_ref[:, cols], NN, preferred_element_type=F32
            )

        return work

    taps_wide = KERNEL_TAPS * INNER
    products = [grad_conv(slice(k, min(k + 768, taps_wide))) for k in range(0, taps_wide, 768)]
    products += [grad_out(slice(k, min(k + 768, D))) for k in range(0, D, 768)]

    def tile_work(products, turned):
        fill_taps(taps_ref.at[slot], ext_ref, mask_ref, step * tile)
        pre_ref[...] = lax.dot_general(
            taps_ref[slot], wc_ref[...], NN, preferred_element_type=F32
        )
        dh_ref[...] = lax.dot_general(cot_ref[...], wt_ref[...], NN, preferred_element_type=F32)
        for n in range(turned):
            tap = jnp.minimum(turned * (step - 1) + n, KERNEL_TAPS - 1)
            source = wc_ref[pl.ds(pl.multiple_of(tap * INNER, SUB), INNER), :]
            target = pl.multiple_of((KERNEL_TAPS - 1 - tap) * INNER, SUB)
            wct_ref[pl.ds(target, INNER), :] = jnp.transpose(source)

        def stats(rows, _):
            return row_stats(pre_ref, rows)

        def work(rows, kept):
            mean, rstd = kept
            sums = [0.0, 0.0]
            for b in lane_blocks(INNER):
                gains = slice(D + INNER + b.start, D + INNER + b.stop)
                gain = np_ref[0:1, gains]
                xhat = (pre_ref[rows, b] - mean) * rstd
                hidden, slope = gelu_and_slope(xhat * gain + np_ref[1:2, gains])
                hid_ref[rows, b] = hidden.astype(BF16)
                dy = dh_ref[rows, b] * slope
                add_terms(acc_ref, b, dy, xhat)
                dxhat = dy * gain
                xhat_ref[rows, b] = xhat
                dh_ref[rows, b] = dxhat
                sums = [sums[0] + dxhat, sums[1] + dxhat * xhat]
            return row_means(sums, INNER) + [rstd]

        def finish(rows, means):
            def put(b, value):
                dconv_ref[rows, b] = value.astype(BF16)

            norm_back(rows, dh_ref, xhat_ref, means, put)

        in_stages(tile, [stats, work, finish], products)
        dt_ref[...] = jnp.transpose(dconv_ref[...])
        ht_ref[...] = jnp.transpose(hid_ref[...])

    @pl.when(step == 0)
    def _():
        tile_work([], 0)

    @pl.when((step > 0) & (step < steps))
    def _():
        tile_work(products, TURNED)

    put_edges(place_ref, inner_ref, outer_ref, dconv_ref, step == 0, step == steps - 1)

    @pl.when(step == steps)
    def _():
        copy = pltpu.make_async_copy(wct_ref, turned_ref, sem.at[4])
        copy.start()
        for work in products:
            work()
        core = lax.rem(place_ref[0], 2)
        _, rows_conv, rows_out = rows_of
        stage_turned(stage1_ref, core, gc_ref, rows_conv, 0, slice(0, CUT // LANE))
        first_tiles = rows_conv // SUB * (CUT // LANE)
        stage_plain(stage1_ref, core, go_ref, rows_out, first_tiles)
        copies = stage_copies(stage1_ref, outs[0], outs[1], spans(CHUNKS[0], rows_of)[1], sem, 0)
        for each in copies:
            each.start()
        stage_turned(stage2_ref, core, gc_ref, rows_conv, 0, slice(CUT // LANE, INNER // LANE))
        more = stage_copies(stage2_ref, outs[2], outs[3], spans(CHUNKS[1], rows_of)[1], sem, 2)
        for each in more:
            each.start()
        for each in copies + more + [copy]:
            each.wait()
        sums_ref[0:1, :] = jnp.sum(acc_ref[0:8, :], axis=0, keepdims=True)
        sums_ref[1:2, :] = jnp.sum(acc_ref[8:16, :], axis=0, keepdims=True)


def stage_tiles(stage_ref, core, first_row, rows_each, base, block0, blocks, value):
    for g in range(value.shape[0] // SUB):
        row = first_row + g * SUB
        owner, inside = row // rows_each, row % rows_each // SUB
        side = core ^ (owner % 2)
        for b in range(value.shape[1] // LANE):
            tile = value[g * SUB : (g + 1) * SUB, b * LANE : (b + 1) * LANE]
            at = base + inside * blocks + block0 + b
            stage_ref[side, owner // 2, at] = tile.astype(BF16)


def stage_plain(stage_ref, core, grad_ref, rows_each, base):
    blocks = grad_ref.shape[1] // LANE
    for row in range(0, grad_ref.shape[0], SUB):
        part = grad_ref[row : row + SUB, :]
        stage_tiles(stage_ref, core, row, rows_each, base, 0, blocks, part)


def stage_turned(stage_ref, core, turned_ref, rows_each, base, blocks):
    count = blocks.stop - blocks.start
    for row in range(0, turned_ref.shape[1], LANE):
        for b in range(count):
            at = (blocks.start + b) * LANE
            part = jnp.transpose(turned_ref[at : at + LANE, row : row + LANE].astype(BF16))
            stage_tiles(stage_ref, core, row, rows_each, base, b, count, part)


def stage_copies(stage_ref, keep_ref, send_ref, used, sem, first):
    count = stage_ref.shape[2]
    if used < count:
        dims = stage_ref.shape[:2] + (count - used, SUB, LANE)
        stage_ref[:, :, used:] = jnp.zeros(dims, BF16)
    return [
        pltpu.make_async_copy(stage_ref.at[n], ref, sem.at[first + n])
        for n, ref in enumerate((keep_ref, send_ref))
    ]


def back_conv_kernel(
    last, rows_in, place_ref, low_ref, d_ref, high_ref, turned_ref, mask_ref, xhat_ref, rstd_ref, slope_ref, hid_ref, np_ref, *refs
):
    if last:
        before_ref, dpre_ref, sums_ref, keep_ref, send_ref, stage_ref = refs[:6]
    else:
        dpre_ref, sums_ref, part_ref = refs[:3]
    ext_ref, wt_ref, taps_ref, dmov_ref, grad_ref, acc_ref, sem = refs[-7:]
    step, steps = pl.program_id(0), pl.num_programs(0)
    tile = taps_ref.shape[0]
    open_sums(acc_ref)

    @pl.when(step == 0)
    def _():
        copies = load_window(place_ref, low_ref, d_ref, high_ref, ext_ref, sem)
        copies.append(pltpu.make_async_copy(turned_ref, wt_ref, sem.at[3]))
        if last:
            copies.append(pltpu.make_async_copy(before_ref, grad_ref, sem.at[4]))
        for copy in copies:
            copy.start()
        if not last:
            grad_ref[...] = jnp.zeros_like(grad_ref)
        for copy in copies:
            copy.wait()

    fill_taps(taps_ref, ext_ref, mask_ref, (steps * last + step) * tile)
    for half in halves_of(tile):
        dmov_ref[half, :] = lax.dot_general(
            taps_ref[half, :], wt_ref[...], NN, preferred_element_type=F32
        )

    def work(rows, _):
        live = mask_ref[rows, MID : MID + 1]
        sums = [0.0, 0.0]
        for b in lane_blocks(INNER):
            xhat = xhat_ref[rows, b].astype(F32)
            dy = dmov_ref[rows, b] * live * slope_ref[rows, b].astype(F32)
            add_terms(acc_ref, b, dy, xhat)
            dxhat = dy * np_ref[0:1, D + b.start : D + b.stop]
            dmov_ref[rows, b] = dxhat
            sums = [sums[0] + dxhat, sums[1] + dxhat * xhat]
        return row_means(sums, INNER) + [rstd_ref[rows, :]]

    def finish(rows, means):
        def put(b, value):
            dpre_ref[rows, b] = value.astype(BF16)

        norm_back(rows, dmov_ref, xhat_ref, means, put)

    in_stages(tile, [work, finish])
    close_sums(sums_ref, acc_ref)
    grad_ref[...] += lax.dot_general(dpre_ref[...], hid_ref[...], TN, preferred_element_type=F32)

    @pl.when(step == steps - 1)
    def _():
        if last:
            all_blocks = slice(0, INNER // LANE)
            stage_turned(stage_ref, lax.rem(place_ref[0], 2), grad_ref, rows_in, 0, all_blocks)
            used = rows_in // SUB * (INNER // LANE)
            run_copies(stage_copies(stage_ref, keep_ref, send_ref, used, sem, 0))
        else:
            run_copies([pltpu.make_async_copy(grad_ref, part_ref, sem.at[0])])


def back_a_kernel(pieces, half, place_ref, dpre0_ref, dpre1_ref, xhat_ref, rstd_ref, slope_ref, cot_ref, np_ref, *refs):
    piece_refs = refs[:pieces]
    grad_ref, sums_ref, w_ref, wt_ref, dh_ref, acc_ref, sem = refs[-7:]
    open_sums(acc_ref)

    @pl.when(pl.program_id(0) == 0)
    def _():
        run_copies(piece_copies(piece_refs, w_ref, place_ref[0], sem))
        for k in range(0, D, 256):
            wt_ref[:, k : k + 256] = jnp.transpose(w_ref[k : k + 256, :])

    second = (jnp.zeros((1, 1), jnp.int32) + pl.program_id(0)) >= half
    d_pre = jnp.where(second, dpre1_ref[...], dpre0_ref[...])
    dh_ref[...] = lax.dot_general(d_pre, wt_ref[...], NN, preferred_element_type=F32)

    def work(rows, _):
        sums = [0.0, 0.0]
        for b in lane_blocks(D):
            xhat = xhat_ref[rows, b].astype(F32)
            dy = dh_ref[rows, b] * slope_ref[rows, b].astype(F32)
            add_terms(acc_ref, b, dy, xhat)
            dxhat = dy * np_ref[0:1, b]
            dh_ref[rows, b] = dxhat
            sums = [sums[0] + dxhat, sums[1] + dxhat * xhat]
        return row_means(sums, D) + [rstd_ref[rows, :]]

    def finish(rows, means):
        def put(b, value):
            grad_ref[rows, b] = cot_ref[rows, b].astype(F32) + value

        norm_back(rows, dh_ref, xhat_ref, means, put)

    in_stages(dpre0_ref.shape[0], [work, finish])
    close_sums(sums_ref, acc_ref)


def out_kernel(pieces, place_ref, hid_ref, tok_ref, *refs):
    piece_refs = refs[:pieces]
    out_ref, w_ref, sem = refs[pieces:]

    @pl.when(pl.program_id(0) == 0)
    def _():
        run_copies(out_copies(piece_refs, w_ref, place_ref[0], sem))

    branch = lax.dot_general(hid_ref[...], w_ref[...], NN, preferred_element_type=F32)
    out_ref[...] = (tok_ref[...].astype(F32) + branch).astype(BF16)


WIDTHS = (INNER, INNER, D)
LANE0 = (0, INNER, 2 * INNER)
CUT = 2 * LANE
CHUNKS = (((1, 0, CUT), (2, 0, D)), ((1, CUT, INNER - CUT),), ((0, 0, INNER),))


def spans(chunk, rows):
    found, first = [], 0
    for weight, col, cols in chunk:
        tiles = rows[weight] // SUB * (cols // LANE)
        found.append((weight, col // LANE, cols // LANE, first, tiles))
        first += tiles
    return found, first


def column_sums(pack_ref, row, ref, chunk, rows):
    for weight, block0, blocks, first, tiles in spans(chunk, rows)[0]:

        def body(g, carry, first=first, blocks=blocks):
            new = []
            for b in range(blocks):
                value = ref[first + g * blocks + b].astype(F32)
                new.append(carry[b] + fold(value * value + 1e-30))
            return tuple(new)

        zero = tuple(jnp.zeros((8, LANE), F32) for _ in range(blocks))
        cols = lax.fori_loop(0, tiles // blocks, body, zero, unroll=5)
        for b in range(blocks):
            lane = LANE0[weight] + (block0 + b) * LANE
            pack_ref[row : row + 1, lane : lane + LANE] = jnp.sum(cols[b], axis=0, keepdims=True)


def load_full(refs, place_ref, first, full_ref, sem, at):
    pieces = refs[0].shape[0]
    each = full_ref.shape[0] // (len(refs) * pieces)
    outer = pieces if len(refs) == 2 else pieces // 2
    y = place_ref[2] % 2
    copies = []
    for n, (ref, side) in enumerate(zip(refs, (y, 1 - y))):
        for p in range(pieces):
            index = side * outer + p if len(refs) == 2 else p % 2 * outer + p // 2
            target = full_ref.at[pl.ds(index * each, each)]
            source = ref.at[p, first : first + each]
            copies.append(pltpu.make_async_copy(source, target, sem.at[at + n * pieces + p]))
    return copies


def load_halves(mine_ref, other_ref, place_ref, full_ref, sem):
    y, each = lax.rem(place_ref[2], 2), mine_ref.shape[0]
    return [
        pltpu.make_async_copy(ref, full_ref.at[pl.ds(side * each, each)], sem.at[n])
        for n, (ref, side) in enumerate(((mine_ref, y), (other_ref, 1 - y)))
    ]


PACK_BLOCKS = (D + 2 * INNER) // LANE


def pack_line(pack_ref, row, lane0, width):
    parts = []
    for lane in range(lane0, lane0 + width, LANE):
        at = row * PACK_BLOCKS + lane // LANE
        parts.append(pack_ref[at // SUB, at % SUB : at % SUB + 1, :])
    return jnp.concatenate(parts, axis=1)


def pack_kernel(rows, pieces, place_ref, part_ref, *refs):
    states, sums, (pack_ref, acc_ref) = refs[0:3], refs[3:7], refs[7:9]
    pack_ref[...] = jnp.zeros_like(pack_ref)

    def add(row, lane, value):
        at = row * PACK_BLOCKS + lane // LANE
        pack_ref[at // SUB, at % SUB : at % SUB + 1, :] += value

    lanes_of = ((0, D), (D, D + INNER), (D, D + INNER), (D + INNER, D + 2 * INNER))
    for part, (lane0, lane1) in zip(sums, lanes_of):
        for lane in range(lane0, lane1, LANE):
            for row in range(2):
                add(row, lane, part[row : row + 1, lane - lane0 : lane - lane0 + LANE])
    lanes = lax.broadcasted_iota(jnp.int32, (1, LANE), 1)
    for k in range(3):
        total = jnp.sum(states[k][...].reshape(1, -1), axis=1, keepdims=True)
        add(3, 0, jnp.where(lanes == k, total, 0.0))
    acc_ref[...] = jnp.zeros_like(acc_ref)
    spare = acc_ref.shape[0] - 1
    outer = place_ref[3] // 2
    piece = place_ref[2] % 2 * outer + place_ref[2] // 2
    at = 0
    for chunk, each in zip(CHUNKS[:2], pieces):
        found, _ = spans(chunk, rows)
        start = piece * each

        def body(k, carry, found=found, start=start, at=at):
            n = start + k
            slot = spare
            for weight, block0, blocks, first, tiles in found:
                here = LANE0[weight] // LANE + block0 + lax.rem(jnp.maximum(n - first, 0), blocks)
                slot = jnp.where((n >= first) & (n < first + tiles), here, slot)
            value = part_ref[at + k].astype(F32)
            acc_ref[slot] += value * value + 1e-30
            return carry

        lax.fori_loop(0, each, body, 0, unroll=2)
        at += each
    for slot in range(spare):
        add(2, slot * LANE, jnp.sum(acc_ref[slot], axis=0, keepdims=True))


def pack_in_kernel(rows, place_ref, mine_ref, other_ref, pack_ref, full_ref, sem):
    run_copies(load_halves(mine_ref, other_ref, place_ref, full_ref, sem))
    pack_ref[...] = jnp.zeros_like(pack_ref)
    column_sums(pack_ref, 0, full_ref, CHUNKS[2], rows)


def update_weight(
    k, squares, states_sum, source, weight, state, col_state, grad_ref, new, row_new_ref, col_new_ref, scratch, step=0, steps=1
):
    line_ref, state_ref, new_ref, scaled_ref = scratch
    width, fan, rows_here = WIDTHS[k], (D, KERNEL_TAPS * INNER, INNER)[k], state.shape[0]
    whole_rows = rows_here + -rows_here % LANE
    groups = rows_here // SUB // steps
    rate = 0.5 / fan**0.5

    def before():
        col_new = DECAY * col_state[...].reshape(1, -1) + (1.0 - DECAY) * (squares * (1.0 / fan))
        col_new_ref[...] = col_new.reshape(-1)
        total = DECAY * states_sum
        total = total + (1.0 - DECAY) * (1.0 / width) * jnp.sum(squares, axis=1, keepdims=True)
        scaled_ref[0:1, 0:width] = col_new / (total * (1.0 / fan))
        line_ref[0:1, 0:rows_here] = state[...].reshape(1, -1)
        for c in range(0, whole_rows, LANE):
            state_ref[c : c + LANE, :] = column(line_ref[0:1, c : c + LANE])

    def after():
        for c in range(0, whole_rows, LANE):
            line_ref[0:1, c : c + LANE] = jnp.transpose(new_ref[c : c + LANE, :])[0:1, :]
        row_new_ref[...] = line_ref[0:1, 0:rows_here].reshape(-1)

    def body(g, carry):
        here = pl.ds(pl.multiple_of(g * SUB, SUB), SUB)
        at = step * groups + g
        rows = pl.ds(pl.multiple_of(at * SUB, SUB), SUB)
        square = 0.0
        for ref, block0, blocks, first in source:
            for b in range(blocks):
                value = ref[first + at * blocks + b].astype(F32)
                grad_ref[here, (block0 + b) * LANE : (block0 + b + 1) * LANE] = value
                square = square + (value * value + 1e-30)
        mean = jnp.sum(square, axis=1, keepdims=True) * (1.0 / width)
        row_new = DECAY * state_ref[rows, :] + (1.0 - DECAY) * mean
        new_ref[rows, :] = row_new
        for ref, block0, blocks, first in source:
            for b in range(blocks):
                lanes = slice((block0 + b) * LANE, (block0 + b + 1) * LANE)
                value = ref[first + at * blocks + b].astype(F32)
                change = value * lax.rsqrt(row_new * scaled_ref[0:1, lanes])
                new[here, lanes] = weight[here, lanes] - rate * change
        return carry

    if steps == 1:
        before()
        lax.fori_loop(0, groups, body, 0, unroll=5)
        after()
    else:
        pl.when(step == 0)(before)
        lax.fori_loop(0, groups, body, 0, unroll=5)
        pl.when(step == steps - 1)(after)


def sources_of(chunk, ref, rows):
    return {w: (ref, block0, blocks, first) for w, block0, blocks, first, _ in spans(chunk, rows)[0]}


def update_kernel(rows, copies_of, place_ref, mine_ref, other_ref, pack_ref, *refs):
    weights, states, col_states = refs[0:2], refs[2:4], refs[4:6]
    grads, news, rows_new, cols_new = refs[6:8], refs[8:10], refs[10:12], refs[12:14]
    conv_scratch, out_scratch = refs[14:18], refs[18:22]
    full1_ref, full2_ref, sem = refs[22:25]
    both = (mine_ref, other_ref)
    count = 2 * mine_ref.shape[0]
    step, steps = pl.program_id(0), pl.num_programs(0)

    @pl.when(step == 0)
    def _():
        copies = load_full(both, place_ref, 0, full1_ref, sem, 0)
        copies += load_full(both, place_ref, full1_ref.shape[0] // count, full2_ref, sem, count)
        run_copies(copies)

    from1 = sources_of(CHUNKS[0], full1_ref, rows)
    from2 = sources_of(CHUNKS[1], full2_ref, rows)

    def update(n, k, source, scratch, *steps):
        squares = pack_line(pack_ref, 2, LANE0[k], WIDTHS[k])
        update_weight(
            k, squares, pack_line(pack_ref, 3, 0, LANE)[:, k : k + 1] * (1.0 / copies_of), source, weights[n],
            states[n], col_states[n], grads[n], news[n], rows_new[n], cols_new[n], scratch, *steps,
        )

    update(0, 1, [from1[1], from2[1]], conv_scratch, step, UPDATE_STEPS)

    @pl.when(step == steps - 1)
    def _():
        update(1, 2, [from1[2]], out_scratch)


def update_in_kernel(
    rows, copies_of, place_ref, mine_ref, other_ref, pack_in_ref, pack_ref, np_ref, second_ref, *refs
):
    weight, state, col_state, grad_ref, new_ref, row_new_ref, col_new_ref = refs[0:7]
    ngrad_ref, nsecond_ref, nnew_ref = refs[7:10]
    full_ref, sem = refs[14:16]
    copies = load_halves(mine_ref, other_ref, place_ref, full_ref, sem)
    for copy in copies:
        copy.start()
    lines = [pack_line(pack_ref, row, 0, D + 2 * INNER) for row in range(2)]
    grad = jnp.concatenate(lines, axis=0)
    second = DECAY * second_ref[...] + (1.0 - DECAY) * (grad * grad + 1e-30)
    ngrad_ref[...] = grad
    nsecond_ref[...] = second
    nnew_ref[...] = np_ref[...] - 0.2 * grad * lax.rsqrt(second)
    for copy in copies:
        copy.wait()
    update_weight(
        0, pack_in_ref[0:1, :], pack_line(pack_ref, 3, 0, LANE)[:, 0:1] * (1.0 / copies_of),
        [sources_of(CHUNKS[2], full_ref, rows)[0]], weight, state, col_state, grad_ref, new_ref,
        row_new_ref, col_new_ref, refs[10:14],
    )


class Places:
    def __init__(self):
        self.seq, self.fsdp = lax.axis_size("seq"), lax.axis_size("fsdp")
        self.q = lax.axis_index("fsdp")
        self.s = lax.axis_index("seq")

    def flip(self, x, axis, bit):
        pairs = []
        for s in range(self.seq):
            for f in range(self.fsdp):
                s2, f2 = (s ^ bit, f) if axis == "seq" else (s, f ^ bit)
                pairs.append((s * self.fsdp + f, s2 * self.fsdp + f2))
        return lax.ppermute(x, AXES, pairs)


def bits_of(count):
    return [1 << k for k in range(count.bit_length() - 1)]


def tie(x, *others):
    return lax.optimization_barrier((x, *others))[0]


def gather_pieces(piece, place, after, later=()):
    found = {0: piece}
    for bit in reversed(bits_of(place.fsdp)):
        for k in list(found):
            moving = found[k]
            if bit == 1:
                moving = tie(moving, *((after,) if k == 0 or not later else later))
            found[k | bit] = place.flip(moving, "fsdp", bit)
    return [found[k] for k in range(place.fsdp)]


def sum_over(x, place, *axes):
    for axis in axes:
        for bit in bits_of(getattr(place, axis)):
            x = x + place.flip(x, axis, bit)
    return x


def sum_along_z(x, place):
    terms = [x] + [place.flip(x, "seq", 2 * k) for k in range(1, place.seq // 2)]
    while len(terms) > 1:
        terms = [a + b for a, b in zip(terms[::2], terms[1::2])]
    return terms[0]


def pick(x, index, axis):
    return lax.dynamic_index_in_dim(x, index, axis=axis, keepdims=False)


class Reduction:
    def __init__(self, place, keep, send):
        self.place, self.near = place, keep
        self.got = place.flip(send, "fsdp", 1)

    def halve(self, axis, side, flip_axis, bit):
        dims = self.near.shape
        parts = dims[:axis] + (2, dims[axis] // 2) + dims[axis + 1 :]
        near, got = self.near.reshape(parts), self.got.reshape(parts)
        away = pick(near, 1 - side, axis).astype(F32) + pick(got, 1 - side, axis).astype(F32)
        self.near = pick(near, side, axis).astype(F32) + pick(got, side, axis).astype(F32)
        away = away.astype(BF16)
        self.got = self.place.flip(away, flip_axis, bit)
        return away

    def x(self):
        bit = self.place.fsdp // 2
        while bit > 1:
            away = self.halve(0, (self.place.q // bit) % 2, "fsdp", bit)
            bit //= 2
        return away

    def y(self):
        return self.halve(1, self.place.s % 2, "seq", 1)

    def whole_half(self):
        self.near = self.rounded(self.near + self.got.astype(F32))

    def rounded(self, total):
        return lax.optimization_barrier(total.astype(BF16))

    def send_half(self, bit):
        self.got = self.place.flip(self.near, "seq", bit)

    def add_half(self):
        self.near = self.rounded(self.near.astype(F32) + self.got.astype(F32))

    def pieces(self):
        total = (self.near + self.got.astype(F32)).astype(BF16)
        return total.reshape((self.place.seq // 2, -1) + total.shape[2:])


def arrive(result, *reductions):
    result, *gots = lax.optimization_barrier((result, *[r.got for r in reductions]))
    for reduction, got in zip(reductions, gots):
        reduction.got = got
    return result


def summed_f32(got):
    return jnp.sum(got.astype(F32), axis=0)


def summed(got):
    return summed_f32(got).astype(BF16)


def exchange(place, sent):
    line = [[y + 2 * z for z in range(place.seq // 2)] for y in range(2)]
    return lax.all_to_all(sent, "seq", 0, 0, axis_index_groups=line)


def on_device(
    tokens, input_mask, doc_lengths, cotangent, w_in, w_conv, w_out, norm_params,
    row_in, col_in, row_conv, col_conv, row_out, col_out, norm_second,
):
    place = Places()
    rows = tokens.shape[0]
    pieces = place.fsdp
    spots = jnp.stack(
        [place.q, (place.s * place.fsdp + place.q) * rows, place.s, place.seq]
    ).astype(jnp.int32)
    docs = doc_lengths.shape[0]
    live = input_mask.reshape(-1, LANE)
    weights = (w_in, w_conv, w_out)
    rows_of = [w.shape[0] for w in weights]

    tile_a, tile = 256, 512
    steps = rows // tile
    params_spec = whole(2, D + 2 * INNER)
    dma = pltpu.SemaphoreType.DMA

    out_sides = (w_out[:, : D // 2], w_out[:, D // 2 :])
    conv_out = jnp.concatenate([w_conv, *out_sides], axis=0).astype(BF16)
    hidden_a, slope_a, xhat_a, rstd_a = call(
        norm_a_kernel,
        (rows // tile_a,),
        [rows_spec(tile_a, D), params_spec],
        [rows_spec(tile_a, D)] * 3 + [rows_spec(tile_a, LANE)],
        [shape((rows, D), BF16)] * 3 + [shape((rows, LANE), F32)],
        us=17,
    )(tokens, tie(norm_params, conv_out))

    in_pieces = gather_pieces(w_in.astype(BF16), place, hidden_a)

    def in_call(tiles, count, before):
        at, stride = tiles

        def here_spec(width):
            return pl.BlockSpec((tile, width), lambda i: (at + stride * i, 0))

        out_shapes = [shape((rows, INNER), BF16)] * 3 + [shape((rows, LANE), F32)] * 2
        out_specs = [here_spec(INNER)] * 3 + [here_spec(LANE)] * 2
        if at == 0:
            out_shapes += [shape((REACH, INNER), BF16)] * 2
            out_specs += [whole(REACH, INNER)] * 2
        return call(
            functools.partial(in_kernel, pieces, tiles),
            (count,),
            [SMEM, whole(docs), here_spec(D), whole(*live.shape), params_spec]
            + [ANY] * (pieces + len(before)),
            out_specs,
            out_shapes,
            [pltpu.VMEM((D, INNER), BF16), pltpu.VMEM((tile, INNER), F32)]
            + [pltpu.VMEM((8, docs + -docs % LANE), F32), dma((pieces,))],
            us=3,
            aliases={5 + pieces + k: k for k in range(len(before))},
        )(spots, doc_lengths, hidden_a, live, norm_params, *in_pieces, *before)

    *kept, m_first, m_last = in_call((0, steps - 1), 2, ())
    moved, slope_b, xhat_b, rstd_b, masks = in_call((1, 1), steps - 2, kept)

    def halo(inner, outer):
        total = place.seq * place.fsdp
        across = [(i, i + 1 if i % 2 else i - 1) for i in range(1, total - 1)]
        return place.flip(inner, "fsdp", 1), lax.ppermute(outer, AXES, across)

    m_inner, m_outer = halo(m_first, m_last)
    conv_pieces = gather_pieces(conv_out, place, m_first, (moved, m_inner, m_outer))

    ext = pltpu.VMEM((rows + 2 * REACH, INNER), BF16)
    taps_wide = KERNEL_TAPS * INNER
    wide = pltpu.VMEM((taps_wide, INNER), BF16)
    shards = place.fsdp // 2

    def half_dims(chunk):
        count = spans(chunk, rows_of)[1]
        return (shards, count + -count % place.seq, SUB, LANE)

    def tile_spec(width, ahead):
        return pl.BlockSpec((tile, width), lambda i: (jnp.clip(i + ahead, 0, steps - 1), 0))

    halves = [half_dims(CHUNKS[0])] * 2 + [half_dims(CHUNKS[1])] * 2
    work = pltpu.VMEM((tile, INNER), F32)
    turned_tile = pltpu.VMEM((INNER, tile), BF16)
    hidden_c, d_conv, d_first, d_last, sums_c, turned, keep1, send1, keep2, send2 = call(
        functools.partial(conv_kernel, pieces, rows_of),
        (steps + 1,),
        [SMEM, ANY, ANY, ANY, tile_spec(LANE, 0), tile_spec(D, 0), tile_spec(D, -1), params_spec]
        + [ANY] * pieces,
        [tile_spec(INNER, 0)] * 2
        + [whole(REACH, INNER), whole(REACH, INNER), whole(2, INNER)]
        + [ANY] * 5,
        [
            shape((rows, INNER), BF16),
            shape((rows, INNER), BF16),
            shape((REACH, INNER), BF16),
            shape((REACH, INNER), BF16),
            shape((2, INNER), F32),
            shape((taps_wide, INNER), BF16),
        ]
        + [shape(dims, BF16) for dims in halves],
        [ext, wide, wide, pltpu.VMEM((INNER, D), BF16), pltpu.VMEM((D, INNER), BF16)]
        + [pltpu.VMEM((2, tile, taps_wide), BF16), work, work, work, turned_tile, turned_tile]
        + [pltpu.VMEM((INNER, taps_wide), F32), pltpu.VMEM((INNER, D), F32)]
        + [pltpu.VMEM((16, INNER), F32)]
        + [pltpu.VMEM((2,) + halves[0], BF16), pltpu.VMEM((2,) + halves[2], BF16)]
        + [dma((3 + 3 * pieces,))],
        us=45,
    )(
        spots, m_inner, moved, m_outer, masks, cotangent, cotangent, norm_params, *conv_pieces
    )
    d_inner, d_outer = halo(d_first, d_last)
    first, second = Reduction(place, keep1, send1), Reduction(place, keep2, send2)
    (block_out,) = call(
        functools.partial(out_kernel, pieces),
        (steps,),
        [SMEM, rows_spec(tile, INNER), rows_spec(tile, D)] + [ANY] * pieces,
        [rows_spec(tile, D)],
        [shape((rows, D), BF16)],
        [pltpu.VMEM((INNER, D), BF16), dma((2 * pieces,))],
        us=9,
    )(spots, hidden_c, tokens, *conv_pieces)

    def back_conv(last, spots, before):
        here = steps // 2
        at = here * last

        def here_spec(width):
            return pl.BlockSpec((tile, width), lambda i: (i + at, 0))

        dims = half_dims(CHUNKS[2])
        return call(
            functools.partial(back_conv_kernel, last, w_in.shape[0]),
            (here,),
            [SMEM] + [ANY] * 4
            + [here_spec(LANE), here_spec(INNER), here_spec(LANE), here_spec(INNER), here_spec(D)]
            + [params_spec]
            + [ANY] * last,
            [rows_spec(tile, INNER), whole(2, INNER)] + [ANY] * (1 + last),
            [shape((rows // 2, INNER), BF16), shape((2, INNER), F32)]
            + ([shape(dims, BF16)] * 2 if last else [shape((INNER, D), F32)]),
            ([pltpu.VMEM((2,) + dims, BF16)] if last else [])
            + [
                ext,
                wide,
                pltpu.VMEM((tile, taps_wide), BF16),
                pltpu.VMEM((tile, INNER), F32),
                pltpu.VMEM((INNER, D), F32),
                pltpu.VMEM((16, INNER), F32),
                dma((5,)),
            ],
            us=16,
        )(
            spots, d_inner, d_conv, d_outer, turned, masks, xhat_b, rstd_b, slope_b, hidden_a,
            norm_params, *before,
        )

    block_out, d_inner, d_outer = arrive((block_out, d_inner, d_outer), first, second)
    away = (first.x(), second.y())
    d_pre0, sums_b0, grad_part = back_conv(0, tie(spots, *away), ())
    d_pre0 = arrive(d_pre0, first, second)
    away = (first.y(), second.x())
    d_pre1, sums_b1, keep, send = back_conv(1, tie(spots, *away), (grad_part,))
    send = arrive(send, first, second)
    third = Reduction(place, keep, send)
    sent = jnp.concatenate([first.pieces(), second.pieces()], axis=1)
    got = exchange(place, sent)
    third.got = tie(third.got, sent)
    away = (sent, third.x())
    input_grad, sums_a = call(
        functools.partial(back_a_kernel, pieces, steps // 2),
        (steps,),
        [SMEM]
        + [
            pl.BlockSpec((tile, INNER), lambda i: (jnp.minimum(i, steps // 2 - 1), 0)),
            pl.BlockSpec((tile, INNER), lambda i: (jnp.maximum(i - steps // 2, 0), 0)),
        ]
        + [rows_spec(tile, D), rows_spec(tile, LANE), rows_spec(tile, D), rows_spec(tile, D)]
        + [params_spec]
        + [ANY] * pieces,
        [rows_spec(tile, D), whole(2, D)],
        [shape((rows, D), F32), shape((2, D), F32)],
        [
            pltpu.VMEM((D, INNER), BF16),
            pltpu.VMEM((INNER, D), BF16),
            pltpu.VMEM((tile, D), F32),
            pltpu.VMEM((16, D), F32),
            dma((pieces,)),
        ],
        us=17,
    )(
        tie(spots, *away), d_pre0, d_pre1, xhat_a, rstd_a, slope_a, cotangent, norm_params, *in_pieces
    )

    row_states, col_states = (row_in, row_conv, row_out), (col_in, col_conv, col_out)
    row_specs = [whole(*r.shape) for r in row_states]
    col_specs = [whole(*c.shape) for c in col_states]
    cols_all = D + 2 * INNER
    pack_dims = (4 * PACK_BLOCKS // SUB, SUB, LANE)
    pack_spec = whole(*pack_dims)
    fulls = [pltpu.VMEM(half_dims(c)[1:], BF16) for c in CHUNKS]
    sums = (sums_a, sums_b0, sums_b1, sums_c)
    got, third.got, input_grad = lax.optimization_barrier((got, third.got, input_grad))
    part = summed(got)
    sent = jnp.broadcast_to(part[None], (place.seq // 2,) + part.shape)
    mine = exchange(place, sent)
    third.got = tie(third.got, sent)
    away = third.y()
    (pack,) = call(
        functools.partial(pack_kernel, rows_of, [half_dims(c)[1] // place.seq for c in CHUNKS]),
        (1,),
        [SMEM, whole(*part.shape)] + row_specs + [whole(*x.shape) for x in sums],
        [pack_spec],
        [shape(pack_dims, F32)],
        [pltpu.VMEM((cols_all // LANE + 1, SUB, LANE), F32)],
        us=2,
        mib=16,
    )(tie(spots, away), part, *row_states, *sums)
    pack = sum_over(pack, place, "fsdp")
    third.got, pack = lax.optimization_barrier((third.got, pack))
    seq_bits = bits_of(place.seq)
    third.whole_half()
    for bit in seq_bits[1:-1]:
        third.send_half(bit)
        pack = pack + place.flip(pack, "seq", 1) if bit == 2 else pack
        if bit != seq_bits[-2]:
            third.add_half()
    mine, third.got, pack = lax.optimization_barrier((mine, third.got, pack))
    other = place.flip(mine, "seq", 1)
    third.add_half()
    third.send_half(seq_bits[-1])
    pack = sum_along_z(pack, place)
    third.got, other, pack = lax.optimization_barrier((third.got, other, pack))
    third.add_half()
    line = third.near.reshape(third.near.shape[1:])
    line_other = place.flip(line, "seq", 1)

    def update_scratch(weight):
        lines = weight.shape[0] + -weight.shape[0] % LANE
        return (
            [pltpu.VMEM((8, lines), F32)]
            + [pltpu.VMEM((lines, LANE), F32)] * 2
            + [pltpu.VMEM((8, weight.shape[1]), F32)]
        )

    weight_specs = [whole(*w.shape) for w in weights]
    conv_block = pl.BlockSpec((w_conv.shape[0] // UPDATE_STEPS, INNER), lambda i: (i, 0))
    both_specs = [conv_block, weight_specs[2]]
    results = call(
        functools.partial(update_kernel, rows_of, place.seq),
        (UPDATE_STEPS,),
        [SMEM, ANY, ANY, pack_spec] + both_specs + row_specs[1:] + col_specs[1:],
        both_specs * 2 + row_specs[1:] + col_specs[1:],
        [shape(w.shape, F32) for w in weights[1:]] * 2
        + [shape(r.shape, F32) for r in row_states[1:] + col_states[1:]],
        update_scratch(w_conv)
        + update_scratch(w_out)
        + fulls[:2]
        + [dma((2 * place.seq,))],
        us=8,
        mib=32,
    )(spots, mine, other, pack, *weights[1:], *row_states[1:], *col_states[1:])
    grad_conv, grad_out, new_conv, new_out, row_conv_new, row_out_new, col_conv_new, col_out_new = (
        results
    )
    line_other, grad_out = lax.optimization_barrier((line_other, grad_out))
    (pack_in,) = call(
        functools.partial(pack_in_kernel, rows_of),
        (1,),
        [SMEM, ANY, ANY],
        [whole(8, INNER)],
        [shape((8, INNER), F32)],
        [fulls[2], dma((place.seq,))],
        us=2,
        mib=16,
    )(spots, line, line_other)
    pack_in = sum_over(pack_in, place, "fsdp")
    grad_in, new_in, row_in_new, col_in_new, *norm_results = call(
        functools.partial(update_in_kernel, rows_of, place.seq),
        (1,),
        [SMEM, ANY, ANY, whole(8, INNER), pack_spec, params_spec, params_spec]
        + [weight_specs[0], row_specs[0], col_specs[0]],
        [weight_specs[0]] * 2 + [row_specs[0], col_specs[0]] + [params_spec] * 3,
        [shape(w_in.shape, F32)] * 2
        + [shape(row_in.shape, F32), shape(col_in.shape, F32)]
        + [shape((2, cols_all), F32)] * 3,
        update_scratch(w_in) + [fulls[2], dma((place.seq,))],
        us=4,
        mib=24,
    )(
        spots, line, line_other, pack_in, pack, norm_params, norm_second, w_in, row_in, col_in
    )
    return (
        block_out,
        input_grad,
        grad_in,
        grad_conv,
        grad_out,
        new_in,
        new_conv,
        new_out,
        row_in_new,
        col_in_new,
        row_conv_new,
        col_conv_new,
        row_out_new,
        col_out_new,
        *norm_results,
    )


def solution(mesh):
    both, rows = P(AXES, None), P("fsdp", None)
    in_specs = (
        both, P(AXES), P(), both, rows, rows, rows, P(),
        P("fsdp"), P(), P("fsdp"), P(), P("fsdp"), P(), P(),
    )
    out_specs = (
        both, both, rows, rows, rows, rows, rows, rows,
        P("fsdp"), P(), P("fsdp"), P(), P("fsdp"), P(), P(), P(), P(),
    )
    return jax.shard_map(
        on_device, mesh=mesh, in_specs=in_specs, out_specs=out_specs, check_vma=False
    )
```

profile of v0, /device:TPU:0, one launch (start us, length us, event | category | flops | bytes accessed | tf_op | source)
XLA Modules:
  0.0 256.6 jit_solution(5755219946211417796)
XLA Ops:
  0.7 1.3 convert_element_type.205.refs_0_
  2.0 3.0 %collective-permute-start.1 = (bf16[320,640]{1,0:T(8,128)(2,1)S(1)}, bf16[320,640]{1,0:T(8,128)(2,1)S(1)}, u32[]{:S(2)}, u32[]{:S(2)}) collective-permute-start(bf16[320,640]{1,0:T(8,128)(2,1)S(1)} %convert_element_type.205.refs_0_), channel_id=1, source_target_pairs={{0,2},{1,3},{2,0},{3,1},{4,6},{5,7},{6,4},{7,5},{8,10},{9,11},{10,... | collective-permute-start | bytes 1228808 | tf_op jit(solution)/shard_map/ppermute | solution.py:844
  6.0 16.8 %shard_map.278 = (bf16[2048,1280]{1,0:T(8,128)(2,1)}, bf16[2048,1280]{1,0:T(8,128)(2,1)}, bf16[2048,1280]{1,0:T(8,128)(2,1)}, f32[2048,128]{1,0:T(8,128)}) custom-call(bf16[2048,1280]{1,0:T(8,128)(2,1)} %tok_ref.3, f32[2,2560]{1,0:T(2,128)} %np_ref.14), custom_call_target="tpu_custom_call" | custom-call | flops 18699999232 | bytes 57800000 | tf_op jit(solution)/shard_map/pallas_call | solution.py:968
  25.9 9.9 %shard_map.279 = (bf16[2048,640]{1,0:T(8,128)(2,1)}, bf16[2048,640]{1,0:T(8,128)(2,1)}, bf16[2048,640]{1,0:T(8,128)(2,1)}, f32[2048,128]{1,0:T(8,128)}, f32[2048...) custom-call(s32[4]{0:T(128)} %pad_add_fusion.place_ref, s32[129]{0:T(256)} %lengths_ref.3, ...), custom_call_target="tpu_custom_call" | custom-call | flops 3300000000 | bytes 10200000 | tf_op jit(solution)/shard_map/pallas_call | solution.py:990
  36.7 2.9 %collective-permute-start.5 = (bf16[1120,640]{1,0:T(8,128)(2,1)S(1)}, bf16[1120,640]{1,0:T(8,128)(2,1)S(1)}, u32[]{:S(2)}, u32[]{:S(2)}) collective-permute-start(bf16[1120,640]{1,0:T(8,128)(2,1)S(1)} %pad_maximum_fusion.refs_0_), channel_id=1, source_target_pairs={{0,1},{1,0},{2,3},{3,2},{4,5},{5,4},{6,7},{7,6},{8,9},{9,8},{10,11... | collective-permute-start | bytes 4300808 | tf_op jit(solution)/shard_map/ppermute | solution.py:844
  39.6 9.6 %shard_map.280 = (bf16[2048,640]{1,0:T(8,128)(2,1)}, bf16[2048,640]{1,0:T(8,128)(2,1)}, bf16[2048,640]{1,0:T(8,128)(2,1)}, f32[2048,128]{1,0:T(8,128)}, f32[2048,128]{1,0:T(8,128)}) custom-call(s32[4]{0:T(128)} %pad_add_fusion.place_ref, s32[129]{0:T(256)} %lengths_ref.3, ...), custom_call_target="tpu_custom_call", output_to_operand_aliasing={{0}: (9, {}), {1}: (10, {}), {2}: (11, {}), {3}: (12, {}), ... | custom-call | flops 3300000000 | bytes 10200000 | tf_op jit(solution)/shard_map/pallas_call | solution.py:990
  49.3 2.8 %collective-permute-start.7 = (bf16[1120,640]{1,0:T(8,128)(2,1)}, bf16[1120,640]{1,0:T(8,128)(2,1)S(1)}, u32[]{:S(2)}, u32[]{:S(2)}) collective-permute-start(bf16[1120,640]{1,0:T(8,128)(2,1)} %collective-permute-done.6.refs_2_), channel_id=1, source_target_pairs={{0,1},{1,0},{2,3},{3,2},{4,5},{5,4},{6,7},{7,6},{8,9},{9,8},{10,11... | collective-permute-start | bytes 4300808 | tf_op jit(solution)/shard_map/ppermute | solution.py:844
  52.1 3.0 %collective-permute-done.7.refs_3_ = bf16[1120,640]{1,0:T(8,128)(2,1)S(1)} collective-permute-done((bf16[1120,640]{1,0:T(8,128)(2,1)}, bf16[1120,640]{1,0:T(8,128)(2,1)S(1)}, u32[]{:S(2)}, u32[]{:S(2)}) %collective-permute-start.7) | collective-permute-done | bytes 1433632 | tf_op jit(solution)/shard_map/ppermute | solution.py:844
  55.1 1.1 copy-done.30
  56.2 54.6 %shard_map.281 = (bf16[2048,640]{1,0:T(8,128)(2,1)}, bf16[2048,640]{1,0:T(8,128)(2,1)}, bf16[256,640]{1,0:T(8,128)(2,1)}, bf16[256,640]{1,0:T(8,128)(2,1)}, f32[...) custom-call(s32[4]{0:T(128)} %pad_add_fusion.place_ref, ...), custom_call_target="tpu_custom_call" | custom-call | flops 49500000256 | bytes 153000000 | tf_op jit(solution)/shard_map/pallas_call | solution.py:1029
  112.5 10.1 %shard_map.282 = bf16[2048,1280]{1,0:T(8,128)(2,1)} custom-call(s32[4]{0:T(128)} %pad_add_fusion.place_ref, bf16[2048,640]{1,0:T(8,128)(2,1)} %get-tuple-element.117.hid_ref, bf16[2048,1280]{1,0:T(8,128)(2,1)} %tok_ref.3, bf16[1120,640]{1,0:T(8,128)(2,1)} %copy-done.22, bf16[1120,640]{1,0:T(8,128)(2,1)} %copy-done.29, ...), custom_call_target="tpu_custom_call" | custom-call | flops 9900000256 | bytes 30600000 | tf_op jit(solution)/shard_map/pallas_call | solution.py:1058
  122.7 0.7 copy-done.32
  123.4 1.1 convert_add_fusion.1
  124.5 5.1 %collective-permute-start.13 = (bf16[2,76,16,128]{3,2,1,0:T(8,128)(2,1)}, bf16[2,76,16,128]{3,2,1,0:T(8,128)(2,1)S(1)}, u32[]{:S(2)}, u32[]{:S(2)}) collective-permute-start(bf16[2,76,16,128]{3,2,1,0:T(8,128)(2,1)} %get-tuple-element.190), channel_id=1, source_target_pairs={{0,4},{1,5},{2,6},{3,7},{4,0},{5,1},{6,2},{7,3},{8,12},{9,13},{10,... | collective-permute-start | bytes 1867784 | tf_op jit(solution)/shard_map/ppermute | solution.py:844
  130.1 16.7 %shard_map.283 = (bf16[1024,640]{1,0:T(8,128)(2,1)}, f32[2,640]{1,0:T(2,128)}, f32[640,1280]{1,0:T(8,128)}) custom-call(s32[4]{0:T(128)} %pad_add_fusion.place_ref, bf16[256,640]{1,0:T(8,128)(2,1)} %copy-done.31, bf16[2048,640]{1,0:T(8,128)(2,1)} %get-tuple-element.129.d_ref, bf16[256,640]{1,0:T(8,128)(2,1)} %copy-done.32, ...), custom_call_target="tpu_custom_call" | custom-call | flops 17600000000 | bytes 54400000 | tf_op jit(solution)/shard_map/pallas_call | solution.py:1076
  146.9 2.8 %collective-permute-done.12 = bf16[1,200,16,128]{3,2,1,0:T(8,128)(2,1)S(1)} collective-permute-done((bf16[1,200,16,128]{3,2,1,0:T(8,128)(2,1)S(1)}, bf16[1,200,16,128]{3,2,1,0:T(8,128)(2,1)S(1)}, u32[]{:S(2)}, u32[]{:S(2)}) %collective-permute-start.12) | collective-permute-done | bytes 819232 | tf_op jit(solution)/shard_map/ppermute | solution.py:844
  149.8 1.3 collective-permute-start.15
  151.2 0.9 collective-permute-start.14
  152.0 17.4 %shard_map.284 = (bf16[1024,640]{1,0:T(8,128)(2,1)}, f32[2,640]{1,0:T(2,128)}, bf16[2,104,16,128]{3,2,1,0:T(8,128)(2,1)}, bf16[2,104,16,128]{3,2,1,0:T(8,128)(2,1)}) custom-call(s32[4]{0:T(128)} %pad_add_fusion.place_ref, bf16[256,640]{1,0:T(8,128)(2,1)} %copy-done.31, bf16[2048,640]{1,0:T(8,128)(2,1)} %get-tuple-element.129.d_ref, ...), custom_call_target="tpu_custom_call" | custom-call | flops 17600000000 | bytes 54400000 | tf_op jit(solution)/shard_map/pallas_call | solution.py:1076
  169.6 1.1 fusion.3
  170.8 0.9 pad_maximum_fusion.1
  171.7 4.8 %all-to-all-start = ((bf16[4,44,16,128]{3,2,1,0:T(8,128)(2,1)}), bf16[4,44,16,128]{3,2,1,0:T(8,128)(2,1)S(1)}, u32[]{:S(2)}, u32[]{:S(2)}) async-start(bf16[4,44,16,128]{3,2,1,0:T(8,128)(2,1)} %pad_maximum_fusion.1), calls=%async_computation | async-start | bytes 1441792 | tf_op jit(solution)/shard_map/all_to_all | solution.py:943
  176.5 1.0 convert_add_fusion.2
  177.5 1.5 collective-permute-start.17
  179.0 17.1 %shard_map.285 = (f32[2048,1280]{1,0:T(8,128)}, f32[2,1280]{1,0:T(2,128)}) custom-call(s32[4]{0:T(128)} %pad_add_fusion.place_ref, bf16[1024,640]{1,0:T(8,128)(2,1)} %get-tuple-element.147.dpre0_ref, bf16[1024,640]{1,0:T(8,128)(2,1)} %get-tuple-element.148.dpre1_ref, bf16[2048,1280]{1,0:T(8,128)(2,1)} %get-tuple-element.149.xhat_ref, ...), custom_call_target="tpu_custom_call" | custom-call | flops 18699999232 | bytes 57800000 | tf_op jit(solution)/shard_map/pallas_call | solution.py:1114
  196.3 1.0 broadcast_in_dim.2
  197.3 5.1 %all-to-all-start.1 = ((bf16[4,44,16,128]{3,2,1,0:T(8,128)(2,1)}), bf16[4,44,16,128]{3,2,1,0:T(8,128)(2,1)}, u32[]{:S(2)}, u32[]{:S(2)}) async-start(bf16[4,44,16,128]{3,2,1,0:T(8,128)(2,1)} %broadcast_in_dim.2), calls=%async_computation.1 | async-start | bytes 1441792 | tf_op jit(solution)/shard_map/all_to_all | solution.py:943
  202.4 0.9 collective-permute-start.18
  203.4 1.0 shard_map.286
  204.6 1.2 collective-permute-done.19
  206.3 3.5 %collective-permute-done.20 = f32[5,16,128]{2,1,0:T(8,128)S(1)} collective-permute-done((f32[5,16,128]{2,1,0:T(8,128)S(1)}, f32[5,16,128]{2,1,0:T(8,128)S(1)}, u32[]{:S(2)}, u32[]{:S(2)}) %collective-permute-start.20) | collective-permute-done | bytes 40992 | tf_op jit(solution)/shard_map/ppermute | solution.py:844
  209.9 2.1 collective-permute-start.21
  212.0 1.2 collective-permute-start.22
  213.2 2.8 %collective-permute-done.22 = f32[5,16,128]{2,1,0:T(8,128)S(1)} collective-permute-done((f32[5,16,128]{2,1,0:T(8,128)S(1)}, f32[5,16,128]{2,1,0:T(8,128)S(1)}, u32[]{:S(2)}, u32[]{:S(2)}) %collective-permute-start.22) | collective-permute-done | bytes 40992 | tf_op jit(solution)/shard_map/ppermute | solution.py:844
  216.0 3.2 %collective-permute-done.21 = bf16[1,52,16,128]{3,2,1,0:T(8,128)(2,1)S(1)} collective-permute-done((bf16[1,52,16,128]{3,2,1,0:T(8,128)(2,1)S(1)}, bf16[1,52,16,128]{3,2,1,0:T(8,128)(2,1)S(1)}, u32[]{:S(2)}, u32[]{:S(2)}) %collective-permute-start.21) | collective-permute-done | bytes 213024 | tf_op jit(solution)/shard_map/ppermute | solution.py:844
  219.2 1.8 all-to-all-done.1.mine_ref
  221.0 0.8 collective-permute-start.24
  221.9 3.4 %collective-permute-start.26 = (f32[5,16,128]{2,1,0:T(8,128)S(1)}, f32[5,16,128]{2,1,0:T(8,128)S(1)}, u32[]{:S(2)}, u32[]{:S(2)}) collective-permute-start(f32[5,16,128]{2,1,0:T(8,128)S(1)} %add.213), channel_id=1, source_target_pairs={{0,16},{1,17},{2,18},{3,19},{4,20},{5,21},{6,22},{7,23},{8,24},{9,... | collective-permute-start | bytes 122888 | tf_op jit(solution)/shard_map/ppermute | solution.py:844
  225.2 1.0 collective-permute-start.27
  226.3 1.3 collective-permute-start.23
  227.8 3.4 %collective-permute-done.27 = f32[5,16,128]{2,1,0:T(8,128)S(1)} collective-permute-done((f32[5,16,128]{2,1,0:T(8,128)S(1)}, f32[5,16,128]{2,1,0:T(8,128)S(1)}, u32[]{:S(2)}, u32[]{:S(2)}) %collective-permute-start.27) | collective-permute-done | bytes 40992 | tf_op jit(solution)/shard_map/ppermute | solution.py:844
  231.2 6.4 %collective-permute-done.23 = bf16[1,52,16,128]{3,2,1,0:T(8,128)(2,1)S(1)} collective-permute-done((bf16[1,52,16,128]{3,2,1,0:T(8,128)(2,1)S(1)}, bf16[1,52,16,128]{3,2,1,0:T(8,128)(2,1)S(1)}, u32[]{:S(2)}, u32[]{:S(2)}) %collective-permute-start.23) | collective-permute-done | bytes 213024 | tf_op jit(solution)/shard_map/ppermute | solution.py:844
  238.4 0.9 collective-permute-start.28
  239.3 7.5 %shard_map.287 = (f32[800,640]{1,0:T(8,128)}, f32[160,1280]{1,0:T(8,128)}, f32[800,640]{1,0:T(8,128)}, f32[160,1280]{1,0:T(8,128)}, f32[800]{0:T(1024)}, /*index=5*/f32[160]{0:T(256)}, f32[640]{0:T(1024)}, f32[1280]{0:T(1024)}) custom-call(s32[4]{0:T(128)S(1)} %copy-done.6, bf16[4,44,16,128]{3,2,1,0:T(8,128)(2,1)} %all-to-all-done.1.mine_ref, ...), custom_call_target="tpu_custom_call" | custom-call | flops 8800000000 | bytes 27200000 | tf_op jit(solution)/shard_map/pallas_call | solution.py:1193
  246.8 1.3 shard_map.288
  248.2 1.2 collective-permute-done.29
  249.9 3.2 %collective-permute-done.30 = f32[8,640]{1,0:T(8,128)S(1)} collective-permute-done((f32[8,640]{1,0:T(8,128)S(1)}, f32[8,640]{1,0:T(8,128)S(1)}, u32[]{:S(2)}, u32[]{:S(2)}) %collective-permute-start.30) | collective-permute-done | bytes 20512 | tf_op jit(solution)/shard_map/ppermute | solution.py:844
  253.2 3.1 %shard_map.289 = (f32[320,640]{1,0:T(8,128)}, f32[320,640]{1,0:T(8,128)}, f32[320]{0:T(512)}, f32[640]{0:T(1024)}, f32[2,2560]{1,0:T(2,128)}, /*index=5*/f32[2,2560]{1,0:T(2,128)}, f32[2,2560]{1,0:T(2,128)}) custom-call(s32[4]{0:T(128)S(1)} %copy-done.6, bf16[52,16,128]{2,1,0:T(8,128)(2,1)S(1)} %bitcast.39, ...), custom_call_target="tpu_custom_call" | custom-call | flops 4400000000 | bytes 13600000 | tf_op jit(solution)/shard_map/pallas_call | solution.py:1222
  (126 shorter events, 10.2 us)
Async XLA Ops:
  2.0 20.8 %copy-start.21 = (bf16[320,640]{1,0:T(8,128)(2,1)}, bf16[320,640]{1,0:T(8,128)(2,1)S(1)}, u32[]{:S(2)}) copy-start(bf16[320,640]{1,0:T(8,128)(2,1)S(1)} %convert_element_type.205.refs_0_) | copy-start | bytes 1228804
  2.0 20.8 %collective-permute-start.1 = (bf16[320,640]{1,0:T(8,128)(2,1)S(1)}, bf16[320,640]{1,0:T(8,128)(2,1)S(1)}, u32[]{:S(2)}, u32[]{:S(2)}) collective-permute-start(bf16[320,640]{1,0:T(8,128)(2,1)S(1)} %convert_element_type.205.refs_0_), channel_id=1, source_target_pairs={{0,2},{1,3},{2,0},{3,1},{4,6},{5,7},{6,4},{7,5},{8,10},{9,11},{10,... | collective-permute-start | bytes 1228808 | tf_op jit(solution)/shard_map/ppermute | solution.py:844
  5.4 31.3 %copy-start.22 = (bf16[1120,640]{1,0:T(8,128)(2,1)}, bf16[1120,640]{1,0:T(8,128)(2,1)S(1)}, u32[]{:S(2)}) copy-start(bf16[1120,640]{1,0:T(8,128)(2,1)S(1)} %pad_maximum_fusion.refs_0_) | copy-start | bytes 4300804
  5.4 43.9 %collective-permute-start.6 = (bf16[1120,640]{1,0:T(8,128)(2,1)S(1)}, bf16[1120,640]{1,0:T(8,128)(2,1)}, u32[]{:S(2)}, u32[]{:S(2)}) collective-permute-start(bf16[1120,640]{1,0:T(8,128)(2,1)S(1)} %pad_maximum_fusion.refs_0_), channel_id=1, source_target_pairs={{0,2},{1,3},{2,0},{3,1},{4,6},{5,7},{6,4},{7,5},{8,10},{9,11},{10,... | collective-permute-start | bytes 4300808 | tf_op jit(solution)/shard_map/ppermute | solution.py:844
  22.8 1.8 collective-permute-start
  22.9 2.3 collective-permute-start.2
  35.8 13.4 %collective-permute-start.3 = (bf16[256,640]{1,0:T(8,128)(2,1)}, bf16[256,640]{1,0:T(8,128)(2,1)S(1)}, u32[]{:S(2)}, u32[]{:S(2)}) collective-permute-start(bf16[256,640]{1,0:T(8,128)(2,1)} %get-tuple-element.106), channel_id=1, source_target_pairs={{0,1},{1,0},{2,3},{3,2},{4,5},{5,4},{6,7},{7,6},{8,9},{9,8},{10,11... | collective-permute-start | bytes 983048 | tf_op jit(solution)/shard_map/ppermute | solution.py:844
  36.1 13.2 %collective-permute-start.4 = (bf16[256,640]{1,0:T(8,128)(2,1)}, bf16[256,640]{1,0:T(8,128)(2,1)S(1)}, u32[]{:S(2)}, u32[]{:S(2)}) collective-permute-start(bf16[256,640]{1,0:T(8,128)(2,1)} %get-tuple-element.113), channel_id=1, source_target_pairs={{1,2},{2,1},{3,4},{4,3},{5,6},{6,5},{7,8},{8,7},{9,10},{10,9},{11,... | collective-permute-start | bytes 983048 | tf_op jit(solution)/shard_map/ppermute | solution.py:1009
  36.7 15.3 %collective-permute-start.5 = (bf16[1120,640]{1,0:T(8,128)(2,1)S(1)}, bf16[1120,640]{1,0:T(8,128)(2,1)S(1)}, u32[]{:S(2)}, u32[]{:S(2)}) collective-permute-start(bf16[1120,640]{1,0:T(8,128)(2,1)S(1)} %pad_maximum_fusion.refs_0_), channel_id=1, source_target_pairs={{0,1},{1,0},{2,3},{3,2},{4,5},{5,4},{6,7},{7,6},{8,9},{9,8},{10,11... | collective-permute-start | bytes 4300808 | tf_op jit(solution)/shard_map/ppermute | solution.py:844
  49.3 5.8 %collective-permute-start.7 = (bf16[1120,640]{1,0:T(8,128)(2,1)}, bf16[1120,640]{1,0:T(8,128)(2,1)S(1)}, u32[]{:S(2)}, u32[]{:S(2)}) collective-permute-start(bf16[1120,640]{1,0:T(8,128)(2,1)} %collective-permute-done.6.refs_2_), channel_id=1, source_target_pairs={{0,1},{1,0},{2,3},{3,2},{4,5},{5,4},{6,7},{7,6},{8,9},{9,8},{10,11... | collective-permute-start | bytes 4300808 | tf_op jit(solution)/shard_map/ppermute | solution.py:844
  110.9 11.8 %collective-permute-start.10 = (bf16[2,200,16,128]{3,2,1,0:T(8,128)(2,1)}, bf16[2,200,16,128]{3,2,1,0:T(8,128)(2,1)S(1)}, u32[]{:S(2)}, u32[]{:S(2)}) collective-permute-start(bf16[2,200,16,128]{3,2,1,0:T(8,128)(2,1)} %get-tuple-element.120), channel_id=1, source_target_pairs={{0,1},{1,0},{2,3},{3,2},{4,5},{5,4},{6,7},{7,6},{8,9},{9,8},{10,11... | collective-permute-start | bytes 4915208 | tf_op jit(solution)/shard_map/ppermute | solution.py:844
  111.3 11.3 %collective-permute-start.11 = (bf16[2,152,16,128]{3,2,1,0:T(8,128)(2,1)}, bf16[2,152,16,128]{3,2,1,0:T(8,128)(2,1)S(1)}, u32[]{:S(2)}, u32[]{:S(2)}) collective-permute-start(bf16[2,152,16,128]{3,2,1,0:T(8,128)(2,1)} %get-tuple-element.121), channel_id=1, source_target_pairs={{0,1},{1,0},{2,3},{3,2},{4,5},{5,4},{6,7},{7,6},{8,9},{9,8},{10,11... | collective-permute-start | bytes 3735560 | tf_op jit(solution)/shard_map/ppermute | solution.py:844
  111.4 11.2 %collective-permute-start.8 = (bf16[256,640]{1,0:T(8,128)(2,1)}, bf16[256,640]{1,0:T(8,128)(2,1)S(1)}, u32[]{:S(2)}, u32[]{:S(2)}) collective-permute-start(bf16[256,640]{1,0:T(8,128)(2,1)} %get-tuple-element.118), channel_id=1, source_target_pairs={{0,1},{1,0},{2,3},{3,2},{4,5},{5,4},{6,7},{7,6},{8,9},{9,8},{10,11... | collective-permute-start | bytes 983048 | tf_op jit(solution)/shard_map/ppermute | solution.py:844
  111.8 10.8 %collective-permute-start.9 = (bf16[256,640]{1,0:T(8,128)(2,1)}, bf16[256,640]{1,0:T(8,128)(2,1)S(1)}, u32[]{:S(2)}, u32[]{:S(2)}) collective-permute-start(bf16[256,640]{1,0:T(8,128)(2,1)} %get-tuple-element.119), channel_id=1, source_target_pairs={{1,2},{2,1},{3,4},{4,3},{5,6},{6,5},{7,8},{8,7},{9,10},{10,9},{11,... | collective-permute-start | bytes 983048 | tf_op jit(solution)/shard_map/ppermute | solution.py:1009
  112.5 10.9 %copy-start.23 = (bf16[2,152,16,128]{3,2,1,0:T(8,128)(2,1)S(1)}, bf16[2,152,16,128]{3,2,1,0:T(8,128)(2,1)}, u32[]{:S(2)}) copy-start(bf16[2,152,16,128]{3,2,1,0:T(8,128)(2,1)} %get-tuple-element.125) | copy-start | bytes 3735556
  124.5 22.3 %collective-permute-start.13 = (bf16[2,76,16,128]{3,2,1,0:T(8,128)(2,1)}, bf16[2,76,16,128]{3,2,1,0:T(8,128)(2,1)S(1)}, u32[]{:S(2)}, u32[]{:S(2)}) collective-permute-start(bf16[2,76,16,128]{3,2,1,0:T(8,128)(2,1)} %get-tuple-element.190), channel_id=1, source_target_pairs={{0,4},{1,5},{2,6},{3,7},{4,0},{5,1},{6,2},{7,3},{8,12},{9,13},{10,... | collective-permute-start | bytes 1867784 | tf_op jit(solution)/shard_map/ppermute | solution.py:844
  130.0 19.7 %collective-permute-start.12 = (bf16[1,200,16,128]{3,2,1,0:T(8,128)(2,1)S(1)}, bf16[1,200,16,128]{3,2,1,0:T(8,128)(2,1)S(1)}, u32[]{:S(2)}, u32[]{:S(2)}) collective-permute-start(bf16[1,200,16,128]{3,2,1,0:T(8,128)(2,1)S(1)} %get-tuple-element.187), channel_id=1, source_target_pairs={{0,2},{1,3},{2,0},{3,1},{4,6},{5,7},{6,4},{7,5},{8,10},{9,11},{10,... | collective-permute-start | bytes 2457608 | tf_op jit(solution)/shard_map/ppermute | solution.py:844
  146.9 22.6 %copy-start.25 = (bf16[2,76,16,128]{3,2,1,0:T(8,128)(2,1)}, bf16[2,76,16,128]{3,2,1,0:T(8,128)(2,1)S(1)}, u32[]{:S(2)}) copy-start(bf16[2,76,16,128]{3,2,1,0:T(8,128)(2,1)S(1)} %collective-permute-done.13) | copy-start | bytes 1867780
  149.8 19.7 %collective-permute-start.15 = (bf16[1,76,16,128]{3,2,1,0:T(8,128)(2,1)S(1)}, bf16[1,76,16,128]{3,2,1,0:T(8,128)(2,1)S(1)}, u32[]{:S(2)}, u32[]{:S(2)}) collective-permute-start(bf16[1,76,16,128]{3,2,1,0:T(8,128)(2,1)S(1)} %fusion.4), channel_id=1, source_target_pairs={{0,2},{1,3},{2,0},{3,1},{4,6},{5,7},{6,4},{7,5},{8,10},{9,11},{10,... | collective-permute-start | bytes 933896 | tf_op jit(solution)/shard_map/ppermute | solution.py:844
  151.2 18.3 %collective-permute-start.14 = (bf16[1,100,16,128]{3,2,1,0:T(8,128)(2,1)S(1)}, bf16[1,100,16,128]{3,2,1,0:T(8,128)(2,1)S(1)}, u32[]{:S(2)}, u32[]{:S(2)}) collective-permute-start(bf16[1,100,16,128]{3,2,1,0:T(8,128)(2,1)S(1)} %fusion.6), channel_id=1, source_target_pairs={{0,4},{1,5},{2,6},{3,7},{4,0},{5,1},{6,2},{7,3},{8,12},{9,13},{10,... | collective-permute-start | bytes 1228808 | tf_op jit(solution)/shard_map/ppermute | solution.py:844
  169.5 7.0 %collective-permute-start.16 = (bf16[2,104,16,128]{3,2,1,0:T(8,128)(2,1)}, bf16[2,104,16,128]{3,2,1,0:T(8,128)(2,1)S(1)}, u32[]{:S(2)}, u32[]{:S(2)}) collective-permute-start(bf16[2,104,16,128]{3,2,1,0:T(8,128)(2,1)} %get-tuple-element.144), channel_id=1, source_target_pairs={{0,1},{1,0},{2,3},{3,2},{4,5},{5,4},{6,7},{7,6},{8,9},{9,8},{10,11... | collective-permute-start | bytes 2555912 | tf_op jit(solution)/shard_map/ppermute | solution.py:844
  171.7 24.4 %all-to-all-start = ((bf16[4,44,16,128]{3,2,1,0:T(8,128)(2,1)}), bf16[4,44,16,128]{3,2,1,0:T(8,128)(2,1)S(1)}, u32[]{:S(2)}, u32[]{:S(2)}) async-start(bf16[4,44,16,128]{3,2,1,0:T(8,128)(2,1)} %pad_maximum_fusion.1), calls=%async_computation | async-start | bytes 1441792 | tf_op jit(solution)/shard_map/all_to_all | solution.py:943
  177.5 24.9 %copy-start.18 = (f32[1,104,16,128]{3,2,1,0:T(8,128)}, f32[1,104,16,128]{3,2,1,0:T(8,128)S(1)}, u32[]{:S(2)}) copy-start(f32[1,104,16,128]{3,2,1,0:T(8,128)S(1)} %get-tuple-element.191) | copy-start | bytes 2555908
  177.5 18.6 %collective-permute-start.17 = (bf16[1,104,16,128]{3,2,1,0:T(8,128)(2,1)}, bf16[1,104,16,128]{3,2,1,0:T(8,128)(2,1)S(1)}, u32[]{:S(2)}, u32[]{:S(2)}) collective-permute-start(bf16[1,104,16,128]{3,2,1,0:T(8,128)(2,1)} %get-tuple-element.192), channel_id=1, source_target_pairs={{0,2},{1,3},{2,0},{3,1},{4,6},{5,7},{6,4},{7,5},{8,10},{9,11},{10,... | collective-permute-start | bytes 1277960 | tf_op jit(solution)/shard_map/ppermute | solution.py:844
  196.3 7.1 %copy-start.6 = (s32[4]{0:T(128)S(1)}, s32[4]{0:T(128)}, u32[]{:S(2)}) copy-start(s32[4]{0:T(128)} %pad_add_fusion.place_ref) | copy-start | bytes 52
  196.3 7.1 %copy-start.9 = (f32[800]{0:T(1024)S(1)}, f32[800]{0:T(1024)}, u32[]{:S(2)}) copy-start(f32[800]{0:T(1024)} %refs_2_.4) | copy-start | bytes 9604
  196.3 7.1 %copy-start.12 = (f32[320]{0:T(512)S(1)}, f32[320]{0:T(512)}, u32[]{:S(2)}) copy-start(f32[320]{0:T(512)} %refs_1_.5) | copy-start | bytes 3844
  196.3 7.1 %copy-start.13 = (f32[160]{0:T(256)S(1)}, f32[160]{0:T(256)}, u32[]{:S(2)}) copy-start(f32[160]{0:T(256)} %refs_3_.1) | copy-start | bytes 1924
  196.3 7.0 %copy-start.14 = (f32[2,1280]{1,0:T(2,128)S(1)}, f32[2,1280]{1,0:T(2,128)}, u32[]{:S(2)}) copy-start(f32[2,1280]{1,0:T(2,128)} %get-tuple-element.158.refs_3_) | copy-start | bytes 30724
  196.3 7.0 %copy-start.15 = (f32[2,640]{1,0:T(2,128)S(1)}, f32[2,640]{1,0:T(2,128)}, u32[]{:S(2)}) copy-start(f32[2,640]{1,0:T(2,128)} %get-tuple-element.161.refs_6_) | copy-start | bytes 15364
  197.3 23.7 %all-to-all-start.1 = ((bf16[4,44,16,128]{3,2,1,0:T(8,128)(2,1)}), bf16[4,44,16,128]{3,2,1,0:T(8,128)(2,1)}, u32[]{:S(2)}, u32[]{:S(2)}) async-start(bf16[4,44,16,128]{3,2,1,0:T(8,128)(2,1)} %broadcast_in_dim.2), calls=%async_computation.1 | async-start | bytes 1441792 | tf_op jit(solution)/shard_map/all_to_all | solution.py:943
  202.4 7.3 %collective-permute-start.18 = (bf16[1,52,16,128]{3,2,1,0:T(8,128)(2,1)S(1)}, bf16[1,52,16,128]{3,2,1,0:T(8,128)(2,1)S(1)}, u32[]{:S(2)}, u32[]{:S(2)}) collective-permute-start(bf16[1,52,16,128]{3,2,1,0:T(8,128)(2,1)S(1)} %fusion.7), channel_id=1, source_target_pairs={{0,4},{1,5},{2,6},{3,7},{4,0},{5,1},{6,2},{7,3},{8,12},{9,13},{10,... | collective-permute-start | bytes 638984 | tf_op jit(solution)/shard_map/ppermute | solution.py:844
  204.4 34.8 %copy-start.1 = (f32[800,640]{1,0:T(8,128)S(1)}, f32[800,640]{1,0:T(8,128)}, u32[]{:S(2)}) copy-start(f32[800,640]{1,0:T(8,128)} %refs_0_.4) | copy-start | bytes 6144004
  204.4 34.8 %copy-start.3 = (f32[160,1280]{1,0:T(8,128)S(1)}, f32[160,1280]{1,0:T(8,128)}, u32[]{:S(2)}) copy-start(f32[160,1280]{1,0:T(8,128)} %refs_1_.4) | copy-start | bytes 2457604
  204.5 34.8 %copy-start.8 = (f32[1280]{0:T(1024)S(1)}, f32[1280]{0:T(1024)}, u32[]{:S(2)}) copy-start(f32[1280]{0:T(1024)} %refs_5_.1) | copy-start | bytes 15364
  204.5 34.8 %copy-start.10 = (f32[640]{0:T(1024)S(1)}, f32[640]{0:T(1024)}, u32[]{:S(2)}) copy-start(f32[640]{0:T(1024)} %refs_4_.1) | copy-start | bytes 7684
  204.5 1.3 collective-permute-start.19
  205.8 4.0 %collective-permute-start.20 = (f32[5,16,128]{2,1,0:T(8,128)S(1)}, f32[5,16,128]{2,1,0:T(8,128)S(1)}, u32[]{:S(2)}, u32[]{:S(2)}) collective-permute-start(f32[5,16,128]{2,1,0:T(8,128)S(1)} %add.210), channel_id=1, source_target_pairs={{0,2},{1,3},{2,0},{3,1},{4,6},{5,7},{6,4},{7,5},{8,10},{9,11},{10,... | collective-permute-start | bytes 122888 | tf_op jit(solution)/shard_map/ppermute | solution.py:844
  209.9 9.3 %collective-permute-start.21 = (bf16[1,52,16,128]{3,2,1,0:T(8,128)(2,1)S(1)}, bf16[1,52,16,128]{3,2,1,0:T(8,128)(2,1)S(1)}, u32[]{:S(2)}, u32[]{:S(2)}) collective-permute-start(bf16[1,52,16,128]{3,2,1,0:T(8,128)(2,1)S(1)} %fusion.5), channel_id=1, source_target_pairs={{0,8},{1,9},{2,10},{3,11},{4,12},{5,13},{6,14},{7,15},{8,0},{9,1},... | collective-permute-start | bytes 638984 | tf_op jit(solution)/shard_map/ppermute | solution.py:844
  212.0 4.0 %collective-permute-start.22 = (f32[5,16,128]{2,1,0:T(8,128)S(1)}, f32[5,16,128]{2,1,0:T(8,128)S(1)}, u32[]{:S(2)}, u32[]{:S(2)}) collective-permute-start(f32[5,16,128]{2,1,0:T(8,128)S(1)} %add.211), channel_id=1, source_target_pairs={{0,4},{1,5},{2,6},{3,7},{4,0},{5,1},{6,2},{7,3},{8,12},{9,13},{10,... | collective-permute-start | bytes 122888 | tf_op jit(solution)/shard_map/ppermute | solution.py:844
  221.0 17.3 %collective-permute-start.24 = (bf16[4,44,16,128]{3,2,1,0:T(8,128)(2,1)}, bf16[4,44,16,128]{3,2,1,0:T(8,128)(2,1)S(1)}, u32[]{:S(2)}, u32[]{:S(2)}) collective-permute-start(bf16[4,44,16,128]{3,2,1,0:T(8,128)(2,1)} %all-to-all-done.1.mine_ref), channel_id=1, source_target_pairs={{0,4},{1,5},{2,6},{3,7},{4,0},{5,1},{6,2},{7,3},{8,12},{9,13},{10,... | collective-permute-start | bytes 2162696 | tf_op jit(solution)/shard_map/ppermute | solution.py:844
  221.8 5.7 %collective-permute-start.25 = (f32[5,16,128]{2,1,0:T(8,128)S(1)}, f32[5,16,128]{2,1,0:T(8,128)S(1)}, u32[]{:S(2)}, u32[]{:S(2)}) collective-permute-start(f32[5,16,128]{2,1,0:T(8,128)S(1)} %add.213), channel_id=1, source_target_pairs={{0,8},{1,9},{2,10},{3,11},{4,12},{5,13},{6,14},{7,15},{8,0},{9,1},... | collective-permute-start | bytes 122888 | tf_op jit(solution)/shard_map/ppermute | solution.py:844
  221.9 5.9 %collective-permute-start.26 = (f32[5,16,128]{2,1,0:T(8,128)S(1)}, f32[5,16,128]{2,1,0:T(8,128)S(1)}, u32[]{:S(2)}, u32[]{:S(2)}) collective-permute-start(f32[5,16,128]{2,1,0:T(8,128)S(1)} %add.213), channel_id=1, source_target_pairs={{0,16},{1,17},{2,18},{3,19},{4,20},{5,21},{6,22},{7,23},{8,24},{9,... | collective-permute-start | bytes 122888 | tf_op jit(solution)/shard_map/ppermute | solution.py:844
  225.2 5.9 %collective-permute-start.27 = (f32[5,16,128]{2,1,0:T(8,128)S(1)}, f32[5,16,128]{2,1,0:T(8,128)S(1)}, u32[]{:S(2)}, u32[]{:S(2)}) collective-permute-start(f32[5,16,128]{2,1,0:T(8,128)S(1)} %add.213), channel_id=1, source_target_pairs={{0,24},{1,25},{2,26},{3,27},{4,28},{5,29},{6,30},{7,31},{8,16},{9,... | collective-permute-start | bytes 122888 | tf_op jit(solution)/shard_map/ppermute | solution.py:844
  226.3 11.3 %collective-permute-start.23 = (bf16[1,52,16,128]{3,2,1,0:T(8,128)(2,1)S(1)}, bf16[1,52,16,128]{3,2,1,0:T(8,128)(2,1)S(1)}, u32[]{:S(2)}, u32[]{:S(2)}) collective-permute-start(bf16[1,52,16,128]{3,2,1,0:T(8,128)(2,1)S(1)} %add_convert_fusion.5), channel_id=1, source_target_pairs={{0,16},{1,17},{2,18},{3,19},{4,20},{5,21},{6,22},{7,23},{8,24},{9,... | collective-permute-start | bytes 638984 | tf_op jit(solution)/shard_map/ppermute | solution.py:844
  238.4 8.4 %collective-permute-start.28 = (bf16[52,16,128]{2,1,0:T(8,128)(2,1)S(1)}, bf16[52,16,128]{2,1,0:T(8,128)(2,1)S(1)}, u32[]{:S(2)}, u32[]{:S(2)}) collective-permute-start(bf16[52,16,128]{2,1,0:T(8,128)(2,1)S(1)} %bitcast.37), channel_id=1, source_target_pairs={{0,4},{1,5},{2,6},{3,7},{4,0},{5,1},{6,2},{7,3},{8,12},{9,13},{10,... | collective-permute-start | bytes 638984 | tf_op jit(solution)/shard_map/ppermute | solution.py:844
  248.1 1.3 collective-permute-start.29
  249.4 3.8 %collective-permute-start.30 = (f32[8,640]{1,0:T(8,128)S(1)}, f32[8,640]{1,0:T(8,128)S(1)}, u32[]{:S(2)}, u32[]{:S(2)}) collective-permute-start(f32[8,640]{1,0:T(8,128)S(1)} %add.219), channel_id=1, source_target_pairs={{0,2},{1,3},{2,0},{3,1},{4,6},{5,7},{6,4},{7,5},{8,10},{9,11},{10,... | collective-permute-start | bytes 61448 | tf_op jit(solution)/shard_map/ppermute | solution.py:844
  (20 other events, 89.3 us)
where the time goes:
time: 259 us; the launch traced here: 257 us
  Pallas kernels  165 us (64%)
  starting transfers between devices  43.9 us (17%)
  waiting for transfers between devices  34.8 us (13%)
  other arithmetic  7.39 us (3%)
  local copies, waits for them, and re-layouts  3.76 us (1%)
    pallas_call x1, Pallas kernels, on_device(): call(functools.partial(conv_kernel, pieces, rows_of), (steps + 1,), [SMEM...  54.6 us
    pallas_call x2, Pallas kernels, back_conv(): call(functools.partial(back_conv_kernel, last, w_in.shape[0]), (here,), [...  34.2 us
    ppermute x29, waiting for transfers between devices, flip(): return lax.ppermute(x, AXES, pairs)  33 us
    ppermute x29, starting transfers between devices, flip(): return lax.ppermute(x, AXES, pairs)  32.7 us
    pallas_call x2, Pallas kernels, in_call(): call(functools.partial(in_kernel, pieces, tiles), (count,), [SMEM, whole(...  19.5 us
    pallas_call x1, Pallas kernels, on_device(): call(functools.partial(back_a_kernel, pieces, steps // 2), (steps,), [SME...  17.1 us
    pallas_call x1, Pallas kernels, on_device(): call(norm_a_kernel, (rows // tile_a,), [rows_spec(tile_a, D), params_spec...  16.8 us
    pallas_call x1, Pallas kernels, on_device(): call(functools.partial(out_kernel, pieces), (steps,), [SMEM, rows_spec(ti...  10.1 us
  transfers between devices with their start and end apart: 33, of which 15 were waited for; matrix products, arithmetic and copies ran while one was open for 2% of the time, Pallas kernels for 41%

commit v1 on v0

--- a/solution.py
+++ b/solution.py
@@ -110,8 +110,9 @@
     return total
 
 
-def in_stages(count, stages, between=()):
-    chunks = [slice(k, k + CHUNK) for k in range(0, count, CHUNK)]
+def in_stages(count, stages, between=(), chunk=None):
+    chunk = chunk or CHUNK
+    chunks = [slice(k, k + chunk) for k in range(0, count, chunk)]
     kept, rounds = {}, len(chunks) + len(stages) - 1
     for t in range(rounds):
         for n, stage in enumerate(stages):
@@ -202,7 +203,7 @@
 def norm_a_kernel(tok_ref, np_ref, hid_ref, slope_ref, xhat_ref, rstd_ref):
     def stats(rows, _):
         mean, rstd = row_stats(tok_ref, rows)
-        rstd_ref[rows, :] = jnp.broadcast_to(rstd, (CHUNK, LANE))
+        rstd_ref[rows, :] = jnp.broadcast_to(rstd, (rstd.shape[0], LANE))
         return mean, rstd
 
     def work(rows, kept):
@@ -214,7 +215,7 @@
             slope_ref[rows, b] = slope.astype(BF16)
             xhat_ref[rows, b] = xhat.astype(BF16)
 
-    in_stages(tok_ref.shape[0], [stats, work])
+    in_stages(tok_ref.shape[0], [stats, work], chunk=32)
 
 
 def running_ends(ends_ref, lengths_ref):
@@ -270,7 +271,7 @@
 
     def stats(rows, _):
         mean, rstd = row_stats(pre_ref, rows)
-        rstd_ref[rows, :] = jnp.broadcast_to(rstd, (CHUNK, LANE))
+        rstd_ref[rows, :] = jnp.broadcast_to(rstd, (rstd.shape[0], LANE))
         return mean, rstd
 
     def work(rows, kept):
@@ -284,7 +285,7 @@
             slope_ref[rows, b] = slope.astype(BF16)
             xhat_ref[rows, b] = xhat.astype(BF16)
 
-    in_stages(tile, [stats, work])
+    in_stages(tile, [stats, work], chunk=32)
     if edges:
         put_edges(place_ref, outs[5], outs[6], mov_ref, step == 0, step == 1)
 
@@ -1055,16 +1056,6 @@
     )
     d_inner, d_outer = halo(d_first, d_last)
     first, second = Reduction(place, keep1, send1), Reduction(place, keep2, send2)
-    (block_out,) = call(
-        functools.partial(out_kernel, pieces),
-        (steps,),
-        [SMEM, rows_spec(tile, INNER), rows_spec(tile, D)] + [ANY] * pieces,
-        [rows_spec(tile, D)],
-        [shape((rows, D), BF16)],
-        [pltpu.VMEM((INNER, D), BF16), dma((2 * pieces,))],
-        us=9,
-    )(spots, hidden_c, tokens, *conv_pieces)
-
     def back_conv(last, spots, before):
         here = steps // 2
         at = here * last
@@ -1099,7 +1090,7 @@
             norm_params, *before,
         )
 
-    block_out, d_inner, d_outer = arrive((block_out, d_inner, d_outer), first, second)
+    d_inner, d_outer = arrive((d_inner, d_outer), first, second)
     away = (first.x(), second.y())
     d_pre0, sums_b0, grad_part = back_conv(0, tie(spots, *away), ())
     d_pre0 = arrive(d_pre0, first, second)
@@ -1173,8 +1164,19 @@
     other = place.flip(mine, "seq", 1)
     third.add_half()
     third.send_half(seq_bits[-1])
+    (block_out,) = call(
+        functools.partial(out_kernel, pieces),
+        (steps,),
+        [SMEM, rows_spec(tile, INNER), rows_spec(tile, D)] + [ANY] * pieces,
+        [rows_spec(tile, D)],
+        [shape((rows, D), BF16)],
+        [pltpu.VMEM((INNER, D), BF16), dma((2 * pieces,))],
+        us=1,
+    )(tie(spots, pack), hidden_c, tokens, *conv_pieces)
     pack = sum_along_z(pack, place)
-    third.got, other, pack = lax.optimization_barrier((third.got, other, pack))
+    third.got, other, pack, block_out = lax.optimization_barrier(
+        (third.got, other, pack, block_out)
+    )
     third.add_half()
     line = third.near.reshape(third.near.shape[1:])
     line_other = place.flip(line, "seq", 1)

time: 259 us -> 261 us (level)
  waiting for transfers between devices: 34.8 us -> 27.6 us
  starting transfers between devices: 43.9 us -> 50 us
  other arithmetic: 7.39 us -> 10.3 us
    ppermute x29, waiting for transfers between devices: 33 us -> 25.9 us  [flip(): return lax.ppermute(x, AXES, pairs)]
    ppermute x29, starting transfers between devices: 32.7 us -> 38.5 us  [flip(): return lax.ppermute(x, AXES, pairs)]
  transfers between devices with their start and end apart: 33 -> 33, of which waited for: 15 -> 13; matrix products, arithmetic and copies ran while one was open for 2% -> 2% of each run, Pallas kernels for 41% -> 41%
where the time goes in v1:
time: 261 us; the launch traced here: 258 us
  Pallas kernels  165 us (63%)
  starting transfers between devices  50 us (19%)
  waiting for transfers between devices  27.6 us (11%)
  other arithmetic  10.3 us (4%)
  local copies, waits for them, and re-layouts  3.17 us (1%)
    pallas_call x1, Pallas kernels, on_device(): call(functools.partial(conv_kernel, pieces, rows_of), (steps + 1,), [SMEM...  53.9 us
    ppermute x29, starting transfers between devices, flip(): return lax.ppermute(x, AXES, pairs)  38.5 us
    pallas_call x2, Pallas kernels, back_conv(): call(functools.partial(back_conv_kernel, last, w_in.shape[0]), (here,), [...  34.2 us
    ppermute x29, waiting for transfers between devices, flip(): return lax.ppermute(x, AXES, pairs)  25.9 us
    pallas_call x2, Pallas kernels, in_call(): call(functools.partial(in_kernel, pieces, tiles), (count,), [SMEM, whole(...  19.5 us
    pallas_call x1, Pallas kernels, on_device(): call(functools.partial(back_a_kernel, pieces, steps // 2), (steps,), [SME...  17.1 us
    pallas_call x1, Pallas kernels, on_device(): call(norm_a_kernel, (rows // tile_a,), [rows_spec(tile_a, D), params_spec...  16.6 us
    pallas_call x1, Pallas kernels, on_device(): call(functools.partial(out_kernel, pieces), (steps,), [SMEM, rows_spec(ti...  10.5 us
  transfers between devices with their start and end apart: 33, of which 13 were waited for; matrix products, arithmetic and copies ran while one was open for 2% of the time, Pallas kernels for 41%

profile of v1, /device:TPU:0, one launch (start us, length us, event | category | flops | bytes accessed | tf_op | source)
XLA Modules:
  0.0 257.9 jit_solution(1739671641559377154)
XLA Ops:
  0.7 1.3 convert_element_type.205.refs_0_
  2.0 3.0 %collective-permute-start.1 = (bf16[320,640]{1,0:T(8,128)(2,1)S(1)}, bf16[320,640]{1,0:T(8,128)(2,1)}, u32[]{:S(2)}, u32[]{:S(2)}) collective-permute-start(bf16[320,640]{1,0:T(8,128)(2,1)S(1)} %convert_element_type.205.refs_0_), channel_id=1, source_target_pairs={{0,2},{1,3},{2,0},{3,1},{4,6},{5,7},{6,4},{7,5},{8,10},{9,11},{10,... | collective-permute-start | bytes 1228808 | tf_op jit(solution)/shard_map/ppermute | solution.py:845
  6.0 16.6 %shard_map.278 = (bf16[2048,1280]{1,0:T(8,128)(2,1)}, bf16[2048,1280]{1,0:T(8,128)(2,1)}, bf16[2048,1280]{1,0:T(8,128)(2,1)}, f32[2048,128]{1,0:T(8,128)}) custom-call(bf16[2048,1280]{1,0:T(8,128)(2,1)} %tok_ref.3, f32[2,2560]{1,0:T(2,128)} %np_ref.14), custom_call_target="tpu_custom_call" | custom-call | flops 18699999232 | bytes 57800000 | tf_op jit(solution)/shard_map/pallas_call | solution.py:969
  25.3 9.9 %shard_map.279 = (bf16[2048,640]{1,0:T(8,128)(2,1)}, bf16[2048,640]{1,0:T(8,128)(2,1)}, bf16[2048,640]{1,0:T(8,128)(2,1)}, f32[2048,128]{1,0:T(8,128)}, f32[2048...) custom-call(s32[4]{0:T(128)} %pad_add_fusion.place_ref, s32[129]{0:T(256)} %lengths_ref.3, ...), custom_call_target="tpu_custom_call" | custom-call | flops 3300000000 | bytes 10200000 | tf_op jit(solution)/shard_map/pallas_call | solution.py:991
  35.9 2.9 %collective-permute-start.3 = (bf16[256,640]{1,0:T(8,128)(2,1)}, bf16[256,640]{1,0:T(8,128)(2,1)S(1)}, u32[]{:S(2)}, u32[]{:S(2)}) collective-permute-start(bf16[256,640]{1,0:T(8,128)(2,1)} %get-tuple-element.107), channel_id=1, source_target_pairs={{0,1},{1,0},{2,3},{3,2},{4,5},{5,4},{6,7},{7,6},{8,9},{9,8},{10,11... | collective-permute-start | bytes 983048 | tf_op jit(solution)/shard_map/ppermute | solution.py:845
  38.9 9.6 %shard_map.280 = (bf16[2048,640]{1,0:T(8,128)(2,1)}, bf16[2048,640]{1,0:T(8,128)(2,1)}, bf16[2048,640]{1,0:T(8,128)(2,1)}, f32[2048,128]{1,0:T(8,128)}, f32[2048,128]{1,0:T(8,128)}) custom-call(s32[4]{0:T(128)} %pad_add_fusion.place_ref, s32[129]{0:T(256)} %lengths_ref.3, ...), custom_call_target="tpu_custom_call", output_to_operand_aliasing={{0}: (9, {}), {1}: (10, {}), {2}: (11, {}), {3}: (12, {}), ... | custom-call | flops 3300000000 | bytes 10200000 | tf_op jit(solution)/shard_map/pallas_call | solution.py:991
  49.1 3.0 %collective-permute-start.7 = (bf16[1120,640]{1,0:T(8,128)(2,1)S(1)}, bf16[1120,640]{1,0:T(8,128)(2,1)S(1)}, u32[]{:S(2)}, u32[]{:S(2)}) collective-permute-start(bf16[1120,640]{1,0:T(8,128)(2,1)S(1)} %collective-permute-done.6.refs_2_), channel_id=1, source_target_pairs={{0,1},{1,0},{2,3},{3,2},{4,5},{5,4},{6,7},{7,6},{8,9},{9,8},{10,11... | collective-permute-start | bytes 4300808 | tf_op jit(solution)/shard_map/ppermute | solution.py:845
  52.2 2.8 %collective-permute-done.7.refs_3_ = bf16[1120,640]{1,0:T(8,128)(2,1)S(1)} collective-permute-done((bf16[1120,640]{1,0:T(8,128)(2,1)S(1)}, bf16[1120,640]{1,0:T(8,128)(2,1)S(1)}, u32[]{:S(2)}, u32[]{:S(2)}) %collective-permute-start.7) | collective-permute-done | bytes 1433632 | tf_op jit(solution)/shard_map/ppermute | solution.py:845
  55.0 1.1 copy-done.24
  56.1 53.9 %shard_map.281 = (bf16[2048,640]{1,0:T(8,128)(2,1)}, bf16[2048,640]{1,0:T(8,128)(2,1)}, bf16[256,640]{1,0:T(8,128)(2,1)}, bf16[256,640]{1,0:T(8,128)(2,1)}, f32[...) custom-call(s32[4]{0:T(128)} %pad_add_fusion.place_ref, ...), custom_call_target="tpu_custom_call" | custom-call | flops 49500000256 | bytes 153000000 | tf_op jit(solution)/shard_map/pallas_call | solution.py:1030
  111.8 4.3 %collective-permute-done.8.low_ref = bf16[256,640]{1,0:T(8,128)(2,1)S(1)} collective-permute-done((bf16[256,640]{1,0:T(8,128)(2,1)}, bf16[256,640]{1,0:T(8,128)(2,1)S(1)}, u32[]{:S(2)}, u32[]{:S(2)}) %collective-permute-start.8) | collective-permute-done | bytes 327712 | tf_op jit(solution)/shard_map/ppermute | solution.py:845
  116.2 2.6 %convert_add_fusion.1 = (f32[2,1,76,16,128]{4,3,2,1,0:T(8,128)S(1)}, bf16[2,76,16,128]{3,2,1,0:T(8,128)(2,1)}) fusion(bf16[2,2,76,16,128]{4,3,2,1,0:T(8,128)(2,1)S(1)} %bitcast.46, s32[]{:T(128)S(6)} %select_n.72, bf16[2,2,76,16,128]{4,3,2,1,0:T(8,128)(2,1)} %bitcast.45, s32[]{:T(128)S(6)} %select_n.70), kind=kLoop, calls=%fused_computation.3 | loop fusion | flops 2179072 | bytes 4358152 | tf_op jit(solution)/shard_map/add | solution.py:895
  118.8 8.6 %collective-permute-start.13 = (bf16[2,76,16,128]{3,2,1,0:T(8,128)(2,1)}, bf16[2,76,16,128]{3,2,1,0:T(8,128)(2,1)}, u32[]{:S(2)}, u32[]{:S(2)}) collective-permute-start(bf16[2,76,16,128]{3,2,1,0:T(8,128)(2,1)} %get-tuple-element.192), channel_id=1, source_target_pairs={{0,4},{1,5},{2,6},{3,7},{4,0},{5,1},{6,2},{7,3},{8,12},{9,13},{10,... | collective-permute-start | bytes 1867784 | tf_op jit(solution)/shard_map/ppermute | solution.py:845
  127.8 1.1 collective-permute-start.12
  128.9 16.7 %shard_map.282 = (bf16[1024,640]{1,0:T(8,128)(2,1)}, f32[2,640]{1,0:T(2,128)}, f32[640,1280]{1,0:T(8,128)}) custom-call(s32[4]{0:T(128)} %pad_add_fusion.place_ref, bf16[256,640]{1,0:T(8,128)(2,1)} %copy-done.27, bf16[2048,640]{1,0:T(8,128)(2,1)} %get-tuple-element.128.d_ref, bf16[256,640]{1,0:T(8,128)(2,1)} %copy-done.28, ...), custom_call_target="tpu_custom_call" | custom-call | flops 17600000000 | bytes 54400000 | tf_op jit(solution)/shard_map/pallas_call | solution.py:1067
  145.6 1.3 collective-permute-done.12
  146.9 1.0 fusion.4
  147.9 1.2 collective-permute-start.15
  149.2 1.8 collective-permute-start.14
  151.0 17.5 %shard_map.283 = (bf16[1024,640]{1,0:T(8,128)(2,1)}, f32[2,640]{1,0:T(2,128)}, bf16[2,104,16,128]{3,2,1,0:T(8,128)(2,1)}, bf16[2,104,16,128]{3,2,1,0:T(8,128)(2,1)}) custom-call(s32[4]{0:T(128)} %pad_add_fusion.place_ref, bf16[256,640]{1,0:T(8,128)(2,1)} %copy-done.27, bf16[2048,640]{1,0:T(8,128)(2,1)} %get-tuple-element.128.d_ref, ...), custom_call_target="tpu_custom_call" | custom-call | flops 17600000000 | bytes 54400000 | tf_op jit(solution)/shard_map/pallas_call | solution.py:1067
  168.6 1.1 fusion.3
  169.9 0.9 pad_maximum_fusion.1
  170.8 5.1 %all-to-all-start = ((bf16[4,44,16,128]{3,2,1,0:T(8,128)(2,1)}), bf16[4,44,16,128]{3,2,1,0:T(8,128)(2,1)S(1)}, u32[]{:S(2)}, u32[]{:S(2)}) async-start(bf16[4,44,16,128]{3,2,1,0:T(8,128)(2,1)} %pad_maximum_fusion.1), calls=%async_computation | async-start | bytes 1441792 | tf_op jit(solution)/shard_map/all_to_all | solution.py:944
  175.9 0.9 copy-done.26
  176.8 1.3 convert_add_fusion.2
  178.1 1.4 collective-permute-start.17
  179.6 17.1 %shard_map.284 = (f32[2048,1280]{1,0:T(8,128)}, f32[2,1280]{1,0:T(2,128)}) custom-call(s32[4]{0:T(128)} %pad_add_fusion.place_ref, bf16[1024,640]{1,0:T(8,128)(2,1)} %get-tuple-element.146.dpre0_ref, bf16[1024,640]{1,0:T(8,128)(2,1)} %get-tuple-element.147.dpre1_ref, bf16[2048,1280]{1,0:T(8,128)(2,1)} %get-tuple-element.148.xhat_ref, ...), custom_call_target="tpu_custom_call" | custom-call | flops 18699999232 | bytes 57800000 | tf_op jit(solution)/shard_map/pallas_call | solution.py:1105
  196.9 1.0 broadcast_in_dim.2
  197.9 5.1 %all-to-all-start.1 = ((bf16[4,44,16,128]{3,2,1,0:T(8,128)(2,1)}), bf16[4,44,16,128]{3,2,1,0:T(8,128)(2,1)S(1)}, u32[]{:S(2)}, u32[]{:S(2)}) async-start(bf16[4,44,16,128]{3,2,1,0:T(8,128)(2,1)} %broadcast_in_dim.2), calls=%async_computation.1 | async-start | bytes 1441792 | tf_op jit(solution)/shard_map/all_to_all | solution.py:944
  203.0 1.2 collective-permute-start.18
  204.3 1.0 shard_map.285
  205.4 1.2 collective-permute-done.19
  206.9 3.7 %collective-permute-done.20 = f32[5,16,128]{2,1,0:T(8,128)S(1)} collective-permute-done((f32[5,16,128]{2,1,0:T(8,128)S(1)}, f32[5,16,128]{2,1,0:T(8,128)S(1)}, u32[]{:S(2)}, u32[]{:S(2)}) %collective-permute-start.20) | collective-permute-done | bytes 40992 | tf_op jit(solution)/shard_map/ppermute | solution.py:845
  210.7 2.1 collective-permute-start.21
  213.7 3.1 %collective-permute-done.22 = f32[5,16,128]{2,1,0:T(8,128)S(1)} collective-permute-done((f32[5,16,128]{2,1,0:T(8,128)S(1)}, f32[5,16,128]{2,1,0:T(8,128)S(1)}, u32[]{:S(2)}, u32[]{:S(2)}) %collective-permute-start.22) | collective-permute-done | bytes 40992 | tf_op jit(solution)/shard_map/ppermute | solution.py:845
  216.8 2.9 %collective-permute-done.21 = bf16[1,52,16,128]{3,2,1,0:T(8,128)(2,1)S(1)} collective-permute-done((bf16[1,52,16,128]{3,2,1,0:T(8,128)(2,1)S(1)}, bf16[1,52,16,128]{3,2,1,0:T(8,128)(2,1)S(1)}, u32[]{:S(2)}, u32[]{:S(2)}) %collective-permute-start.21) | collective-permute-done | bytes 213024 | tf_op jit(solution)/shard_map/ppermute | solution.py:845
  219.8 1.7 all-to-all-done.1.mine_ref
  221.5 1.2 collective-permute-start.24
  222.6 2.5 collective-permute-start.27
  225.2 1.9 collective-permute-start.25
  227.1 1.4 collective-permute-start.23
  228.5 10.5 %shard_map.286 = bf16[2048,1280]{1,0:T(8,128)(2,1)} custom-call(s32[4]{0:T(128)} %pad_add_fusion.place_ref, bf16[2048,640]{1,0:T(8,128)(2,1)} %get-tuple-element.166.hid_ref, bf16[2048,1280]{1,0:T(8,128)(2,1)} %tok_ref.3, bf16[1120,640]{1,0:T(8,128)(2,1)} %copy-done.19, bf16[1120,640]{1,0:T(8,128)(2,1)} %copy-done.23, bf16[1120,640]{1,0:T(8,128)(2,1)} %copy-done.22, ...), custom_call_target="tpu_custom_call" | custom-call | flops 1100000000 | bytes 3400000 | tf_op jit(solution)/shard_map/pallas_call | solution.py:1167
  239.1 0.9 collective-permute-start.28
  240.1 8.0 %shard_map.287 = (f32[800,640]{1,0:T(8,128)}, f32[160,1280]{1,0:T(8,128)}, f32[800,640]{1,0:T(8,128)}, f32[160,1280]{1,0:T(8,128)}, f32[800]{0:T(1024)}, /*index=5*/f32[160]{0:T(256)}, f32[640]{0:T(1024)}, f32[1280]{0:T(1024)}) custom-call(s32[4]{0:T(128)S(1)} %copy-done.7, bf16[4,44,16,128]{3,2,1,0:T(8,128)(2,1)S(1)} %all-to-all-done.1.mine_ref, ...), custom_call_target="tpu_custom_call" | custom-call | flops 8800000000 | bytes 27200000 | tf_op jit(solution)/shard_map/pallas_call | solution.py:1195
  248.1 1.3 shard_map.288
  249.5 1.2 collective-permute-done.29
  251.4 3.1 %collective-permute-done.30 = f32[8,640]{1,0:T(8,128)S(1)} collective-permute-done((f32[8,640]{1,0:T(8,128)S(1)}, f32[8,640]{1,0:T(8,128)S(1)}, u32[]{:S(2)}, u32[]{:S(2)}) %collective-permute-start.30) | collective-permute-done | bytes 20512 | tf_op jit(solution)/shard_map/ppermute | solution.py:845
  254.5 3.1 %shard_map.289 = (f32[320,640]{1,0:T(8,128)}, f32[320,640]{1,0:T(8,128)}, f32[320]{0:T(512)}, f32[640]{0:T(1024)}, f32[2,2560]{1,0:T(2,128)}, /*index=5*/f32[2,2560]{1,0:T(2,128)}, f32[2,2560]{1,0:T(2,128)}) custom-call(s32[4]{0:T(128)S(1)} %copy-done.7, bf16[52,16,128]{2,1,0:T(8,128)(2,1)S(1)} %bitcast.39, ...), custom_call_target="tpu_custom_call" | custom-call | flops 4400000000 | bytes 13600000 | tf_op jit(solution)/shard_map/pallas_call | solution.py:1224
  (118 shorter events, 9.9 us)
Async XLA Ops:
  2.0 20.6 %copy-start.21 = (bf16[320,640]{1,0:T(8,128)(2,1)}, bf16[320,640]{1,0:T(8,128)(2,1)S(1)}, u32[]{:S(2)}) copy-start(bf16[320,640]{1,0:T(8,128)(2,1)S(1)} %convert_element_type.205.refs_0_) | copy-start | bytes 1228804
  2.0 20.6 %collective-permute-start.1 = (bf16[320,640]{1,0:T(8,128)(2,1)S(1)}, bf16[320,640]{1,0:T(8,128)(2,1)}, u32[]{:S(2)}, u32[]{:S(2)}) collective-permute-start(bf16[320,640]{1,0:T(8,128)(2,1)S(1)} %convert_element_type.205.refs_0_), channel_id=1, source_target_pairs={{0,2},{1,3},{2,0},{3,1},{4,6},{5,7},{6,4},{7,5},{8,10},{9,11},{10,... | collective-permute-start | bytes 1228808 | tf_op jit(solution)/shard_map/ppermute | solution.py:845
  5.4 33.4 %copy-start.19 = (bf16[1120,640]{1,0:T(8,128)(2,1)}, bf16[1120,640]{1,0:T(8,128)(2,1)S(1)}, u32[]{:S(2)}) copy-start(bf16[1120,640]{1,0:T(8,128)(2,1)S(1)} %pad_maximum_fusion.refs_0_) | copy-start | bytes 4300804
  5.4 43.7 %collective-permute-start.6 = (bf16[1120,640]{1,0:T(8,128)(2,1)S(1)}, bf16[1120,640]{1,0:T(8,128)(2,1)S(1)}, u32[]{:S(2)}, u32[]{:S(2)}) collective-permute-start(bf16[1120,640]{1,0:T(8,128)(2,1)S(1)} %pad_maximum_fusion.refs_0_), channel_id=1, source_target_pairs={{0,2},{1,3},{2,0},{3,1},{4,6},{5,7},{6,4},{7,5},{8,10},{9,11},{10,... | collective-permute-start | bytes 4300808 | tf_op jit(solution)/shard_map/ppermute | solution.py:845
  22.6 1.9 collective-permute-start
  22.7 2.6 %collective-permute-start.2 = (bf16[320,640]{1,0:T(8,128)(2,1)}, bf16[320,640]{1,0:T(8,128)(2,1)}, u32[]{:S(2)}, u32[]{:S(2)}) collective-permute-start(bf16[320,640]{1,0:T(8,128)(2,1)} %collective-permute-done.1.refs_2_), channel_id=1, source_target_pairs={{0,1},{1,0},{2,3},{3,2},{4,5},{5,4},{6,7},{7,6},{8,9},{9,8},{10,11... | collective-permute-start | bytes 1228808 | tf_op jit(solution)/shard_map/ppermute | solution.py:845
  35.2 13.3 %collective-permute-start.4 = (bf16[256,640]{1,0:T(8,128)(2,1)}, bf16[256,640]{1,0:T(8,128)(2,1)S(1)}, u32[]{:S(2)}, u32[]{:S(2)}) collective-permute-start(bf16[256,640]{1,0:T(8,128)(2,1)} %get-tuple-element.114), channel_id=1, source_target_pairs={{1,2},{2,1},{3,4},{4,3},{5,6},{6,5},{7,8},{8,7},{9,10},{10,9},{11,... | collective-permute-start | bytes 983048 | tf_op jit(solution)/shard_map/ppermute | solution.py:1010
  35.9 12.6 %collective-permute-start.3 = (bf16[256,640]{1,0:T(8,128)(2,1)}, bf16[256,640]{1,0:T(8,128)(2,1)S(1)}, u32[]{:S(2)}, u32[]{:S(2)}) collective-permute-start(bf16[256,640]{1,0:T(8,128)(2,1)} %get-tuple-element.107), channel_id=1, source_target_pairs={{0,1},{1,0},{2,3},{3,2},{4,5},{5,4},{6,7},{7,6},{8,9},{9,8},{10,11... | collective-permute-start | bytes 983048 | tf_op jit(solution)/shard_map/ppermute | solution.py:845
  38.8 13.3 %collective-permute-start.5 = (bf16[1120,640]{1,0:T(8,128)(2,1)S(1)}, bf16[1120,640]{1,0:T(8,128)(2,1)S(1)}, u32[]{:S(2)}, u32[]{:S(2)}) collective-permute-start(bf16[1120,640]{1,0:T(8,128)(2,1)S(1)} %pad_maximum_fusion.refs_0_), channel_id=1, source_target_pairs={{0,1},{1,0},{2,3},{3,2},{4,5},{5,4},{6,7},{7,6},{8,9},{9,8},{10,11... | collective-permute-start | bytes 4300808 | tf_op jit(solution)/shard_map/ppermute | solution.py:845
  48.5 7.6 %copy-start.29 = (bf16[256,640]{1,0:T(8,128)(2,1)}, bf16[256,640]{1,0:T(8,128)(2,1)S(1)}, u32[]{:S(2)}) copy-start(bf16[256,640]{1,0:T(8,128)(2,1)S(1)} %collective-permute-done.4.high_ref) | copy-start | bytes 983044
  48.6 7.6 %copy-start.30 = (bf16[256,640]{1,0:T(8,128)(2,1)}, bf16[256,640]{1,0:T(8,128)(2,1)S(1)}, u32[]{:S(2)}) copy-start(bf16[256,640]{1,0:T(8,128)(2,1)S(1)} %collective-permute-done.3.low_ref) | copy-start | bytes 983044
  49.1 5.9 %collective-permute-start.7 = (bf16[1120,640]{1,0:T(8,128)(2,1)S(1)}, bf16[1120,640]{1,0:T(8,128)(2,1)S(1)}, u32[]{:S(2)}, u32[]{:S(2)}) collective-permute-start(bf16[1120,640]{1,0:T(8,128)(2,1)S(1)} %collective-permute-done.6.refs_2_), channel_id=1, source_target_pairs={{0,1},{1,0},{2,3},{3,2},{4,5},{5,4},{6,7},{7,6},{8,9},{9,8},{10,11... | collective-permute-start | bytes 4300808 | tf_op jit(solution)/shard_map/ppermute | solution.py:845
  110.1 6.0 %collective-permute-start.10 = (bf16[2,200,16,128]{3,2,1,0:T(8,128)(2,1)}, bf16[2,200,16,128]{3,2,1,0:T(8,128)(2,1)S(1)}, u32[]{:S(2)}, u32[]{:S(2)}) collective-permute-start(bf16[2,200,16,128]{3,2,1,0:T(8,128)(2,1)} %get-tuple-element.121), channel_id=1, source_target_pairs={{0,1},{1,0},{2,3},{3,2},{4,5},{5,4},{6,7},{7,6},{8,9},{9,8},{10,11... | collective-permute-start | bytes 4915208 | tf_op jit(solution)/shard_map/ppermute | solution.py:845
  110.5 5.6 %collective-permute-start.11 = (bf16[2,152,16,128]{3,2,1,0:T(8,128)(2,1)}, bf16[2,152,16,128]{3,2,1,0:T(8,128)(2,1)S(1)}, u32[]{:S(2)}, u32[]{:S(2)}) collective-permute-start(bf16[2,152,16,128]{3,2,1,0:T(8,128)(2,1)} %get-tuple-element.122), channel_id=1, source_target_pairs={{0,1},{1,0},{2,3},{3,2},{4,5},{5,4},{6,7},{7,6},{8,9},{9,8},{10,11... | collective-permute-start | bytes 3735560 | tf_op jit(solution)/shard_map/ppermute | solution.py:845
  110.7 5.5 %collective-permute-start.8 = (bf16[256,640]{1,0:T(8,128)(2,1)}, bf16[256,640]{1,0:T(8,128)(2,1)S(1)}, u32[]{:S(2)}, u32[]{:S(2)}) collective-permute-start(bf16[256,640]{1,0:T(8,128)(2,1)} %get-tuple-element.119), channel_id=1, source_target_pairs={{0,1},{1,0},{2,3},{3,2},{4,5},{5,4},{6,7},{7,6},{8,9},{9,8},{10,11... | collective-permute-start | bytes 983048 | tf_op jit(solution)/shard_map/ppermute | solution.py:845
  111.1 5.1 %collective-permute-start.9 = (bf16[256,640]{1,0:T(8,128)(2,1)}, bf16[256,640]{1,0:T(8,128)(2,1)S(1)}, u32[]{:S(2)}, u32[]{:S(2)}) collective-permute-start(bf16[256,640]{1,0:T(8,128)(2,1)} %get-tuple-element.120), channel_id=1, source_target_pairs={{1,2},{2,1},{3,4},{4,3},{5,6},{6,5},{7,8},{8,7},{9,10},{10,9},{11,... | collective-permute-start | bytes 983048 | tf_op jit(solution)/shard_map/ppermute | solution.py:1010
  116.2 11.2 %copy-start.20 = (bf16[2,200,16,128]{3,2,1,0:T(8,128)(2,1)S(1)}, bf16[2,200,16,128]{3,2,1,0:T(8,128)(2,1)}, u32[]{:S(2)}) copy-start(bf16[2,200,16,128]{3,2,1,0:T(8,128)(2,1)} %get-tuple-element.118) | copy-start | bytes 4915204
  118.8 26.8 %collective-permute-start.13 = (bf16[2,76,16,128]{3,2,1,0:T(8,128)(2,1)}, bf16[2,76,16,128]{3,2,1,0:T(8,128)(2,1)}, u32[]{:S(2)}, u32[]{:S(2)}) collective-permute-start(bf16[2,76,16,128]{3,2,1,0:T(8,128)(2,1)} %get-tuple-element.192), channel_id=1, source_target_pairs={{0,4},{1,5},{2,6},{3,7},{4,0},{5,1},{6,2},{7,3},{8,12},{9,13},{10,... | collective-permute-start | bytes 1867784 | tf_op jit(solution)/shard_map/ppermute | solution.py:845
  127.8 19.1 %collective-permute-start.12 = (bf16[1,200,16,128]{3,2,1,0:T(8,128)(2,1)S(1)}, bf16[1,200,16,128]{3,2,1,0:T(8,128)(2,1)S(1)}, u32[]{:S(2)}, u32[]{:S(2)}) collective-permute-start(bf16[1,200,16,128]{3,2,1,0:T(8,128)(2,1)S(1)} %get-tuple-element.189), channel_id=1, source_target_pairs={{0,2},{1,3},{2,0},{3,1},{4,6},{5,7},{6,4},{7,5},{8,10},{9,11},{10,... | collective-permute-start | bytes 2457608 | tf_op jit(solution)/shard_map/ppermute | solution.py:845
  147.9 20.6 %collective-permute-start.15 = (bf16[1,76,16,128]{3,2,1,0:T(8,128)(2,1)S(1)}, bf16[1,76,16,128]{3,2,1,0:T(8,128)(2,1)S(1)}, u32[]{:S(2)}, u32[]{:S(2)}) collective-permute-start(bf16[1,76,16,128]{3,2,1,0:T(8,128)(2,1)S(1)} %fusion.4), channel_id=1, source_target_pairs={{0,2},{1,3},{2,0},{3,1},{4,6},{5,7},{6,4},{7,5},{8,10},{9,11},{10,... | collective-permute-start | bytes 933896 | tf_op jit(solution)/shard_map/ppermute | solution.py:845
  149.2 19.3 %collective-permute-start.14 = (bf16[1,100,16,128]{3,2,1,0:T(8,128)(2,1)S(1)}, bf16[1,100,16,128]{3,2,1,0:T(8,128)(2,1)S(1)}, u32[]{:S(2)}, u32[]{:S(2)}) collective-permute-start(bf16[1,100,16,128]{3,2,1,0:T(8,128)(2,1)S(1)} %fusion.6), channel_id=1, source_target_pairs={{0,4},{1,5},{2,6},{3,7},{4,0},{5,1},{6,2},{7,3},{8,12},{9,13},{10,... | collective-permute-start | bytes 1228808 | tf_op jit(solution)/shard_map/ppermute | solution.py:845
  168.6 7.3 %collective-permute-start.16 = (bf16[2,104,16,128]{3,2,1,0:T(8,128)(2,1)}, bf16[2,104,16,128]{3,2,1,0:T(8,128)(2,1)S(1)}, u32[]{:S(2)}, u32[]{:S(2)}) collective-permute-start(bf16[2,104,16,128]{3,2,1,0:T(8,128)(2,1)} %get-tuple-element.141), channel_id=1, source_target_pairs={{0,1},{1,0},{2,3},{3,2},{4,5},{5,4},{6,7},{7,6},{8,9},{9,8},{10,11... | collective-permute-start | bytes 2555912 | tf_op jit(solution)/shard_map/ppermute | solution.py:845
  170.8 25.8 %all-to-all-start = ((bf16[4,44,16,128]{3,2,1,0:T(8,128)(2,1)}), bf16[4,44,16,128]{3,2,1,0:T(8,128)(2,1)S(1)}, u32[]{:S(2)}, u32[]{:S(2)}) async-start(bf16[4,44,16,128]{3,2,1,0:T(8,128)(2,1)} %pad_maximum_fusion.1), calls=%async_computation | async-start | bytes 1441792 | tf_op jit(solution)/shard_map/all_to_all | solution.py:944
  178.1 18.5 %collective-permute-start.17 = (bf16[1,104,16,128]{3,2,1,0:T(8,128)(2,1)S(1)}, bf16[1,104,16,128]{3,2,1,0:T(8,128)(2,1)S(1)}, u32[]{:S(2)}, u32[]{:S(2)}) collective-permute-start(bf16[1,104,16,128]{3,2,1,0:T(8,128)(2,1)S(1)} %get-tuple-element.194), channel_id=1, source_target_pairs={{0,2},{1,3},{2,0},{3,1},{4,6},{5,7},{6,4},{7,5},{8,10},{9,11},{10,... | collective-permute-start | bytes 1277960 | tf_op jit(solution)/shard_map/ppermute | solution.py:845
  196.8 7.4 %copy-start.6 = (s32[4]{0:T(128)S(1)}, s32[4]{0:T(128)}, u32[]{:S(2)}) copy-start(s32[4]{0:T(128)} %pad_add_fusion.place_ref) | copy-start | bytes 52
  196.8 7.4 %copy-start.10 = (f32[800]{0:T(1024)S(1)}, f32[800]{0:T(1024)}, u32[]{:S(2)}) copy-start(f32[800]{0:T(1024)} %refs_2_.4) | copy-start | bytes 9604
  196.8 7.4 %copy-start.13 = (f32[320]{0:T(512)S(1)}, f32[320]{0:T(512)}, u32[]{:S(2)}) copy-start(f32[320]{0:T(512)} %refs_1_.5) | copy-start | bytes 3844
  196.8 7.4 %copy-start.14 = (f32[160]{0:T(256)S(1)}, f32[160]{0:T(256)}, u32[]{:S(2)}) copy-start(f32[160]{0:T(256)} %refs_3_.1) | copy-start | bytes 1924
  196.9 7.4 %copy-start.15 = (f32[2,1280]{1,0:T(2,128)S(1)}, f32[2,1280]{1,0:T(2,128)}, u32[]{:S(2)}) copy-start(f32[2,1280]{1,0:T(2,128)} %get-tuple-element.156.refs_3_) | copy-start | bytes 30724
  197.9 23.6 %all-to-all-start.1 = ((bf16[4,44,16,128]{3,2,1,0:T(8,128)(2,1)}), bf16[4,44,16,128]{3,2,1,0:T(8,128)(2,1)S(1)}, u32[]{:S(2)}, u32[]{:S(2)}) async-start(bf16[4,44,16,128]{3,2,1,0:T(8,128)(2,1)} %broadcast_in_dim.2), calls=%async_computation.1 | async-start | bytes 1441792 | tf_op jit(solution)/shard_map/all_to_all | solution.py:944
  203.0 7.6 %collective-permute-start.18 = (bf16[1,52,16,128]{3,2,1,0:T(8,128)(2,1)S(1)}, bf16[1,52,16,128]{3,2,1,0:T(8,128)(2,1)S(1)}, u32[]{:S(2)}, u32[]{:S(2)}) collective-permute-start(bf16[1,52,16,128]{3,2,1,0:T(8,128)(2,1)S(1)} %fusion.7), channel_id=1, source_target_pairs={{0,4},{1,5},{2,6},{3,7},{4,0},{5,1},{6,2},{7,3},{8,12},{9,13},{10,... | collective-permute-start | bytes 638984 | tf_op jit(solution)/shard_map/ppermute | solution.py:845
  205.3 1.3 collective-permute-start.19
  206.6 4.0 %collective-permute-start.20 = (f32[5,16,128]{2,1,0:T(8,128)S(1)}, f32[5,16,128]{2,1,0:T(8,128)S(1)}, u32[]{:S(2)}, u32[]{:S(2)}) collective-permute-start(f32[5,16,128]{2,1,0:T(8,128)S(1)} %add.210), channel_id=1, source_target_pairs={{0,2},{1,3},{2,0},{3,1},{4,6},{5,7},{6,4},{7,5},{8,10},{9,11},{10,... | collective-permute-start | bytes 122888 | tf_op jit(solution)/shard_map/ppermute | solution.py:845
  210.7 9.0 %collective-permute-start.21 = (bf16[1,52,16,128]{3,2,1,0:T(8,128)(2,1)S(1)}, bf16[1,52,16,128]{3,2,1,0:T(8,128)(2,1)S(1)}, u32[]{:S(2)}, u32[]{:S(2)}) collective-permute-start(bf16[1,52,16,128]{3,2,1,0:T(8,128)(2,1)S(1)} %fusion.5), channel_id=1, source_target_pairs={{0,8},{1,9},{2,10},{3,11},{4,12},{5,13},{6,14},{7,15},{8,0},{9,1},... | collective-permute-start | bytes 638984 | tf_op jit(solution)/shard_map/ppermute | solution.py:845
  212.8 4.0 %collective-permute-start.22 = (f32[5,16,128]{2,1,0:T(8,128)S(1)}, f32[5,16,128]{2,1,0:T(8,128)S(1)}, u32[]{:S(2)}, u32[]{:S(2)}) collective-permute-start(f32[5,16,128]{2,1,0:T(8,128)S(1)} %add.211), channel_id=1, source_target_pairs={{0,4},{1,5},{2,6},{3,7},{4,0},{5,1},{6,2},{7,3},{8,12},{9,13},{10,... | collective-permute-start | bytes 122888 | tf_op jit(solution)/shard_map/ppermute | solution.py:845
  221.5 17.6 %collective-permute-start.24 = (bf16[4,44,16,128]{3,2,1,0:T(8,128)(2,1)S(1)}, bf16[4,44,16,128]{3,2,1,0:T(8,128)(2,1)S(1)}, u32[]{:S(2)}, u32[]{:S(2)}) collective-permute-start(bf16[4,44,16,128]{3,2,1,0:T(8,128)(2,1)S(1)} %all-to-all-done.1.mine_ref), channel_id=1, source_target_pairs={{0,4},{1,5},{2,6},{3,7},{4,0},{5,1},{6,2},{7,3},{8,12},{9,13},{10,... | collective-permute-start | bytes 2162696 | tf_op jit(solution)/shard_map/ppermute | solution.py:845
  222.6 16.4 %collective-permute-start.27 = (f32[5,16,128]{2,1,0:T(8,128)S(1)}, f32[5,16,128]{2,1,0:T(8,128)S(1)}, u32[]{:S(2)}, u32[]{:S(2)}) collective-permute-start(f32[5,16,128]{2,1,0:T(8,128)S(1)} %add.213), channel_id=1, source_target_pairs={{0,24},{1,25},{2,26},{3,27},{4,28},{5,29},{6,30},{7,31},{8,16},{9,... | collective-permute-start | bytes 122888 | tf_op jit(solution)/shard_map/ppermute | solution.py:845
  225.2 13.8 %collective-permute-start.26 = (f32[5,16,128]{2,1,0:T(8,128)S(1)}, f32[5,16,128]{2,1,0:T(8,128)S(1)}, u32[]{:S(2)}, u32[]{:S(2)}) collective-permute-start(f32[5,16,128]{2,1,0:T(8,128)S(1)} %add.213), channel_id=1, source_target_pairs={{0,16},{1,17},{2,18},{3,19},{4,20},{5,21},{6,22},{7,23},{8,24},{9,... | collective-permute-start | bytes 122888 | tf_op jit(solution)/shard_map/ppermute | solution.py:845
  225.2 13.9 %collective-permute-start.25 = (f32[5,16,128]{2,1,0:T(8,128)S(1)}, f32[5,16,128]{2,1,0:T(8,128)S(1)}, u32[]{:S(2)}, u32[]{:S(2)}) collective-permute-start(f32[5,16,128]{2,1,0:T(8,128)S(1)} %add.213), channel_id=1, source_target_pairs={{0,8},{1,9},{2,10},{3,11},{4,12},{5,13},{6,14},{7,15},{8,0},{9,1},... | collective-permute-start | bytes 122888 | tf_op jit(solution)/shard_map/ppermute | solution.py:845
  227.1 12.0 %collective-permute-start.23 = (bf16[1,52,16,128]{3,2,1,0:T(8,128)(2,1)S(1)}, bf16[1,52,16,128]{3,2,1,0:T(8,128)(2,1)S(1)}, u32[]{:S(2)}, u32[]{:S(2)}) collective-permute-start(bf16[1,52,16,128]{3,2,1,0:T(8,128)(2,1)S(1)} %add_convert_fusion.5), channel_id=1, source_target_pairs={{0,16},{1,17},{2,18},{3,19},{4,20},{5,21},{6,22},{7,23},{8,24},{9,... | collective-permute-start | bytes 638984 | tf_op jit(solution)/shard_map/ppermute | solution.py:845
  228.5 11.6 %copy-start.1 = (f32[800,640]{1,0:T(8,128)S(1)}, f32[800,640]{1,0:T(8,128)}, u32[]{:S(2)}) copy-start(f32[800,640]{1,0:T(8,128)} %refs_0_.4) | copy-start | bytes 6144004
  228.5 11.6 %copy-start.3 = (f32[160,1280]{1,0:T(8,128)S(1)}, f32[160,1280]{1,0:T(8,128)}, u32[]{:S(2)}) copy-start(f32[160,1280]{1,0:T(8,128)} %refs_1_.4) | copy-start | bytes 2457604
  228.5 11.6 %copy-start.7 = (s32[4]{0:T(128)S(1)}, s32[4]{0:T(128)}, u32[]{:S(2)}) copy-start(s32[4]{0:T(128)} %pad_add_fusion.place_ref) | copy-start | bytes 52
  228.5 11.6 %copy-start.9 = (f32[1280]{0:T(1024)S(1)}, f32[1280]{0:T(1024)}, u32[]{:S(2)}) copy-start(f32[1280]{0:T(1024)} %refs_5_.1) | copy-start | bytes 15364
  228.5 11.6 %copy-start.11 = (f32[640]{0:T(1024)S(1)}, f32[640]{0:T(1024)}, u32[]{:S(2)}) copy-start(f32[640]{0:T(1024)} %refs_4_.1) | copy-start | bytes 7684
  239.1 8.9 %collective-permute-start.28 = (bf16[52,16,128]{2,1,0:T(8,128)(2,1)S(1)}, bf16[52,16,128]{2,1,0:T(8,128)(2,1)S(1)}, u32[]{:S(2)}, u32[]{:S(2)}) collective-permute-start(bf16[52,16,128]{2,1,0:T(8,128)(2,1)S(1)} %bitcast.37), channel_id=1, source_target_pairs={{0,4},{1,5},{2,6},{3,7},{4,0},{5,1},{6,2},{7,3},{8,12},{9,13},{10,... | collective-permute-start | bytes 638984 | tf_op jit(solution)/shard_map/ppermute | solution.py:845
  249.5 1.3 collective-permute-start.29
  250.7 3.8 %collective-permute-start.30 = (f32[8,640]{1,0:T(8,128)S(1)}, f32[8,640]{1,0:T(8,128)S(1)}, u32[]{:S(2)}, u32[]{:S(2)}) collective-permute-start(f32[8,640]{1,0:T(8,128)S(1)} %add.219), channel_id=1, source_target_pairs={{0,2},{1,3},{2,0},{3,1},{4,6},{5,7},{6,4},{7,5},{8,10},{9,11},{10,... | collective-permute-start | bytes 61448 | tf_op jit(solution)/shard_map/ppermute | solution.py:845
  (16 other events, 81.9 us)

commit v2 on v0

--- a/solution.py
+++ b/solution.py
@@ -436,11 +436,14 @@
         _, rows_conv, rows_out = rows_of
         stage_turned(stage1_ref, core, gc_ref, rows_conv, 0, slice(0, CUT // LANE))
         first_tiles = rows_conv // SUB * (CUT // LANE)
-        stage_plain(stage1_ref, core, go_ref, rows_out, first_tiles)
+        stage_plain(stage1_ref, core, go_ref, rows_out, first_tiles, slice(0, OUT_CUT // LANE))
         copies = stage_copies(stage1_ref, outs[0], outs[1], spans(CHUNKS[0], rows_of)[1], sem, 0)
         for each in copies:
             each.start()
         stage_turned(stage2_ref, core, gc_ref, rows_conv, 0, slice(CUT // LANE, INNER // LANE))
+        second_tiles = rows_conv // SUB * ((INNER - CUT) // LANE)
+        rest = slice(OUT_CUT // LANE, D // LANE)
+        stage_plain(stage2_ref, core, go_ref, rows_out, second_tiles, rest)
         more = stage_copies(stage2_ref, outs[2], outs[3], spans(CHUNKS[1], rows_of)[1], sem, 2)
         for each in more:
             each.start()
@@ -461,11 +464,11 @@
             stage_ref[side, owner // 2, at] = tile.astype(BF16)
 
 
-def stage_plain(stage_ref, core, grad_ref, rows_each, base):
-    blocks = grad_ref.shape[1] // LANE
+def stage_plain(stage_ref, core, grad_ref, rows_each, base, blocks):
+    lanes = slice(blocks.start * LANE, blocks.stop * LANE)
     for row in range(0, grad_ref.shape[0], SUB):
-        part = grad_ref[row : row + SUB, :]
-        stage_tiles(stage_ref, core, row, rows_each, base, 0, blocks, part)
+        part = grad_ref[row : row + SUB, lanes]
+        stage_tiles(stage_ref, core, row, rows_each, base, 0, blocks.stop - blocks.start, part)
 
 
 def stage_turned(stage_ref, core, turned_ref, rows_each, base, blocks):
@@ -603,7 +606,12 @@
 WIDTHS = (INNER, INNER, D)
 LANE0 = (0, INNER, 2 * INNER)
 CUT = 2 * LANE
-CHUNKS = (((1, 0, CUT), (2, 0, D)), ((1, CUT, INNER - CUT),), ((0, 0, INNER),))
+OUT_CUT = 8 * LANE
+CHUNKS = (
+    ((1, 0, CUT), (2, 0, OUT_CUT)),
+    ((1, CUT, INNER - CUT), (2, OUT_CUT, D - OUT_CUT)),
+    ((0, 0, INNER),),
+)
 
 
 def spans(chunk, rows):
@@ -802,7 +810,7 @@
 
     @pl.when(step == steps - 1)
     def _():
-        update(1, 2, [from1[2]], out_scratch)
+        update(1, 2, [from1[2], from2[2]], out_scratch)
 
 
 def update_in_kernel(
@@ -870,8 +878,8 @@
     return x
 
 
-def sum_along_z(x, place):
-    terms = [x] + [place.flip(x, "seq", 2 * k) for k in range(1, place.seq // 2)]
+def sum_at_once(x, place, axis, bits):
+    terms = [x] + [place.flip(x, axis, bits * k) for k in range(1, getattr(place, axis) // bits)]
     while len(terms) > 1:
         terms = [a + b for a, b in zip(terms[::2], terms[1::2])]
     return terms[0]
@@ -1173,7 +1181,7 @@
     other = place.flip(mine, "seq", 1)
     third.add_half()
     third.send_half(seq_bits[-1])
-    pack = sum_along_z(pack, place)
+    pack = sum_at_once(pack, place, "seq", 2)
     third.got, other, pack = lax.optimization_barrier((third.got, other, pack))
     third.add_half()
     line = third.near.reshape(third.near.shape[1:])
@@ -1218,7 +1226,7 @@
         us=2,
         mib=16,
     )(spots, line, line_other)
-    pack_in = sum_over(pack_in, place, "fsdp")
+    pack_in = sum_at_once(pack_in, place, "fsdp", 1)
     grad_in, new_in, row_in_new, col_in_new, *norm_results = call(
         functools.partial(update_in_kernel, rows_of, place.seq),
         (1,),

time: 259 us -> 258 us (level)
  waiting for transfers between devices: 34.8 us -> 31.9 us
    ppermute x29 -> x30, waiting for transfers between devices: 33 us -> 29.7 us  [flip(): return lax.ppermute(x, AXES, pairs)]
    ppermute x29 -> x30, starting transfers between devices: 32.7 us -> 34 us  [flip(): return lax.ppermute(x, AXES, pairs)]
  transfers between devices with their start and end apart: 33 -> 34, of which waited for: 15 -> 16; matrix products, arithmetic and copies ran while one was open for 2% -> 2% of each run, Pallas kernels for 41% -> 42%
where the time goes in v2:
time: 258 us; the launch traced here: 255 us
  Pallas kernels  165 us (64%)
  starting transfers between devices  45.1 us (17%)
  waiting for transfers between devices  31.9 us (12%)
  other arithmetic  7.49 us (3%)
  local copies, waits for them, and re-layouts  3.82 us (1%)
    pallas_call x1, Pallas kernels, on_device(): call(functools.partial(conv_kernel, pieces, rows_of), (steps + 1,), [SMEM...  54.7 us
    pallas_call x2, Pallas kernels, back_conv(): call(functools.partial(back_conv_kernel, last, w_in.shape[0]), (here,), [...  34.2 us
    ppermute x30, starting transfers between devices, flip(): return lax.ppermute(x, AXES, pairs)  34 us
    ppermute x30, waiting for transfers between devices, flip(): return lax.ppermute(x, AXES, pairs)  29.7 us
    pallas_call x2, Pallas kernels, in_call(): call(functools.partial(in_kernel, pieces, tiles), (count,), [SMEM, whole(...  19.5 us
    pallas_call x1, Pallas kernels, on_device(): call(functools.partial(back_a_kernel, pieces, steps // 2), (steps,), [SME...  17.1 us
    pallas_call x1, Pallas kernels, on_device(): call(norm_a_kernel, (rows // tile_a,), [rows_spec(tile_a, D), params_spec...  16.8 us
    pallas_call x1, Pallas kernels, on_device(): call(functools.partial(out_kernel, pieces), (steps,), [SMEM, rows_spec(ti...  10.1 us
  transfers between devices with their start and end apart: 34, of which 16 were waited for; matrix products, arithmetic and copies ran while one was open for 2% of the time, Pallas kernels for 42%

profile of v2, /device:TPU:0, one launch (start us, length us, event | category | flops | bytes accessed | tf_op | source)
XLA Modules:
  0.0 255.2 jit_solution(8993918592471078597)
XLA Ops:
  0.7 1.3 convert_element_type.205.refs_0_
  2.0 3.0 %collective-permute-start.1 = (bf16[320,640]{1,0:T(8,128)(2,1)S(1)}, bf16[320,640]{1,0:T(8,128)(2,1)S(1)}, u32[]{:S(2)}, u32[]{:S(2)}) collective-permute-start(bf16[320,640]{1,0:T(8,128)(2,1)S(1)} %convert_element_type.205.refs_0_), channel_id=1, source_target_pairs={{0,2},{1,3},{2,0},{3,1},{4,6},{5,7},{6,4},{7,5},{8,10},{9,11},{10,... | collective-permute-start | bytes 1228808 | tf_op jit(solution)/shard_map/ppermute | solution.py:852
  6.0 16.8 %shard_map.278 = (bf16[2048,1280]{1,0:T(8,128)(2,1)}, bf16[2048,1280]{1,0:T(8,128)(2,1)}, bf16[2048,1280]{1,0:T(8,128)(2,1)}, f32[2048,128]{1,0:T(8,128)}) custom-call(bf16[2048,1280]{1,0:T(8,128)(2,1)} %tok_ref.3, f32[2,2560]{1,0:T(2,128)} %np_ref.14), custom_call_target="tpu_custom_call" | custom-call | flops 18699999232 | bytes 57800000 | tf_op jit(solution)/shard_map/pallas_call | solution.py:976
  25.9 9.9 %shard_map.279 = (bf16[2048,640]{1,0:T(8,128)(2,1)}, bf16[2048,640]{1,0:T(8,128)(2,1)}, bf16[2048,640]{1,0:T(8,128)(2,1)}, f32[2048,128]{1,0:T(8,128)}, f32[2048...) custom-call(s32[4]{0:T(128)} %pad_add_fusion.place_ref, s32[129]{0:T(256)} %lengths_ref.3, ...), custom_call_target="tpu_custom_call" | custom-call | flops 3300000000 | bytes 10200000 | tf_op jit(solution)/shard_map/pallas_call | solution.py:998
  36.7 2.9 %collective-permute-start.5 = (bf16[1120,640]{1,0:T(8,128)(2,1)S(1)}, bf16[1120,640]{1,0:T(8,128)(2,1)S(1)}, u32[]{:S(2)}, u32[]{:S(2)}) collective-permute-start(bf16[1120,640]{1,0:T(8,128)(2,1)S(1)} %pad_maximum_fusion.refs_0_), channel_id=1, source_target_pairs={{0,1},{1,0},{2,3},{3,2},{4,5},{5,4},{6,7},{7,6},{8,9},{9,8},{10,11... | collective-permute-start | bytes 4300808 | tf_op jit(solution)/shard_map/ppermute | solution.py:852
  39.6 9.6 %shard_map.280 = (bf16[2048,640]{1,0:T(8,128)(2,1)}, bf16[2048,640]{1,0:T(8,128)(2,1)}, bf16[2048,640]{1,0:T(8,128)(2,1)}, f32[2048,128]{1,0:T(8,128)}, f32[2048,128]{1,0:T(8,128)}) custom-call(s32[4]{0:T(128)} %pad_add_fusion.place_ref, s32[129]{0:T(256)} %lengths_ref.3, ...), custom_call_target="tpu_custom_call", output_to_operand_aliasing={{0}: (9, {}), {1}: (10, {}), {2}: (11, {}), {3}: (12, {}), ... | custom-call | flops 3300000000 | bytes 10200000 | tf_op jit(solution)/shard_map/pallas_call | solution.py:998
  49.3 2.8 %collective-permute-start.7 = (bf16[1120,640]{1,0:T(8,128)(2,1)}, bf16[1120,640]{1,0:T(8,128)(2,1)S(1)}, u32[]{:S(2)}, u32[]{:S(2)}) collective-permute-start(bf16[1120,640]{1,0:T(8,128)(2,1)} %collective-permute-done.6.refs_2_), channel_id=1, source_target_pairs={{0,1},{1,0},{2,3},{3,2},{4,5},{5,4},{6,7},{7,6},{8,9},{9,8},{10,11... | collective-permute-start | bytes 4300808 | tf_op jit(solution)/shard_map/ppermute | solution.py:852
  52.1 3.0 %collective-permute-done.7.refs_3_ = bf16[1120,640]{1,0:T(8,128)(2,1)S(1)} collective-permute-done((bf16[1120,640]{1,0:T(8,128)(2,1)}, bf16[1120,640]{1,0:T(8,128)(2,1)S(1)}, u32[]{:S(2)}, u32[]{:S(2)}) %collective-permute-start.7) | collective-permute-done | bytes 1433632 | tf_op jit(solution)/shard_map/ppermute | solution.py:852
  55.1 1.1 copy-done.30
  56.2 54.7 %shard_map.281 = (bf16[2048,640]{1,0:T(8,128)(2,1)}, bf16[2048,640]{1,0:T(8,128)(2,1)}, bf16[256,640]{1,0:T(8,128)(2,1)}, bf16[256,640]{1,0:T(8,128)(2,1)}, f32[...) custom-call(s32[4]{0:T(128)} %pad_add_fusion.place_ref, ...), custom_call_target="tpu_custom_call" | custom-call | flops 49500000256 | bytes 153000000 | tf_op jit(solution)/shard_map/pallas_call | solution.py:1037
  112.6 10.1 %shard_map.282 = bf16[2048,1280]{1,0:T(8,128)(2,1)} custom-call(s32[4]{0:T(128)} %pad_add_fusion.place_ref, bf16[2048,640]{1,0:T(8,128)(2,1)} %get-tuple-element.117.hid_ref, bf16[2048,1280]{1,0:T(8,128)(2,1)} %tok_ref.3, bf16[1120,640]{1,0:T(8,128)(2,1)} %copy-done.23, bf16[1120,640]{1,0:T(8,128)(2,1)} %copy-done.29, ...), custom_call_target="tpu_custom_call" | custom-call | flops 9900000256 | bytes 30600000 | tf_op jit(solution)/shard_map/pallas_call | solution.py:1066
  123.6 1.2 convert_add_fusion.1
  124.8 5.1 %collective-permute-start.13 = (bf16[2,88,16,128]{3,2,1,0:T(8,128)(2,1)}, bf16[2,88,16,128]{3,2,1,0:T(8,128)(2,1)S(1)}, u32[]{:S(2)}, u32[]{:S(2)}) collective-permute-start(bf16[2,88,16,128]{3,2,1,0:T(8,128)(2,1)} %get-tuple-element.190), channel_id=1, source_target_pairs={{0,4},{1,5},{2,6},{3,7},{4,0},{5,1},{6,2},{7,3},{8,12},{9,13},{10,... | collective-permute-start | bytes 2162696 | tf_op jit(solution)/shard_map/ppermute | solution.py:852
  130.3 16.8 %shard_map.283 = (bf16[1024,640]{1,0:T(8,128)(2,1)}, f32[2,640]{1,0:T(2,128)}, f32[640,1280]{1,0:T(8,128)}) custom-call(s32[4]{0:T(128)} %pad_add_fusion.place_ref, bf16[256,640]{1,0:T(8,128)(2,1)} %copy-done.31, bf16[2048,640]{1,0:T(8,128)(2,1)} %get-tuple-element.129.d_ref, bf16[256,640]{1,0:T(8,128)(2,1)} %copy-done.32, ...), custom_call_target="tpu_custom_call" | custom-call | flops 17600000000 | bytes 54400000 | tf_op jit(solution)/shard_map/pallas_call | solution.py:1084
  147.1 1.3 collective-permute-done.12
  148.5 1.4 collective-permute-start.15
  150.0 0.8 collective-permute-start.14
  150.8 17.5 %shard_map.284 = (bf16[1024,640]{1,0:T(8,128)(2,1)}, f32[2,640]{1,0:T(2,128)}, bf16[2,104,16,128]{3,2,1,0:T(8,128)(2,1)}, bf16[2,104,16,128]{3,2,1,0:T(8,128)(2,1)}) custom-call(s32[4]{0:T(128)} %pad_add_fusion.place_ref, bf16[256,640]{1,0:T(8,128)(2,1)} %copy-done.31, bf16[2048,640]{1,0:T(8,128)(2,1)} %get-tuple-element.129.d_ref, ...), custom_call_target="tpu_custom_call" | custom-call | flops 17600000000 | bytes 54400000 | tf_op jit(solution)/shard_map/pallas_call | solution.py:1084
  168.4 1.1 fusion.3
  169.6 0.9 pad_maximum_fusion.1
  170.6 4.8 %all-to-all-start = ((bf16[4,45,16,128]{3,2,1,0:T(8,128)(2,1)}), bf16[4,45,16,128]{3,2,1,0:T(8,128)(2,1)S(1)}, u32[]{:S(2)}, u32[]{:S(2)}) async-start(bf16[4,45,16,128]{3,2,1,0:T(8,128)(2,1)} %pad_maximum_fusion.1), calls=%async_computation | async-start | bytes 1474560 | tf_op jit(solution)/shard_map/all_to_all | solution.py:951
  175.4 1.0 convert_add_fusion.2
  176.4 1.5 collective-permute-start.17
  177.9 17.1 %shard_map.285 = (f32[2048,1280]{1,0:T(8,128)}, f32[2,1280]{1,0:T(2,128)}) custom-call(s32[4]{0:T(128)} %pad_add_fusion.place_ref, bf16[1024,640]{1,0:T(8,128)(2,1)} %get-tuple-element.147.dpre0_ref, bf16[1024,640]{1,0:T(8,128)(2,1)} %get-tuple-element.148.dpre1_ref, bf16[2048,1280]{1,0:T(8,128)(2,1)} %get-tuple-element.149.xhat_ref, ...), custom_call_target="tpu_custom_call" | custom-call | flops 18699999232 | bytes 57800000 | tf_op jit(solution)/shard_map/pallas_call | solution.py:1122
  195.4 1.0 broadcast_in_dim.2
  196.3 5.0 %all-to-all-start.1 = ((bf16[4,45,16,128]{3,2,1,0:T(8,128)(2,1)}), bf16[4,45,16,128]{3,2,1,0:T(8,128)(2,1)}, u32[]{:S(2)}, u32[]{:S(2)}) async-start(bf16[4,45,16,128]{3,2,1,0:T(8,128)(2,1)} %broadcast_in_dim.2), calls=%async_computation.1 | async-start | bytes 1474560 | tf_op jit(solution)/shard_map/all_to_all | solution.py:951
  201.3 0.8 collective-permute-start.18
  202.2 1.0 shard_map.286
  203.4 1.2 collective-permute-done.19
  205.3 3.3 %collective-permute-done.20 = f32[5,16,128]{2,1,0:T(8,128)S(1)} collective-permute-done((f32[5,16,128]{2,1,0:T(8,128)S(1)}, f32[5,16,128]{2,1,0:T(8,128)S(1)}, u32[]{:S(2)}, u32[]{:S(2)}) %collective-permute-start.20) | collective-permute-done | bytes 40992 | tf_op jit(solution)/shard_map/ppermute | solution.py:852
  208.7 2.1 collective-permute-start.21
  210.8 1.3 collective-permute-start.22
  212.1 2.7 %collective-permute-done.22 = f32[5,16,128]{2,1,0:T(8,128)S(1)} collective-permute-done((f32[5,16,128]{2,1,0:T(8,128)S(1)}, f32[5,16,128]{2,1,0:T(8,128)S(1)}, u32[]{:S(2)}, u32[]{:S(2)}) %collective-permute-start.22) | collective-permute-done | bytes 40992 | tf_op jit(solution)/shard_map/ppermute | solution.py:852
  214.8 3.4 %collective-permute-done.21 = bf16[1,52,16,128]{3,2,1,0:T(8,128)(2,1)S(1)} collective-permute-done((bf16[1,52,16,128]{3,2,1,0:T(8,128)(2,1)S(1)}, bf16[1,52,16,128]{3,2,1,0:T(8,128)(2,1)S(1)}, u32[]{:S(2)}, u32[]{:S(2)}) %collective-permute-start.21) | collective-permute-done | bytes 213024 | tf_op jit(solution)/shard_map/ppermute | solution.py:852
  218.2 2.1 all-to-all-done.1.mine_ref
  221.0 3.2 %collective-permute-start.26 = (f32[5,16,128]{2,1,0:T(8,128)S(1)}, f32[5,16,128]{2,1,0:T(8,128)S(1)}, u32[]{:S(2)}, u32[]{:S(2)}) collective-permute-start(f32[5,16,128]{2,1,0:T(8,128)S(1)} %add.216), channel_id=1, source_target_pairs={{0,16},{1,17},{2,18},{3,19},{4,20},{5,21},{6,22},{7,23},{8,24},{9,... | collective-permute-start | bytes 122888 | tf_op jit(solution)/shard_map/ppermute | solution.py:852
  224.2 1.2 collective-permute-start.27
  225.5 1.2 collective-permute-start.23
  226.9 3.3 %collective-permute-done.27 = f32[5,16,128]{2,1,0:T(8,128)S(1)} collective-permute-done((f32[5,16,128]{2,1,0:T(8,128)S(1)}, f32[5,16,128]{2,1,0:T(8,128)S(1)}, u32[]{:S(2)}, u32[]{:S(2)}) %collective-permute-start.27) | collective-permute-done | bytes 40992 | tf_op jit(solution)/shard_map/ppermute | solution.py:852
  230.1 6.5 %collective-permute-done.23 = bf16[1,52,16,128]{3,2,1,0:T(8,128)(2,1)S(1)} collective-permute-done((bf16[1,52,16,128]{3,2,1,0:T(8,128)(2,1)S(1)}, bf16[1,52,16,128]{3,2,1,0:T(8,128)(2,1)S(1)}, u32[]{:S(2)}, u32[]{:S(2)}) %collective-permute-start.23) | collective-permute-done | bytes 213024 | tf_op jit(solution)/shard_map/ppermute | solution.py:852
  236.7 1.2 collective-permute-done.24.other_ref
  238.0 0.8 collective-permute-start.28
  238.8 7.4 %shard_map.287 = (f32[800,640]{1,0:T(8,128)}, f32[160,1280]{1,0:T(8,128)}, f32[800,640]{1,0:T(8,128)}, f32[160,1280]{1,0:T(8,128)}, f32[800]{0:T(1024)}, /*index=5*/f32[160]{0:T(256)}, f32[640]{0:T(1024)}, f32[1280]{0:T(1024)}) custom-call(s32[4]{0:T(128)S(1)} %copy-done.6, bf16[4,45,16,128]{3,2,1,0:T(8,128)(2,1)} %all-to-all-done.1.mine_ref, ...), custom_call_target="tpu_custom_call" | custom-call | flops 8800000000 | bytes 27200000 | tf_op jit(solution)/shard_map/pallas_call | solution.py:1201
  246.3 1.3 shard_map.288
  247.7 0.8 collective-permute-start.30
  248.5 1.1 collective-permute-start.31
  249.6 2.1 collective-permute-done.30
  251.8 3.1 %shard_map.289 = (f32[320,640]{1,0:T(8,128)}, f32[320,640]{1,0:T(8,128)}, f32[320]{0:T(512)}, f32[640]{0:T(1024)}, f32[2,2560]{1,0:T(2,128)}, /*index=5*/f32[2,2560]{1,0:T(2,128)}, f32[2,2560]{1,0:T(2,128)}) custom-call(s32[4]{0:T(128)S(1)} %copy-done.6, bf16[52,16,128]{2,1,0:T(8,128)(2,1)S(1)} %bitcast.39, ...), custom_call_target="tpu_custom_call" | custom-call | flops 4400000000 | bytes 13600000 | tf_op jit(solution)/shard_map/pallas_call | solution.py:1230
  (127 shorter events, 10.9 us)
Async XLA Ops:
  2.0 20.8 %copy-start.20 = (bf16[320,640]{1,0:T(8,128)(2,1)}, bf16[320,640]{1,0:T(8,128)(2,1)S(1)}, u32[]{:S(2)}) copy-start(bf16[320,640]{1,0:T(8,128)(2,1)S(1)} %convert_element_type.205.refs_0_) | copy-start | bytes 1228804
  2.0 20.8 %collective-permute-start.1 = (bf16[320,640]{1,0:T(8,128)(2,1)S(1)}, bf16[320,640]{1,0:T(8,128)(2,1)S(1)}, u32[]{:S(2)}, u32[]{:S(2)}) collective-permute-start(bf16[320,640]{1,0:T(8,128)(2,1)S(1)} %convert_element_type.205.refs_0_), channel_id=1, source_target_pairs={{0,2},{1,3},{2,0},{3,1},{4,6},{5,7},{6,4},{7,5},{8,10},{9,11},{10,... | collective-permute-start | bytes 1228808 | tf_op jit(solution)/shard_map/ppermute | solution.py:852
  5.4 31.3 %copy-start.23 = (bf16[1120,640]{1,0:T(8,128)(2,1)}, bf16[1120,640]{1,0:T(8,128)(2,1)S(1)}, u32[]{:S(2)}) copy-start(bf16[1120,640]{1,0:T(8,128)(2,1)S(1)} %pad_maximum_fusion.refs_0_) | copy-start | bytes 4300804
  5.4 43.9 %collective-permute-start.6 = (bf16[1120,640]{1,0:T(8,128)(2,1)S(1)}, bf16[1120,640]{1,0:T(8,128)(2,1)}, u32[]{:S(2)}, u32[]{:S(2)}) collective-permute-start(bf16[1120,640]{1,0:T(8,128)(2,1)S(1)} %pad_maximum_fusion.refs_0_), channel_id=1, source_target_pairs={{0,2},{1,3},{2,0},{3,1},{4,6},{5,7},{6,4},{7,5},{8,10},{9,11},{10,... | collective-permute-start | bytes 4300808 | tf_op jit(solution)/shard_map/ppermute | solution.py:852
  22.8 1.8 collective-permute-start
  22.9 2.3 collective-permute-start.2
  35.8 13.4 %collective-permute-start.3 = (bf16[256,640]{1,0:T(8,128)(2,1)}, bf16[256,640]{1,0:T(8,128)(2,1)S(1)}, u32[]{:S(2)}, u32[]{:S(2)}) collective-permute-start(bf16[256,640]{1,0:T(8,128)(2,1)} %get-tuple-element.106), channel_id=1, source_target_pairs={{0,1},{1,0},{2,3},{3,2},{4,5},{5,4},{6,7},{7,6},{8,9},{9,8},{10,11... | collective-permute-start | bytes 983048 | tf_op jit(solution)/shard_map/ppermute | solution.py:852
  36.0 13.2 %collective-permute-start.4 = (bf16[256,640]{1,0:T(8,128)(2,1)}, bf16[256,640]{1,0:T(8,128)(2,1)S(1)}, u32[]{:S(2)}, u32[]{:S(2)}) collective-permute-start(bf16[256,640]{1,0:T(8,128)(2,1)} %get-tuple-element.113), channel_id=1, source_target_pairs={{1,2},{2,1},{3,4},{4,3},{5,6},{6,5},{7,8},{8,7},{9,10},{10,9},{11,... | collective-permute-start | bytes 983048 | tf_op jit(solution)/shard_map/ppermute | solution.py:1017
  36.7 15.3 %collective-permute-start.5 = (bf16[1120,640]{1,0:T(8,128)(2,1)S(1)}, bf16[1120,640]{1,0:T(8,128)(2,1)S(1)}, u32[]{:S(2)}, u32[]{:S(2)}) collective-permute-start(bf16[1120,640]{1,0:T(8,128)(2,1)S(1)} %pad_maximum_fusion.refs_0_), channel_id=1, source_target_pairs={{0,1},{1,0},{2,3},{3,2},{4,5},{5,4},{6,7},{7,6},{8,9},{9,8},{10,11... | collective-permute-start | bytes 4300808 | tf_op jit(solution)/shard_map/ppermute | solution.py:852
  49.3 5.8 %collective-permute-start.7 = (bf16[1120,640]{1,0:T(8,128)(2,1)}, bf16[1120,640]{1,0:T(8,128)(2,1)S(1)}, u32[]{:S(2)}, u32[]{:S(2)}) collective-permute-start(bf16[1120,640]{1,0:T(8,128)(2,1)} %collective-permute-done.6.refs_2_), channel_id=1, source_target_pairs={{0,1},{1,0},{2,3},{3,2},{4,5},{5,4},{6,7},{7,6},{8,9},{9,8},{10,11... | collective-permute-start | bytes 4300808 | tf_op jit(solution)/shard_map/ppermute | solution.py:852
  111.0 11.8 %collective-permute-start.10 = (bf16[2,184,16,128]{3,2,1,0:T(8,128)(2,1)}, bf16[2,184,16,128]{3,2,1,0:T(8,128)(2,1)S(1)}, u32[]{:S(2)}, u32[]{:S(2)}) collective-permute-start(bf16[2,184,16,128]{3,2,1,0:T(8,128)(2,1)} %get-tuple-element.120), channel_id=1, source_target_pairs={{0,1},{1,0},{2,3},{3,2},{4,5},{5,4},{6,7},{7,6},{8,9},{9,8},{10,11... | collective-permute-start | bytes 4521992 | tf_op jit(solution)/shard_map/ppermute | solution.py:852
  111.4 11.3 %collective-permute-start.11 = (bf16[2,176,16,128]{3,2,1,0:T(8,128)(2,1)}, bf16[2,176,16,128]{3,2,1,0:T(8,128)(2,1)S(1)}, u32[]{:S(2)}, u32[]{:S(2)}) collective-permute-start(bf16[2,176,16,128]{3,2,1,0:T(8,128)(2,1)} %get-tuple-element.121), channel_id=1, source_target_pairs={{0,1},{1,0},{2,3},{3,2},{4,5},{5,4},{6,7},{7,6},{8,9},{9,8},{10,11... | collective-permute-start | bytes 4325384 | tf_op jit(solution)/shard_map/ppermute | solution.py:852
  111.6 11.2 %collective-permute-start.8 = (bf16[256,640]{1,0:T(8,128)(2,1)}, bf16[256,640]{1,0:T(8,128)(2,1)S(1)}, u32[]{:S(2)}, u32[]{:S(2)}) collective-permute-start(bf16[256,640]{1,0:T(8,128)(2,1)} %get-tuple-element.118), channel_id=1, source_target_pairs={{0,1},{1,0},{2,3},{3,2},{4,5},{5,4},{6,7},{7,6},{8,9},{9,8},{10,11... | collective-permute-start | bytes 983048 | tf_op jit(solution)/shard_map/ppermute | solution.py:852
  111.9 10.8 %collective-permute-start.9 = (bf16[256,640]{1,0:T(8,128)(2,1)}, bf16[256,640]{1,0:T(8,128)(2,1)S(1)}, u32[]{:S(2)}, u32[]{:S(2)}) collective-permute-start(bf16[256,640]{1,0:T(8,128)(2,1)} %get-tuple-element.119), channel_id=1, source_target_pairs={{1,2},{2,1},{3,4},{4,3},{5,6},{6,5},{7,8},{8,7},{9,10},{10,9},{11,... | collective-permute-start | bytes 983048 | tf_op jit(solution)/shard_map/ppermute | solution.py:1017
  112.6 11.0 %copy-start.22 = (bf16[2,176,16,128]{3,2,1,0:T(8,128)(2,1)S(1)}, bf16[2,176,16,128]{3,2,1,0:T(8,128)(2,1)}, u32[]{:S(2)}) copy-start(bf16[2,176,16,128]{3,2,1,0:T(8,128)(2,1)} %get-tuple-element.125) | copy-start | bytes 4325380
  124.8 22.3 %collective-permute-start.13 = (bf16[2,88,16,128]{3,2,1,0:T(8,128)(2,1)}, bf16[2,88,16,128]{3,2,1,0:T(8,128)(2,1)S(1)}, u32[]{:S(2)}, u32[]{:S(2)}) collective-permute-start(bf16[2,88,16,128]{3,2,1,0:T(8,128)(2,1)} %get-tuple-element.190), channel_id=1, source_target_pairs={{0,4},{1,5},{2,6},{3,7},{4,0},{5,1},{6,2},{7,3},{8,12},{9,13},{10,... | collective-permute-start | bytes 2162696 | tf_op jit(solution)/shard_map/ppermute | solution.py:852
  130.3 18.2 %collective-permute-start.12 = (bf16[1,184,16,128]{3,2,1,0:T(8,128)(2,1)S(1)}, bf16[1,184,16,128]{3,2,1,0:T(8,128)(2,1)S(1)}, u32[]{:S(2)}, u32[]{:S(2)}) collective-permute-start(bf16[1,184,16,128]{3,2,1,0:T(8,128)(2,1)S(1)} %get-tuple-element.187), channel_id=1, source_target_pairs={{0,2},{1,3},{2,0},{3,1},{4,6},{5,7},{6,4},{7,5},{8,10},{9,11},{10,... | collective-permute-start | bytes 2261000 | tf_op jit(solution)/shard_map/ppermute | solution.py:852
  147.1 21.1 %copy-start.25 = (bf16[2,88,16,128]{3,2,1,0:T(8,128)(2,1)}, bf16[2,88,16,128]{3,2,1,0:T(8,128)(2,1)S(1)}, u32[]{:S(2)}) copy-start(bf16[2,88,16,128]{3,2,1,0:T(8,128)(2,1)S(1)} %collective-permute-done.13) | copy-start | bytes 2162692
  148.5 19.8 %collective-permute-start.15 = (bf16[1,88,16,128]{3,2,1,0:T(8,128)(2,1)S(1)}, bf16[1,88,16,128]{3,2,1,0:T(8,128)(2,1)S(1)}, u32[]{:S(2)}, u32[]{:S(2)}) collective-permute-start(bf16[1,88,16,128]{3,2,1,0:T(8,128)(2,1)S(1)} %fusion.4), channel_id=1, source_target_pairs={{0,2},{1,3},{2,0},{3,1},{4,6},{5,7},{6,4},{7,5},{8,10},{9,11},{10,... | collective-permute-start | bytes 1081352 | tf_op jit(solution)/shard_map/ppermute | solution.py:852
  150.0 18.3 %collective-permute-start.14 = (bf16[1,92,16,128]{3,2,1,0:T(8,128)(2,1)S(1)}, bf16[1,92,16,128]{3,2,1,0:T(8,128)(2,1)S(1)}, u32[]{:S(2)}, u32[]{:S(2)}) collective-permute-start(bf16[1,92,16,128]{3,2,1,0:T(8,128)(2,1)S(1)} %fusion.6), channel_id=1, source_target_pairs={{0,4},{1,5},{2,6},{3,7},{4,0},{5,1},{6,2},{7,3},{8,12},{9,13},{10,... | collective-permute-start | bytes 1130504 | tf_op jit(solution)/shard_map/ppermute | solution.py:852
  168.3 7.1 %collective-permute-start.16 = (bf16[2,104,16,128]{3,2,1,0:T(8,128)(2,1)}, bf16[2,104,16,128]{3,2,1,0:T(8,128)(2,1)S(1)}, u32[]{:S(2)}, u32[]{:S(2)}) collective-permute-start(bf16[2,104,16,128]{3,2,1,0:T(8,128)(2,1)} %get-tuple-element.144), channel_id=1, source_target_pairs={{0,1},{1,0},{2,3},{3,2},{4,5},{5,4},{6,7},{7,6},{8,9},{9,8},{10,11... | collective-permute-start | bytes 2555912 | tf_op jit(solution)/shard_map/ppermute | solution.py:852
  170.6 24.5 %all-to-all-start = ((bf16[4,45,16,128]{3,2,1,0:T(8,128)(2,1)}), bf16[4,45,16,128]{3,2,1,0:T(8,128)(2,1)S(1)}, u32[]{:S(2)}, u32[]{:S(2)}) async-start(bf16[4,45,16,128]{3,2,1,0:T(8,128)(2,1)} %pad_maximum_fusion.1), calls=%async_computation | async-start | bytes 1474560 | tf_op jit(solution)/shard_map/all_to_all | solution.py:951
  176.4 24.9 %copy-start.18 = (f32[1,104,16,128]{3,2,1,0:T(8,128)}, f32[1,104,16,128]{3,2,1,0:T(8,128)S(1)}, u32[]{:S(2)}) copy-start(f32[1,104,16,128]{3,2,1,0:T(8,128)S(1)} %get-tuple-element.191) | copy-start | bytes 2555908
  176.4 18.7 %collective-permute-start.17 = (bf16[1,104,16,128]{3,2,1,0:T(8,128)(2,1)}, bf16[1,104,16,128]{3,2,1,0:T(8,128)(2,1)S(1)}, u32[]{:S(2)}, u32[]{:S(2)}) collective-permute-start(bf16[1,104,16,128]{3,2,1,0:T(8,128)(2,1)} %get-tuple-element.192), channel_id=1, source_target_pairs={{0,2},{1,3},{2,0},{3,1},{4,6},{5,7},{6,4},{7,5},{8,10},{9,11},{10,... | collective-permute-start | bytes 1277960 | tf_op jit(solution)/shard_map/ppermute | solution.py:852
  195.3 6.9 %copy-start.6 = (s32[4]{0:T(128)S(1)}, s32[4]{0:T(128)}, u32[]{:S(2)}) copy-start(s32[4]{0:T(128)} %pad_add_fusion.place_ref) | copy-start | bytes 52
  195.3 6.9 %copy-start.9 = (f32[800]{0:T(1024)S(1)}, f32[800]{0:T(1024)}, u32[]{:S(2)}) copy-start(f32[800]{0:T(1024)} %refs_2_.4) | copy-start | bytes 9604
  195.3 6.9 %copy-start.12 = (f32[320]{0:T(512)S(1)}, f32[320]{0:T(512)}, u32[]{:S(2)}) copy-start(f32[320]{0:T(512)} %refs_1_.5) | copy-start | bytes 3844
  195.3 6.9 %copy-start.13 = (f32[160]{0:T(256)S(1)}, f32[160]{0:T(256)}, u32[]{:S(2)}) copy-start(f32[160]{0:T(256)} %refs_3_.1) | copy-start | bytes 1924
  195.3 6.9 %copy-start.14 = (f32[2,1280]{1,0:T(2,128)S(1)}, f32[2,1280]{1,0:T(2,128)}, u32[]{:S(2)}) copy-start(f32[2,1280]{1,0:T(2,128)} %get-tuple-element.158.refs_3_) | copy-start | bytes 30724
  196.3 24.0 %all-to-all-start.1 = ((bf16[4,45,16,128]{3,2,1,0:T(8,128)(2,1)}), bf16[4,45,16,128]{3,2,1,0:T(8,128)(2,1)}, u32[]{:S(2)}, u32[]{:S(2)}) async-start(bf16[4,45,16,128]{3,2,1,0:T(8,128)(2,1)} %broadcast_in_dim.2), calls=%async_computation.1 | async-start | bytes 1474560 | tf_op jit(solution)/shard_map/all_to_all | solution.py:951
  201.3 7.3 %collective-permute-start.18 = (bf16[1,52,16,128]{3,2,1,0:T(8,128)(2,1)S(1)}, bf16[1,52,16,128]{3,2,1,0:T(8,128)(2,1)S(1)}, u32[]{:S(2)}, u32[]{:S(2)}) collective-permute-start(bf16[1,52,16,128]{3,2,1,0:T(8,128)(2,1)S(1)} %fusion.7), channel_id=1, source_target_pairs={{0,4},{1,5},{2,6},{3,7},{4,0},{5,1},{6,2},{7,3},{8,12},{9,13},{10,... | collective-permute-start | bytes 638984 | tf_op jit(solution)/shard_map/ppermute | solution.py:852
  203.3 35.5 %copy-start.1 = (f32[800,640]{1,0:T(8,128)S(1)}, f32[800,640]{1,0:T(8,128)}, u32[]{:S(2)}) copy-start(f32[800,640]{1,0:T(8,128)} %refs_0_.4) | copy-start | bytes 6144004
  203.3 35.5 %copy-start.3 = (f32[160,1280]{1,0:T(8,128)S(1)}, f32[160,1280]{1,0:T(8,128)}, u32[]{:S(2)}) copy-start(f32[160,1280]{1,0:T(8,128)} %refs_1_.4) | copy-start | bytes 2457604
  203.3 35.5 %copy-start.8 = (f32[1280]{0:T(1024)S(1)}, f32[1280]{0:T(1024)}, u32[]{:S(2)}) copy-start(f32[1280]{0:T(1024)} %refs_5_.1) | copy-start | bytes 15364
  203.3 35.5 %copy-start.10 = (f32[640]{0:T(1024)S(1)}, f32[640]{0:T(1024)}, u32[]{:S(2)}) copy-start(f32[640]{0:T(1024)} %refs_4_.1) | copy-start | bytes 7684
  203.3 1.3 collective-permute-start.19
  204.6 4.0 %collective-permute-start.20 = (f32[5,16,128]{2,1,0:T(8,128)S(1)}, f32[5,16,128]{2,1,0:T(8,128)S(1)}, u32[]{:S(2)}, u32[]{:S(2)}) collective-permute-start(f32[5,16,128]{2,1,0:T(8,128)S(1)} %add.213), channel_id=1, source_target_pairs={{0,2},{1,3},{2,0},{3,1},{4,6},{5,7},{6,4},{7,5},{8,10},{9,11},{10,... | collective-permute-start | bytes 122888 | tf_op jit(solution)/shard_map/ppermute | solution.py:852
  208.7 9.5 %collective-permute-start.21 = (bf16[1,52,16,128]{3,2,1,0:T(8,128)(2,1)S(1)}, bf16[1,52,16,128]{3,2,1,0:T(8,128)(2,1)S(1)}, u32[]{:S(2)}, u32[]{:S(2)}) collective-permute-start(bf16[1,52,16,128]{3,2,1,0:T(8,128)(2,1)S(1)} %fusion.5), channel_id=1, source_target_pairs={{0,8},{1,9},{2,10},{3,11},{4,12},{5,13},{6,14},{7,15},{8,0},{9,1},... | collective-permute-start | bytes 638984 | tf_op jit(solution)/shard_map/ppermute | solution.py:852
  210.8 4.0 %collective-permute-start.22 = (f32[5,16,128]{2,1,0:T(8,128)S(1)}, f32[5,16,128]{2,1,0:T(8,128)S(1)}, u32[]{:S(2)}, u32[]{:S(2)}) collective-permute-start(f32[5,16,128]{2,1,0:T(8,128)S(1)} %add.214), channel_id=1, source_target_pairs={{0,4},{1,5},{2,6},{3,7},{4,0},{5,1},{6,2},{7,3},{8,12},{9,13},{10,... | collective-permute-start | bytes 122888 | tf_op jit(solution)/shard_map/ppermute | solution.py:852
  220.3 17.7 %collective-permute-start.24 = (bf16[4,45,16,128]{3,2,1,0:T(8,128)(2,1)}, bf16[4,45,16,128]{3,2,1,0:T(8,128)(2,1)S(1)}, u32[]{:S(2)}, u32[]{:S(2)}) collective-permute-start(bf16[4,45,16,128]{3,2,1,0:T(8,128)(2,1)} %all-to-all-done.1.mine_ref), channel_id=1, source_target_pairs={{0,4},{1,5},{2,6},{3,7},{4,0},{5,1},{6,2},{7,3},{8,12},{9,13},{10,... | collective-permute-start | bytes 2211848 | tf_op jit(solution)/shard_map/ppermute | solution.py:852
  221.0 5.6 %collective-permute-start.25 = (f32[5,16,128]{2,1,0:T(8,128)S(1)}, f32[5,16,128]{2,1,0:T(8,128)S(1)}, u32[]{:S(2)}, u32[]{:S(2)}) collective-permute-start(f32[5,16,128]{2,1,0:T(8,128)S(1)} %add.216), channel_id=1, source_target_pairs={{0,8},{1,9},{2,10},{3,11},{4,12},{5,13},{6,14},{7,15},{8,0},{9,1},... | collective-permute-start | bytes 122888 | tf_op jit(solution)/shard_map/ppermute | solution.py:852
  221.0 5.8 %collective-permute-start.26 = (f32[5,16,128]{2,1,0:T(8,128)S(1)}, f32[5,16,128]{2,1,0:T(8,128)S(1)}, u32[]{:S(2)}, u32[]{:S(2)}) collective-permute-start(f32[5,16,128]{2,1,0:T(8,128)S(1)} %add.216), channel_id=1, source_target_pairs={{0,16},{1,17},{2,18},{3,19},{4,20},{5,21},{6,22},{7,23},{8,24},{9,... | collective-permute-start | bytes 122888 | tf_op jit(solution)/shard_map/ppermute | solution.py:852
  224.2 5.9 %collective-permute-start.27 = (f32[5,16,128]{2,1,0:T(8,128)S(1)}, f32[5,16,128]{2,1,0:T(8,128)S(1)}, u32[]{:S(2)}, u32[]{:S(2)}) collective-permute-start(f32[5,16,128]{2,1,0:T(8,128)S(1)} %add.216), channel_id=1, source_target_pairs={{0,24},{1,25},{2,26},{3,27},{4,28},{5,29},{6,30},{7,31},{8,16},{9,... | collective-permute-start | bytes 122888 | tf_op jit(solution)/shard_map/ppermute | solution.py:852
  225.5 11.2 %collective-permute-start.23 = (bf16[1,52,16,128]{3,2,1,0:T(8,128)(2,1)S(1)}, bf16[1,52,16,128]{3,2,1,0:T(8,128)(2,1)S(1)}, u32[]{:S(2)}, u32[]{:S(2)}) collective-permute-start(bf16[1,52,16,128]{3,2,1,0:T(8,128)(2,1)S(1)} %add_convert_fusion.5), channel_id=1, source_target_pairs={{0,16},{1,17},{2,18},{3,19},{4,20},{5,21},{6,22},{7,23},{8,24},{9,... | collective-permute-start | bytes 638984 | tf_op jit(solution)/shard_map/ppermute | solution.py:852
  238.0 8.3 %collective-permute-start.28 = (bf16[52,16,128]{2,1,0:T(8,128)(2,1)S(1)}, bf16[52,16,128]{2,1,0:T(8,128)(2,1)S(1)}, u32[]{:S(2)}, u32[]{:S(2)}) collective-permute-start(bf16[52,16,128]{2,1,0:T(8,128)(2,1)S(1)} %bitcast.37), channel_id=1, source_target_pairs={{0,4},{1,5},{2,6},{3,7},{4,0},{5,1},{6,2},{7,3},{8,12},{9,13},{10,... | collective-permute-start | bytes 638984 | tf_op jit(solution)/shard_map/ppermute | solution.py:852
  247.6 1.9 collective-permute-start.29
  247.7 3.9 %collective-permute-start.30 = (f32[8,640]{1,0:T(8,128)S(1)}, f32[8,640]{1,0:T(8,128)S(1)}, u32[]{:S(2)}, u32[]{:S(2)}) collective-permute-start(f32[8,640]{1,0:T(8,128)S(1)} %shard_map.288), channel_id=1, source_target_pairs={{0,2},{1,3},{2,0},{3,1},{4,6},{5,7},{6,4},{7,5},{8,10},{9,11},{10,... | collective-permute-start | bytes 61448 | tf_op jit(solution)/shard_map/ppermute | solution.py:852
  248.5 3.3 %collective-permute-start.31 = (f32[8,640]{1,0:T(8,128)S(1)}, f32[8,640]{1,0:T(8,128)S(1)}, u32[]{:S(2)}, u32[]{:S(2)}) collective-permute-start(f32[8,640]{1,0:T(8,128)S(1)} %shard_map.288), channel_id=1, source_target_pairs={{0,3},{1,2},{2,1},{3,0},{4,7},{5,6},{6,5},{7,4},{8,11},{9,10},{10,... | collective-permute-start | bytes 61448 | tf_op jit(solution)/shard_map/ppermute | solution.py:852
  (21 other events, 91.3 us)

commit v3 on v2

--- a/solution.py
+++ b/solution.py
@@ -289,13 +289,16 @@
         put_edges(place_ref, outs[5], outs[6], mov_ref, step == 0, step == 1)
 
 
-def load_window(place_ref, inner, mid, outer, ext_ref, sem):
+def load_window(place_ref, inner, mid, outer, ext_ref, sem, begin=0, end=None):
     rows, core = mid.shape[0], lax.rem(place_ref[0], 2)
+    end = rows if end is None else end
     near = pl.multiple_of((1 - core) * (REACH + rows), SUB)
     far = pl.multiple_of(core * (REACH + rows), SUB)
     return [
         pltpu.make_async_copy(inner, ext_ref.at[pl.ds(near, REACH), :], sem.at[0]),
-        pltpu.make_async_copy(mid, ext_ref.at[REACH : REACH + rows, :], sem.at[1]),
+        pltpu.make_async_copy(
+            mid.at[begin:end, :], ext_ref.at[REACH + begin : REACH + end, :], sem.at[1]
+        ),
         pltpu.make_async_copy(outer, ext_ref.at[pl.ds(far, REACH), :], sem.at[2]),
     ]
 
@@ -505,7 +508,9 @@
 
     @pl.when(step == 0)
     def _():
-        copies = load_window(place_ref, low_ref, d_ref, high_ref, ext_ref, sem)
+        half = d_ref.shape[0] // 2
+        begin, end = (half - REACH, 2 * half) if last else (0, half + REACH)
+        copies = load_window(place_ref, low_ref, d_ref, high_ref, ext_ref, sem, begin, end)
         copies.append(pltpu.make_async_copy(turned_ref, wt_ref, sem.at[3]))
         if last:
             copies.append(pltpu.make_async_copy(before_ref, grad_ref, sem.at[4]))

time: 258 us -> 258 us (level)
  transfers between devices with their start and end apart: 34 -> 34, of which waited for: 16 -> 17; matrix products, arithmetic and copies ran while one was open for 2% -> 2% of each run, Pallas kernels for 42% -> 41%
where the time goes in v3:
time: 258 us; the launch traced here: 255 us
  Pallas kernels  165 us (64%)
  starting transfers between devices  45.1 us (17%)
  waiting for transfers between devices  32.2 us (12%)
  other arithmetic  7.49 us (3%)
  local copies, waits for them, and re-layouts  3.82 us (1%)
    pallas_call x1, Pallas kernels, on_device(): call(functools.partial(conv_kernel, pieces, rows_of), (steps + 1,), [SMEM...  54.7 us
    ppermute x30, starting transfers between devices, flip(): return lax.ppermute(x, AXES, pairs)  34 us
    pallas_call x2, Pallas kernels, back_conv(): call(functools.partial(back_conv_kernel, last, w_in.shape[0]), (here,), [...  33.6 us
    ppermute x30, waiting for transfers between devices, flip(): return lax.ppermute(x, AXES, pairs)  30 us
    pallas_call x2, Pallas kernels, in_call(): call(functools.partial(in_kernel, pieces, tiles), (count,), [SMEM, whole(...  19.5 us
    pallas_call x1, Pallas kernels, on_device(): call(functools.partial(back_a_kernel, pieces, steps // 2), (steps,), [SME...  17.1 us
    pallas_call x1, Pallas kernels, on_device(): call(norm_a_kernel, (rows // tile_a,), [rows_spec(tile_a, D), params_spec...  16.8 us
    pallas_call x1, Pallas kernels, on_device(): call(functools.partial(out_kernel, pieces), (steps,), [SMEM, rows_spec(ti...  10.1 us
  transfers between devices with their start and end apart: 34, of which 17 were waited for; matrix products, arithmetic and copies ran while one was open for 2% of the time, Pallas kernels for 41%

profile of v3, /device:TPU:0, one launch (start us, length us, event | category | flops | bytes accessed | tf_op | source)
XLA Modules:
  0.0 254.9 jit_solution(3313960304104264918)
XLA Ops:
  0.7 1.3 convert_element_type.205.refs_0_
  2.0 3.0 %collective-permute-start.1 = (bf16[320,640]{1,0:T(8,128)(2,1)S(1)}, bf16[320,640]{1,0:T(8,128)(2,1)S(1)}, u32[]{:S(2)}, u32[]{:S(2)}) collective-permute-start(bf16[320,640]{1,0:T(8,128)(2,1)S(1)} %convert_element_type.205.refs_0_), channel_id=1, source_target_pairs={{0,2},{1,3},{2,0},{3,1},{4,6},{5,7},{6,4},{7,5},{8,10},{9,11},{10,... | collective-permute-start | bytes 1228808 | tf_op jit(solution)/shard_map/ppermute | solution.py:857
  6.0 16.8 %shard_map.278 = (bf16[2048,1280]{1,0:T(8,128)(2,1)}, bf16[2048,1280]{1,0:T(8,128)(2,1)}, bf16[2048,1280]{1,0:T(8,128)(2,1)}, f32[2048,128]{1,0:T(8,128)}) custom-call(bf16[2048,1280]{1,0:T(8,128)(2,1)} %tok_ref.3, f32[2,2560]{1,0:T(2,128)} %np_ref.14), custom_call_target="tpu_custom_call" | custom-call | flops 18699999232 | bytes 57800000 | tf_op jit(solution)/shard_map/pallas_call | solution.py:981
  25.9 9.9 %shard_map.279 = (bf16[2048,640]{1,0:T(8,128)(2,1)}, bf16[2048,640]{1,0:T(8,128)(2,1)}, bf16[2048,640]{1,0:T(8,128)(2,1)}, f32[2048,128]{1,0:T(8,128)}, f32[2048...) custom-call(s32[4]{0:T(128)} %pad_add_fusion.place_ref, s32[129]{0:T(256)} %lengths_ref.3, ...), custom_call_target="tpu_custom_call" | custom-call | flops 3300000000 | bytes 10200000 | tf_op jit(solution)/shard_map/pallas_call | solution.py:1003
  36.7 2.9 %collective-permute-start.5 = (bf16[1120,640]{1,0:T(8,128)(2,1)S(1)}, bf16[1120,640]{1,0:T(8,128)(2,1)S(1)}, u32[]{:S(2)}, u32[]{:S(2)}) collective-permute-start(bf16[1120,640]{1,0:T(8,128)(2,1)S(1)} %pad_maximum_fusion.refs_0_), channel_id=1, source_target_pairs={{0,1},{1,0},{2,3},{3,2},{4,5},{5,4},{6,7},{7,6},{8,9},{9,8},{10,11... | collective-permute-start | bytes 4300808 | tf_op jit(solution)/shard_map/ppermute | solution.py:857
  39.6 9.6 %shard_map.280 = (bf16[2048,640]{1,0:T(8,128)(2,1)}, bf16[2048,640]{1,0:T(8,128)(2,1)}, bf16[2048,640]{1,0:T(8,128)(2,1)}, f32[2048,128]{1,0:T(8,128)}, f32[2048,128]{1,0:T(8,128)}) custom-call(s32[4]{0:T(128)} %pad_add_fusion.place_ref, s32[129]{0:T(256)} %lengths_ref.3, ...), custom_call_target="tpu_custom_call", output_to_operand_aliasing={{0}: (9, {}), {1}: (10, {}), {2}: (11, {}), {3}: (12, {}), ... | custom-call | flops 3300000000 | bytes 10200000 | tf_op jit(solution)/shard_map/pallas_call | solution.py:1003
  49.3 2.8 %collective-permute-start.7 = (bf16[1120,640]{1,0:T(8,128)(2,1)}, bf16[1120,640]{1,0:T(8,128)(2,1)S(1)}, u32[]{:S(2)}, u32[]{:S(2)}) collective-permute-start(bf16[1120,640]{1,0:T(8,128)(2,1)} %collective-permute-done.6.refs_2_), channel_id=1, source_target_pairs={{0,1},{1,0},{2,3},{3,2},{4,5},{5,4},{6,7},{7,6},{8,9},{9,8},{10,11... | collective-permute-start | bytes 4300808 | tf_op jit(solution)/shard_map/ppermute | solution.py:857
  52.1 3.0 %collective-permute-done.7.refs_3_ = bf16[1120,640]{1,0:T(8,128)(2,1)S(1)} collective-permute-done((bf16[1120,640]{1,0:T(8,128)(2,1)}, bf16[1120,640]{1,0:T(8,128)(2,1)S(1)}, u32[]{:S(2)}, u32[]{:S(2)}) %collective-permute-start.7) | collective-permute-done | bytes 1433632 | tf_op jit(solution)/shard_map/ppermute | solution.py:857
  55.1 1.1 copy-done.30
  56.2 54.7 %shard_map.281 = (bf16[2048,640]{1,0:T(8,128)(2,1)}, bf16[2048,640]{1,0:T(8,128)(2,1)}, bf16[256,640]{1,0:T(8,128)(2,1)}, bf16[256,640]{1,0:T(8,128)(2,1)}, f32[...) custom-call(s32[4]{0:T(128)} %pad_add_fusion.place_ref, ...), custom_call_target="tpu_custom_call" | custom-call | flops 49500000256 | bytes 153000000 | tf_op jit(solution)/shard_map/pallas_call | solution.py:1042
  112.6 10.1 %shard_map.282 = bf16[2048,1280]{1,0:T(8,128)(2,1)} custom-call(s32[4]{0:T(128)} %pad_add_fusion.place_ref, bf16[2048,640]{1,0:T(8,128)(2,1)} %get-tuple-element.117.hid_ref, bf16[2048,1280]{1,0:T(8,128)(2,1)} %tok_ref.3, bf16[1120,640]{1,0:T(8,128)(2,1)} %copy-done.23, bf16[1120,640]{1,0:T(8,128)(2,1)} %copy-done.29, ...), custom_call_target="tpu_custom_call" | custom-call | flops 9900000256 | bytes 30600000 | tf_op jit(solution)/shard_map/pallas_call | solution.py:1071
  123.6 1.2 convert_add_fusion.1
  124.8 5.1 %collective-permute-start.13 = (bf16[2,88,16,128]{3,2,1,0:T(8,128)(2,1)}, bf16[2,88,16,128]{3,2,1,0:T(8,128)(2,1)S(1)}, u32[]{:S(2)}, u32[]{:S(2)}) collective-permute-start(bf16[2,88,16,128]{3,2,1,0:T(8,128)(2,1)} %get-tuple-element.190), channel_id=1, source_target_pairs={{0,4},{1,5},{2,6},{3,7},{4,0},{5,1},{6,2},{7,3},{8,12},{9,13},{10,... | collective-permute-start | bytes 2162696 | tf_op jit(solution)/shard_map/ppermute | solution.py:857
  130.3 16.5 %shard_map.283 = (bf16[1024,640]{1,0:T(8,128)(2,1)}, f32[2,640]{1,0:T(2,128)}, f32[640,1280]{1,0:T(8,128)}) custom-call(s32[4]{0:T(128)} %pad_add_fusion.place_ref, bf16[256,640]{1,0:T(8,128)(2,1)} %copy-done.31, bf16[2048,640]{1,0:T(8,128)(2,1)} %get-tuple-element.129.d_ref, bf16[256,640]{1,0:T(8,128)(2,1)} %copy-done.32, ...), custom_call_target="tpu_custom_call" | custom-call | flops 17600000000 | bytes 54400000 | tf_op jit(solution)/shard_map/pallas_call | solution.py:1089
  147.1 1.4 collective-permute-done.12
  148.5 1.4 collective-permute-start.15
  150.0 0.8 collective-permute-start.14
  150.8 17.2 %shard_map.284 = (bf16[1024,640]{1,0:T(8,128)(2,1)}, f32[2,640]{1,0:T(2,128)}, bf16[2,104,16,128]{3,2,1,0:T(8,128)(2,1)}, bf16[2,104,16,128]{3,2,1,0:T(8,128)(2,1)}) custom-call(s32[4]{0:T(128)} %pad_add_fusion.place_ref, bf16[256,640]{1,0:T(8,128)(2,1)} %copy-done.31, bf16[2048,640]{1,0:T(8,128)(2,1)} %get-tuple-element.129.d_ref, ...), custom_call_target="tpu_custom_call" | custom-call | flops 17600000000 | bytes 54400000 | tf_op jit(solution)/shard_map/pallas_call | solution.py:1089
  168.1 1.1 fusion.3
  169.4 0.9 pad_maximum_fusion.1
  170.3 4.8 %all-to-all-start = ((bf16[4,45,16,128]{3,2,1,0:T(8,128)(2,1)}), bf16[4,45,16,128]{3,2,1,0:T(8,128)(2,1)S(1)}, u32[]{:S(2)}, u32[]{:S(2)}) async-start(bf16[4,45,16,128]{3,2,1,0:T(8,128)(2,1)} %pad_maximum_fusion.1), calls=%async_computation | async-start | bytes 1474560 | tf_op jit(solution)/shard_map/all_to_all | solution.py:956
  175.2 1.0 convert_add_fusion.2
  176.1 1.5 collective-permute-start.17
  177.6 17.1 %shard_map.285 = (f32[2048,1280]{1,0:T(8,128)}, f32[2,1280]{1,0:T(2,128)}) custom-call(s32[4]{0:T(128)} %pad_add_fusion.place_ref, bf16[1024,640]{1,0:T(8,128)(2,1)} %get-tuple-element.147.dpre0_ref, bf16[1024,640]{1,0:T(8,128)(2,1)} %get-tuple-element.148.dpre1_ref, bf16[2048,1280]{1,0:T(8,128)(2,1)} %get-tuple-element.149.xhat_ref, ...), custom_call_target="tpu_custom_call" | custom-call | flops 18699999232 | bytes 57800000 | tf_op jit(solution)/shard_map/pallas_call | solution.py:1127
  195.1 1.0 broadcast_in_dim.2
  196.0 5.0 %all-to-all-start.1 = ((bf16[4,45,16,128]{3,2,1,0:T(8,128)(2,1)}), bf16[4,45,16,128]{3,2,1,0:T(8,128)(2,1)}, u32[]{:S(2)}, u32[]{:S(2)}) async-start(bf16[4,45,16,128]{3,2,1,0:T(8,128)(2,1)} %broadcast_in_dim.2), calls=%async_computation.1 | async-start | bytes 1474560 | tf_op jit(solution)/shard_map/all_to_all | solution.py:956
  201.1 0.8 collective-permute-start.18
  201.9 1.0 shard_map.286
  203.1 1.2 collective-permute-done.19
  205.1 3.3 %collective-permute-done.20 = f32[5,16,128]{2,1,0:T(8,128)S(1)} collective-permute-done((f32[5,16,128]{2,1,0:T(8,128)S(1)}, f32[5,16,128]{2,1,0:T(8,128)S(1)}, u32[]{:S(2)}, u32[]{:S(2)}) %collective-permute-start.20) | collective-permute-done | bytes 40992 | tf_op jit(solution)/shard_map/ppermute | solution.py:857
  208.4 2.1 collective-permute-start.21
  210.5 1.3 collective-permute-start.22
  211.8 2.7 %collective-permute-done.22 = f32[5,16,128]{2,1,0:T(8,128)S(1)} collective-permute-done((f32[5,16,128]{2,1,0:T(8,128)S(1)}, f32[5,16,128]{2,1,0:T(8,128)S(1)}, u32[]{:S(2)}, u32[]{:S(2)}) %collective-permute-start.22) | collective-permute-done | bytes 40992 | tf_op jit(solution)/shard_map/ppermute | solution.py:857
  214.5 3.4 %collective-permute-done.21 = bf16[1,52,16,128]{3,2,1,0:T(8,128)(2,1)S(1)} collective-permute-done((bf16[1,52,16,128]{3,2,1,0:T(8,128)(2,1)S(1)}, bf16[1,52,16,128]{3,2,1,0:T(8,128)(2,1)S(1)}, u32[]{:S(2)}, u32[]{:S(2)}) %collective-permute-start.21) | collective-permute-done | bytes 213024 | tf_op jit(solution)/shard_map/ppermute | solution.py:857
  217.9 2.1 all-to-all-done.1.mine_ref
  220.7 3.2 %collective-permute-start.26 = (f32[5,16,128]{2,1,0:T(8,128)S(1)}, f32[5,16,128]{2,1,0:T(8,128)S(1)}, u32[]{:S(2)}, u32[]{:S(2)}) collective-permute-start(f32[5,16,128]{2,1,0:T(8,128)S(1)} %add.216), channel_id=1, source_target_pairs={{0,16},{1,17},{2,18},{3,19},{4,20},{5,21},{6,22},{7,23},{8,24},{9,... | collective-permute-start | bytes 122888 | tf_op jit(solution)/shard_map/ppermute | solution.py:857
  224.0 1.1 collective-permute-start.27
  225.2 1.2 collective-permute-start.23
  226.6 3.3 %collective-permute-done.27 = f32[5,16,128]{2,1,0:T(8,128)S(1)} collective-permute-done((f32[5,16,128]{2,1,0:T(8,128)S(1)}, f32[5,16,128]{2,1,0:T(8,128)S(1)}, u32[]{:S(2)}, u32[]{:S(2)}) %collective-permute-start.27) | collective-permute-done | bytes 40992 | tf_op jit(solution)/shard_map/ppermute | solution.py:857
  229.9 6.5 %collective-permute-done.23 = bf16[1,52,16,128]{3,2,1,0:T(8,128)(2,1)S(1)} collective-permute-done((bf16[1,52,16,128]{3,2,1,0:T(8,128)(2,1)S(1)}, bf16[1,52,16,128]{3,2,1,0:T(8,128)(2,1)S(1)}, u32[]{:S(2)}, u32[]{:S(2)}) %collective-permute-start.23) | collective-permute-done | bytes 213024 | tf_op jit(solution)/shard_map/ppermute | solution.py:857
  236.4 1.2 collective-permute-done.24.other_ref
  237.7 0.8 collective-permute-start.28
  238.5 7.4 %shard_map.287 = (f32[800,640]{1,0:T(8,128)}, f32[160,1280]{1,0:T(8,128)}, f32[800,640]{1,0:T(8,128)}, f32[160,1280]{1,0:T(8,128)}, f32[800]{0:T(1024)}, /*index=5*/f32[160]{0:T(256)}, f32[640]{0:T(1024)}, f32[1280]{0:T(1024)}) custom-call(s32[4]{0:T(128)S(1)} %copy-done.6, bf16[4,45,16,128]{3,2,1,0:T(8,128)(2,1)} %all-to-all-done.1.mine_ref, ...), custom_call_target="tpu_custom_call" | custom-call | flops 8800000000 | bytes 27200000 | tf_op jit(solution)/shard_map/pallas_call | solution.py:1206
  246.0 1.3 shard_map.288
  247.4 0.8 collective-permute-start.30
  248.2 1.1 collective-permute-start.31
  249.3 2.1 collective-permute-done.30
  251.5 3.1 %shard_map.289 = (f32[320,640]{1,0:T(8,128)}, f32[320,640]{1,0:T(8,128)}, f32[320]{0:T(512)}, f32[640]{0:T(1024)}, f32[2,2560]{1,0:T(2,128)}, /*index=5*/f32[2,2560]{1,0:T(2,128)}, f32[2,2560]{1,0:T(2,128)}) custom-call(s32[4]{0:T(128)S(1)} %copy-done.6, bf16[52,16,128]{2,1,0:T(8,128)(2,1)S(1)} %bitcast.39, ...), custom_call_target="tpu_custom_call" | custom-call | flops 4400000000 | bytes 13600000 | tf_op jit(solution)/shard_map/pallas_call | solution.py:1235
  (127 shorter events, 11.1 us)
Async XLA Ops:
  2.0 20.8 %copy-start.20 = (bf16[320,640]{1,0:T(8,128)(2,1)}, bf16[320,640]{1,0:T(8,128)(2,1)S(1)}, u32[]{:S(2)}) copy-start(bf16[320,640]{1,0:T(8,128)(2,1)S(1)} %convert_element_type.205.refs_0_) | copy-start | bytes 1228804
  2.0 20.8 %collective-permute-start.1 = (bf16[320,640]{1,0:T(8,128)(2,1)S(1)}, bf16[320,640]{1,0:T(8,128)(2,1)S(1)}, u32[]{:S(2)}, u32[]{:S(2)}) collective-permute-start(bf16[320,640]{1,0:T(8,128)(2,1)S(1)} %convert_element_type.205.refs_0_), channel_id=1, source_target_pairs={{0,2},{1,3},{2,0},{3,1},{4,6},{5,7},{6,4},{7,5},{8,10},{9,11},{10,... | collective-permute-start | bytes 1228808 | tf_op jit(solution)/shard_map/ppermute | solution.py:857
  5.4 31.3 %copy-start.23 = (bf16[1120,640]{1,0:T(8,128)(2,1)}, bf16[1120,640]{1,0:T(8,128)(2,1)S(1)}, u32[]{:S(2)}) copy-start(bf16[1120,640]{1,0:T(8,128)(2,1)S(1)} %pad_maximum_fusion.refs_0_) | copy-start | bytes 4300804
  5.4 43.9 %collective-permute-start.6 = (bf16[1120,640]{1,0:T(8,128)(2,1)S(1)}, bf16[1120,640]{1,0:T(8,128)(2,1)}, u32[]{:S(2)}, u32[]{:S(2)}) collective-permute-start(bf16[1120,640]{1,0:T(8,128)(2,1)S(1)} %pad_maximum_fusion.refs_0_), channel_id=1, source_target_pairs={{0,2},{1,3},{2,0},{3,1},{4,6},{5,7},{6,4},{7,5},{8,10},{9,11},{10,... | collective-permute-start | bytes 4300808 | tf_op jit(solution)/shard_map/ppermute | solution.py:857
  22.8 1.8 collective-permute-start
  22.9 2.3 collective-permute-start.2
  35.8 13.4 %collective-permute-start.3 = (bf16[256,640]{1,0:T(8,128)(2,1)}, bf16[256,640]{1,0:T(8,128)(2,1)S(1)}, u32[]{:S(2)}, u32[]{:S(2)}) collective-permute-start(bf16[256,640]{1,0:T(8,128)(2,1)} %get-tuple-element.106), channel_id=1, source_target_pairs={{0,1},{1,0},{2,3},{3,2},{4,5},{5,4},{6,7},{7,6},{8,9},{9,8},{10,11... | collective-permute-start | bytes 983048 | tf_op jit(solution)/shard_map/ppermute | solution.py:857
  36.0 13.2 %collective-permute-start.4 = (bf16[256,640]{1,0:T(8,128)(2,1)}, bf16[256,640]{1,0:T(8,128)(2,1)S(1)}, u32[]{:S(2)}, u32[]{:S(2)}) collective-permute-start(bf16[256,640]{1,0:T(8,128)(2,1)} %get-tuple-element.113), channel_id=1, source_target_pairs={{1,2},{2,1},{3,4},{4,3},{5,6},{6,5},{7,8},{8,7},{9,10},{10,9},{11,... | collective-permute-start | bytes 983048 | tf_op jit(solution)/shard_map/ppermute | solution.py:1022
  36.7 15.3 %collective-permute-start.5 = (bf16[1120,640]{1,0:T(8,128)(2,1)S(1)}, bf16[1120,640]{1,0:T(8,128)(2,1)S(1)}, u32[]{:S(2)}, u32[]{:S(2)}) collective-permute-start(bf16[1120,640]{1,0:T(8,128)(2,1)S(1)} %pad_maximum_fusion.refs_0_), channel_id=1, source_target_pairs={{0,1},{1,0},{2,3},{3,2},{4,5},{5,4},{6,7},{7,6},{8,9},{9,8},{10,11... | collective-permute-start | bytes 4300808 | tf_op jit(solution)/shard_map/ppermute | solution.py:857
  49.3 5.8 %collective-permute-start.7 = (bf16[1120,640]{1,0:T(8,128)(2,1)}, bf16[1120,640]{1,0:T(8,128)(2,1)S(1)}, u32[]{:S(2)}, u32[]{:S(2)}) collective-permute-start(bf16[1120,640]{1,0:T(8,128)(2,1)} %collective-permute-done.6.refs_2_), channel_id=1, source_target_pairs={{0,1},{1,0},{2,3},{3,2},{4,5},{5,4},{6,7},{7,6},{8,9},{9,8},{10,11... | collective-permute-start | bytes 4300808 | tf_op jit(solution)/shard_map/ppermute | solution.py:857
  111.0 11.8 %collective-permute-start.10 = (bf16[2,184,16,128]{3,2,1,0:T(8,128)(2,1)}, bf16[2,184,16,128]{3,2,1,0:T(8,128)(2,1)S(1)}, u32[]{:S(2)}, u32[]{:S(2)}) collective-permute-start(bf16[2,184,16,128]{3,2,1,0:T(8,128)(2,1)} %get-tuple-element.120), channel_id=1, source_target_pairs={{0,1},{1,0},{2,3},{3,2},{4,5},{5,4},{6,7},{7,6},{8,9},{9,8},{10,11... | collective-permute-start | bytes 4521992 | tf_op jit(solution)/shard_map/ppermute | solution.py:857
  111.4 11.3 %collective-permute-start.11 = (bf16[2,176,16,128]{3,2,1,0:T(8,128)(2,1)}, bf16[2,176,16,128]{3,2,1,0:T(8,128)(2,1)S(1)}, u32[]{:S(2)}, u32[]{:S(2)}) collective-permute-start(bf16[2,176,16,128]{3,2,1,0:T(8,128)(2,1)} %get-tuple-element.121), channel_id=1, source_target_pairs={{0,1},{1,0},{2,3},{3,2},{4,5},{5,4},{6,7},{7,6},{8,9},{9,8},{10,11... | collective-permute-start | bytes 4325384 | tf_op jit(solution)/shard_map/ppermute | solution.py:857
  111.6 11.2 %collective-permute-start.8 = (bf16[256,640]{1,0:T(8,128)(2,1)}, bf16[256,640]{1,0:T(8,128)(2,1)S(1)}, u32[]{:S(2)}, u32[]{:S(2)}) collective-permute-start(bf16[256,640]{1,0:T(8,128)(2,1)} %get-tuple-element.118), channel_id=1, source_target_pairs={{0,1},{1,0},{2,3},{3,2},{4,5},{5,4},{6,7},{7,6},{8,9},{9,8},{10,11... | collective-permute-start | bytes 983048 | tf_op jit(solution)/shard_map/ppermute | solution.py:857
  111.9 10.8 %collective-permute-start.9 = (bf16[256,640]{1,0:T(8,128)(2,1)}, bf16[256,640]{1,0:T(8,128)(2,1)S(1)}, u32[]{:S(2)}, u32[]{:S(2)}) collective-permute-start(bf16[256,640]{1,0:T(8,128)(2,1)} %get-tuple-element.119), channel_id=1, source_target_pairs={{1,2},{2,1},{3,4},{4,3},{5,6},{6,5},{7,8},{8,7},{9,10},{10,9},{11,... | collective-permute-start | bytes 983048 | tf_op jit(solution)/shard_map/ppermute | solution.py:1022
  112.6 11.0 %copy-start.22 = (bf16[2,176,16,128]{3,2,1,0:T(8,128)(2,1)S(1)}, bf16[2,176,16,128]{3,2,1,0:T(8,128)(2,1)}, u32[]{:S(2)}) copy-start(bf16[2,176,16,128]{3,2,1,0:T(8,128)(2,1)} %get-tuple-element.125) | copy-start | bytes 4325380
  124.8 22.3 %collective-permute-start.13 = (bf16[2,88,16,128]{3,2,1,0:T(8,128)(2,1)}, bf16[2,88,16,128]{3,2,1,0:T(8,128)(2,1)S(1)}, u32[]{:S(2)}, u32[]{:S(2)}) collective-permute-start(bf16[2,88,16,128]{3,2,1,0:T(8,128)(2,1)} %get-tuple-element.190), channel_id=1, source_target_pairs={{0,4},{1,5},{2,6},{3,7},{4,0},{5,1},{6,2},{7,3},{8,12},{9,13},{10,... | collective-permute-start | bytes 2162696 | tf_op jit(solution)/shard_map/ppermute | solution.py:857
  130.3 18.2 %collective-permute-start.12 = (bf16[1,184,16,128]{3,2,1,0:T(8,128)(2,1)S(1)}, bf16[1,184,16,128]{3,2,1,0:T(8,128)(2,1)S(1)}, u32[]{:S(2)}, u32[]{:S(2)}) collective-permute-start(bf16[1,184,16,128]{3,2,1,0:T(8,128)(2,1)S(1)} %get-tuple-element.187), channel_id=1, source_target_pairs={{0,2},{1,3},{2,0},{3,1},{4,6},{5,7},{6,4},{7,5},{8,10},{9,11},{10,... | collective-permute-start | bytes 2261000 | tf_op jit(solution)/shard_map/ppermute | solution.py:857
  147.1 20.9 %copy-start.25 = (bf16[2,88,16,128]{3,2,1,0:T(8,128)(2,1)}, bf16[2,88,16,128]{3,2,1,0:T(8,128)(2,1)S(1)}, u32[]{:S(2)}) copy-start(bf16[2,88,16,128]{3,2,1,0:T(8,128)(2,1)S(1)} %collective-permute-done.13) | copy-start | bytes 2162692
  148.5 19.5 %collective-permute-start.15 = (bf16[1,88,16,128]{3,2,1,0:T(8,128)(2,1)S(1)}, bf16[1,88,16,128]{3,2,1,0:T(8,128)(2,1)S(1)}, u32[]{:S(2)}, u32[]{:S(2)}) collective-permute-start(bf16[1,88,16,128]{3,2,1,0:T(8,128)(2,1)S(1)} %fusion.4), channel_id=1, source_target_pairs={{0,2},{1,3},{2,0},{3,1},{4,6},{5,7},{6,4},{7,5},{8,10},{9,11},{10,... | collective-permute-start | bytes 1081352 | tf_op jit(solution)/shard_map/ppermute | solution.py:857
  150.0 18.0 %collective-permute-start.14 = (bf16[1,92,16,128]{3,2,1,0:T(8,128)(2,1)S(1)}, bf16[1,92,16,128]{3,2,1,0:T(8,128)(2,1)S(1)}, u32[]{:S(2)}, u32[]{:S(2)}) collective-permute-start(bf16[1,92,16,128]{3,2,1,0:T(8,128)(2,1)S(1)} %fusion.6), channel_id=1, source_target_pairs={{0,4},{1,5},{2,6},{3,7},{4,0},{5,1},{6,2},{7,3},{8,12},{9,13},{10,... | collective-permute-start | bytes 1130504 | tf_op jit(solution)/shard_map/ppermute | solution.py:857
  168.0 7.1 %collective-permute-start.16 = (bf16[2,104,16,128]{3,2,1,0:T(8,128)(2,1)}, bf16[2,104,16,128]{3,2,1,0:T(8,128)(2,1)S(1)}, u32[]{:S(2)}, u32[]{:S(2)}) collective-permute-start(bf16[2,104,16,128]{3,2,1,0:T(8,128)(2,1)} %get-tuple-element.144), channel_id=1, source_target_pairs={{0,1},{1,0},{2,3},{3,2},{4,5},{5,4},{6,7},{7,6},{8,9},{9,8},{10,11... | collective-permute-start | bytes 2555912 | tf_op jit(solution)/shard_map/ppermute | solution.py:857
  170.3 24.5 %all-to-all-start = ((bf16[4,45,16,128]{3,2,1,0:T(8,128)(2,1)}), bf16[4,45,16,128]{3,2,1,0:T(8,128)(2,1)S(1)}, u32[]{:S(2)}, u32[]{:S(2)}) async-start(bf16[4,45,16,128]{3,2,1,0:T(8,128)(2,1)} %pad_maximum_fusion.1), calls=%async_computation | async-start | bytes 1474560 | tf_op jit(solution)/shard_map/all_to_all | solution.py:956
  176.1 24.9 %copy-start.18 = (f32[1,104,16,128]{3,2,1,0:T(8,128)}, f32[1,104,16,128]{3,2,1,0:T(8,128)S(1)}, u32[]{:S(2)}) copy-start(f32[1,104,16,128]{3,2,1,0:T(8,128)S(1)} %get-tuple-element.191) | copy-start | bytes 2555908
  176.1 18.7 %collective-permute-start.17 = (bf16[1,104,16,128]{3,2,1,0:T(8,128)(2,1)}, bf16[1,104,16,128]{3,2,1,0:T(8,128)(2,1)S(1)}, u32[]{:S(2)}, u32[]{:S(2)}) collective-permute-start(bf16[1,104,16,128]{3,2,1,0:T(8,128)(2,1)} %get-tuple-element.192), channel_id=1, source_target_pairs={{0,2},{1,3},{2,0},{3,1},{4,6},{5,7},{6,4},{7,5},{8,10},{9,11},{10,... | collective-permute-start | bytes 1277960 | tf_op jit(solution)/shard_map/ppermute | solution.py:857
  195.0 6.9 %copy-start.6 = (s32[4]{0:T(128)S(1)}, s32[4]{0:T(128)}, u32[]{:S(2)}) copy-start(s32[4]{0:T(128)} %pad_add_fusion.place_ref) | copy-start | bytes 52
  195.0 6.9 %copy-start.9 = (f32[800]{0:T(1024)S(1)}, f32[800]{0:T(1024)}, u32[]{:S(2)}) copy-start(f32[800]{0:T(1024)} %refs_2_.4) | copy-start | bytes 9604
  195.0 6.9 %copy-start.12 = (f32[320]{0:T(512)S(1)}, f32[320]{0:T(512)}, u32[]{:S(2)}) copy-start(f32[320]{0:T(512)} %refs_1_.5) | copy-start | bytes 3844
  195.0 6.9 %copy-start.13 = (f32[160]{0:T(256)S(1)}, f32[160]{0:T(256)}, u32[]{:S(2)}) copy-start(f32[160]{0:T(256)} %refs_3_.1) | copy-start | bytes 1924
  195.0 6.9 %copy-start.14 = (f32[2,1280]{1,0:T(2,128)S(1)}, f32[2,1280]{1,0:T(2,128)}, u32[]{:S(2)}) copy-start(f32[2,1280]{1,0:T(2,128)} %get-tuple-element.158.refs_3_) | copy-start | bytes 30724
  196.0 23.9 %all-to-all-start.1 = ((bf16[4,45,16,128]{3,2,1,0:T(8,128)(2,1)}), bf16[4,45,16,128]{3,2,1,0:T(8,128)(2,1)}, u32[]{:S(2)}, u32[]{:S(2)}) async-start(bf16[4,45,16,128]{3,2,1,0:T(8,128)(2,1)} %broadcast_in_dim.2), calls=%async_computation.1 | async-start | bytes 1474560 | tf_op jit(solution)/shard_map/all_to_all | solution.py:956
  201.1 7.2 %collective-permute-start.18 = (bf16[1,52,16,128]{3,2,1,0:T(8,128)(2,1)S(1)}, bf16[1,52,16,128]{3,2,1,0:T(8,128)(2,1)S(1)}, u32[]{:S(2)}, u32[]{:S(2)}) collective-permute-start(bf16[1,52,16,128]{3,2,1,0:T(8,128)(2,1)S(1)} %fusion.7), channel_id=1, source_target_pairs={{0,4},{1,5},{2,6},{3,7},{4,0},{5,1},{6,2},{7,3},{8,12},{9,13},{10,... | collective-permute-start | bytes 638984 | tf_op jit(solution)/shard_map/ppermute | solution.py:857
  203.0 35.5 %copy-start.1 = (f32[800,640]{1,0:T(8,128)S(1)}, f32[800,640]{1,0:T(8,128)}, u32[]{:S(2)}) copy-start(f32[800,640]{1,0:T(8,128)} %refs_0_.4) | copy-start | bytes 6144004
  203.0 35.5 %copy-start.3 = (f32[160,1280]{1,0:T(8,128)S(1)}, f32[160,1280]{1,0:T(8,128)}, u32[]{:S(2)}) copy-start(f32[160,1280]{1,0:T(8,128)} %refs_1_.4) | copy-start | bytes 2457604
  203.0 35.5 %copy-start.8 = (f32[1280]{0:T(1024)S(1)}, f32[1280]{0:T(1024)}, u32[]{:S(2)}) copy-start(f32[1280]{0:T(1024)} %refs_5_.1) | copy-start | bytes 15364
  203.0 35.5 %copy-start.10 = (f32[640]{0:T(1024)S(1)}, f32[640]{0:T(1024)}, u32[]{:S(2)}) copy-start(f32[640]{0:T(1024)} %refs_4_.1) | copy-start | bytes 7684
  203.0 1.3 collective-permute-start.19
  204.3 4.0 %collective-permute-start.20 = (f32[5,16,128]{2,1,0:T(8,128)S(1)}, f32[5,16,128]{2,1,0:T(8,128)S(1)}, u32[]{:S(2)}, u32[]{:S(2)}) collective-permute-start(f32[5,16,128]{2,1,0:T(8,128)S(1)} %add.213), channel_id=1, source_target_pairs={{0,2},{1,3},{2,0},{3,1},{4,6},{5,7},{6,4},{7,5},{8,10},{9,11},{10,... | collective-permute-start | bytes 122888 | tf_op jit(solution)/shard_map/ppermute | solution.py:857
  208.4 9.5 %collective-permute-start.21 = (bf16[1,52,16,128]{3,2,1,0:T(8,128)(2,1)S(1)}, bf16[1,52,16,128]{3,2,1,0:T(8,128)(2,1)S(1)}, u32[]{:S(2)}, u32[]{:S(2)}) collective-permute-start(bf16[1,52,16,128]{3,2,1,0:T(8,128)(2,1)S(1)} %fusion.5), channel_id=1, source_target_pairs={{0,8},{1,9},{2,10},{3,11},{4,12},{5,13},{6,14},{7,15},{8,0},{9,1},... | collective-permute-start | bytes 638984 | tf_op jit(solution)/shard_map/ppermute | solution.py:857
  210.5 4.0 %collective-permute-start.22 = (f32[5,16,128]{2,1,0:T(8,128)S(1)}, f32[5,16,128]{2,1,0:T(8,128)S(1)}, u32[]{:S(2)}, u32[]{:S(2)}) collective-permute-start(f32[5,16,128]{2,1,0:T(8,128)S(1)} %add.214), channel_id=1, source_target_pairs={{0,4},{1,5},{2,6},{3,7},{4,0},{5,1},{6,2},{7,3},{8,12},{9,13},{10,... | collective-permute-start | bytes 122888 | tf_op jit(solution)/shard_map/ppermute | solution.py:857
  220.0 17.7 %collective-permute-start.24 = (bf16[4,45,16,128]{3,2,1,0:T(8,128)(2,1)}, bf16[4,45,16,128]{3,2,1,0:T(8,128)(2,1)S(1)}, u32[]{:S(2)}, u32[]{:S(2)}) collective-permute-start(bf16[4,45,16,128]{3,2,1,0:T(8,128)(2,1)} %all-to-all-done.1.mine_ref), channel_id=1, source_target_pairs={{0,4},{1,5},{2,6},{3,7},{4,0},{5,1},{6,2},{7,3},{8,12},{9,13},{10,... | collective-permute-start | bytes 2211848 | tf_op jit(solution)/shard_map/ppermute | solution.py:857
  220.7 5.6 %collective-permute-start.25 = (f32[5,16,128]{2,1,0:T(8,128)S(1)}, f32[5,16,128]{2,1,0:T(8,128)S(1)}, u32[]{:S(2)}, u32[]{:S(2)}) collective-permute-start(f32[5,16,128]{2,1,0:T(8,128)S(1)} %add.216), channel_id=1, source_target_pairs={{0,8},{1,9},{2,10},{3,11},{4,12},{5,13},{6,14},{7,15},{8,0},{9,1},... | collective-permute-start | bytes 122888 | tf_op jit(solution)/shard_map/ppermute | solution.py:857
  220.7 5.8 %collective-permute-start.26 = (f32[5,16,128]{2,1,0:T(8,128)S(1)}, f32[5,16,128]{2,1,0:T(8,128)S(1)}, u32[]{:S(2)}, u32[]{:S(2)}) collective-permute-start(f32[5,16,128]{2,1,0:T(8,128)S(1)} %add.216), channel_id=1, source_target_pairs={{0,16},{1,17},{2,18},{3,19},{4,20},{5,21},{6,22},{7,23},{8,24},{9,... | collective-permute-start | bytes 122888 | tf_op jit(solution)/shard_map/ppermute | solution.py:857
  224.0 5.9 %collective-permute-start.27 = (f32[5,16,128]{2,1,0:T(8,128)S(1)}, f32[5,16,128]{2,1,0:T(8,128)S(1)}, u32[]{:S(2)}, u32[]{:S(2)}) collective-permute-start(f32[5,16,128]{2,1,0:T(8,128)S(1)} %add.216), channel_id=1, source_target_pairs={{0,24},{1,25},{2,26},{3,27},{4,28},{5,29},{6,30},{7,31},{8,16},{9,... | collective-permute-start | bytes 122888 | tf_op jit(solution)/shard_map/ppermute | solution.py:857
  225.2 11.2 %collective-permute-start.23 = (bf16[1,52,16,128]{3,2,1,0:T(8,128)(2,1)S(1)}, bf16[1,52,16,128]{3,2,1,0:T(8,128)(2,1)S(1)}, u32[]{:S(2)}, u32[]{:S(2)}) collective-permute-start(bf16[1,52,16,128]{3,2,1,0:T(8,128)(2,1)S(1)} %add_convert_fusion.5), channel_id=1, source_target_pairs={{0,16},{1,17},{2,18},{3,19},{4,20},{5,21},{6,22},{7,23},{8,24},{9,... | collective-permute-start | bytes 638984 | tf_op jit(solution)/shard_map/ppermute | solution.py:857
  237.7 8.2 %collective-permute-start.28 = (bf16[52,16,128]{2,1,0:T(8,128)(2,1)S(1)}, bf16[52,16,128]{2,1,0:T(8,128)(2,1)S(1)}, u32[]{:S(2)}, u32[]{:S(2)}) collective-permute-start(bf16[52,16,128]{2,1,0:T(8,128)(2,1)S(1)} %bitcast.37), channel_id=1, source_target_pairs={{0,4},{1,5},{2,6},{3,7},{4,0},{5,1},{6,2},{7,3},{8,12},{9,13},{10,... | collective-permute-start | bytes 638984 | tf_op jit(solution)/shard_map/ppermute | solution.py:857
  247.3 1.9 collective-permute-start.29
  247.4 4.0 %collective-permute-start.30 = (f32[8,640]{1,0:T(8,128)S(1)}, f32[8,640]{1,0:T(8,128)S(1)}, u32[]{:S(2)}, u32[]{:S(2)}) collective-permute-start(f32[8,640]{1,0:T(8,128)S(1)} %shard_map.288), channel_id=1, source_target_pairs={{0,2},{1,3},{2,0},{3,1},{4,6},{5,7},{6,4},{7,5},{8,10},{9,11},{10,... | collective-permute-start | bytes 61448 | tf_op jit(solution)/shard_map/ppermute | solution.py:857
  248.2 3.3 %collective-permute-start.31 = (f32[8,640]{1,0:T(8,128)S(1)}, f32[8,640]{1,0:T(8,128)S(1)}, u32[]{:S(2)}, u32[]{:S(2)}) collective-permute-start(f32[8,640]{1,0:T(8,128)S(1)} %shard_map.288), channel_id=1, source_target_pairs={{0,3},{1,2},{2,1},{3,0},{4,7},{5,6},{6,5},{7,4},{8,11},{9,10},{10,... | collective-permute-start | bytes 61448 | tf_op jit(solution)/shard_map/ppermute | solution.py:857
  (21 other events, 91.3 us)
